TPU v7x, 128 devices: a whole 4x4x4 slice. The times are simulated.
128 devices in a mesh: row: 8 (over x_hi, y), col: 16 (over z, x_lo, core).
Axes of the slice: x: 4 (x_hi: 2, x_lo: 2; x = x_hi * 2 + x_lo), y: 4, z: 4, core: 2. Of those that a mesh axis runs over, the one named last changes fastest.
Arguments:
- grad_out: bfloat16 [16384, 8192], P('col', 'row'), may hold values from -4 to 4
- proj_weight: bfloat16 [8192, 4096], P('col', 'row'), may hold values from -0.09375 to 0.09375
- queries: bfloat16 [16384, 4096], P('col', 'row'), may hold values from -5 to 5
- keys: bfloat16 [16384, 4096], P('col', 'row'), may hold values from -5 to 5
- values: bfloat16 [16384, 4096], P('col', 'row'), may hold values from -6 to 6
- cache_keys: bfloat16 [1024, 4096], P('col', 'row'), may hold values from -6 to 6
- cache_values: bfloat16 [1024, 4096], P('col', 'row'), may hold values from -6 to 6
- block_table: int32 [128, 4], P('col'), may hold values from 0 to 7, all different within a row
Outputs:
- grad_q: bfloat16 [16384, 4096], P('col', 'row')
- grad_k: bfloat16 [16384, 4096], P('col', 'row')
- grad_v: bfloat16 [16384, 4096], P('col', 'row')
- grad_cache_k: float32 [1024, 4096], P('col', 'row')
- grad_cache_v: float32 [1024, 4096], P('col', 'row')
- grad_weight: bfloat16 [8192, 4096], P('col', 'row')
Inputs may be any that keep to these rules, and one draw needn't show every extreme that they name: `block_table`: each row names 4 different cached blocks, and every cached block is named by some row.
All inputs are finite; a program needn't handle non-finite values.
Results may differ from a plain program's by a relative error of at most 0.023.
Values may be sent and summed in bfloat16 or wider, within the bound.
No kernel may reach another device: no remote copies, remote signals or barrier semaphores. Data moves between devices by JAX's collectives and lax.ppermute only.
A program may use at most 128 MiB of HBM per device.

v0:
```python
import math

import jax
import jax.numpy as jnp
from jax import lax
from jax.sharding import PartitionSpec as P

HEAD_DIM = 128
BLOCK = 128
CB = 8
KB = 4
CACHE = 1024


def per_device(grad_out, proj_weight, queries, keys, values, cache_keys, cache_values, block_table):
    tok_rows = grad_out.shape[0]
    local_width = queries.shape[1]
    head_count = local_width // HEAD_DIM
    inverse_root = 1.0 / math.sqrt(HEAD_DIM)
    full_grads = lax.all_gather(grad_out, "row", axis=1, tiled=True)
    columns = full_grads
    grad_sum = jnp.dot(
        columns,
        lax.all_gather(proj_weight, "col", axis=0, tiled=True),
        preferred_element_type=jnp.float32,
    )
    grad_attn = grad_sum.astype(jnp.bfloat16)
    cache_k_all, cache_v_all = (
        lax.all_gather(cache_keys, "col", axis=0, tiled=True),
        lax.all_gather(cache_values, "col", axis=0, tiled=True),
    )
    cache_key_blocks = cache_k_all.reshape(CB, BLOCK, head_count, HEAD_DIM)
    cache_value_blocks = cache_v_all.reshape(CB, BLOCK, head_count, HEAD_DIM)
    blocks_here = tok_rows // BLOCK
    group = math.gcd(blocks_here, max(1, 512 // BLOCK))
    turns = blocks_here // group
    positions = jnp.arange(BLOCK, dtype=jnp.int32)
    causal = positions[:, None] >= positions[None, :]
    allowed = jnp.concatenate([jnp.ones((BLOCK, KB * BLOCK), dtype=bool), causal], axis=1)
    block_ids = jnp.arange(CB, dtype=jnp.int32)

    def to_groups(array):
        return array.reshape(turns, group, BLOCK, head_count, HEAD_DIM)

    def one_group(carry, inputs):
        grad_ck, grad_cv = carry
        query, own_keys, own_values, grad_block, chosen = inputs
        picked_keys = cache_key_blocks[chosen].reshape(group, KB * BLOCK, head_count, HEAD_DIM)
        picked_values = cache_value_blocks[chosen].reshape(group, KB * BLOCK, head_count, HEAD_DIM)
        key_list = jnp.concatenate([picked_keys, own_keys], axis=1)
        value_list = jnp.concatenate([picked_values, own_values], axis=1)
        scores = (
            jnp.einsum("gqhd,gkhd->ghqk", query, key_list, preferred_element_type=jnp.float32)
            * inverse_root
        )
        scores = jnp.where(allowed[None, None], scores, -jnp.inf)
        row_max = jnp.max(scores, axis=-1, keepdims=True)
        weights = jnp.exp(scores - row_max)
        probs = weights / jnp.sum(weights, axis=-1, keepdims=True)
        probs_b = probs.astype(jnp.bfloat16)
        attn_full = jnp.einsum(
            "ghqk,gkhd->gqhd", probs_b, value_list, preferred_element_type=jnp.float32
        )
        grad_probs = jnp.einsum(
            "gqhd,gkhd->ghqk", grad_block, value_list, preferred_element_type=jnp.float32
        )
        delta = jnp.sum(grad_block.astype(jnp.float32) * attn_full, axis=-1)
        delta = jnp.transpose(delta, (0, 2, 1))[..., None]
        grad_scores = (probs * (grad_probs - delta)).astype(jnp.bfloat16)
        grad_query = (
            jnp.einsum("ghqk,gkhd->gqhd", grad_scores, key_list, preferred_element_type=jnp.float32)
            * inverse_root
        )
        grad_key_list = (
            jnp.einsum("ghqk,gqhd->gkhd", grad_scores, query, preferred_element_type=jnp.float32)
            * inverse_root
        )
        grad_value_list = jnp.einsum(
            "ghqk,gqhd->gkhd", probs_b, grad_block, preferred_element_type=jnp.float32
        )
        one_hot = (chosen.reshape(group * KB)[:, None] == block_ids[None, :]).astype(jnp.float32)
        cache_key_part = grad_key_list[:, : KB * BLOCK].reshape(group * KB, BLOCK * local_width)
        cache_value_part = grad_value_list[:, : KB * BLOCK].reshape(group * KB, BLOCK * local_width)
        grad_ck = grad_ck + jnp.dot(one_hot.T, cache_key_part, precision=lax.Precision.HIGHEST)
        grad_cv = grad_cv + jnp.dot(one_hot.T, cache_value_part, precision=lax.Precision.HIGHEST)
        outputs = (
            grad_query.astype(jnp.bfloat16),
            grad_key_list[:, KB * BLOCK :].astype(jnp.bfloat16),
            grad_value_list[:, KB * BLOCK :].astype(jnp.bfloat16),
            attn_full.astype(jnp.bfloat16),
        )
        return ((grad_ck, grad_cv), outputs)

    start_carry = (
        jnp.zeros((CB, BLOCK * local_width), jnp.float32),
        jnp.zeros((CB, BLOCK * local_width), jnp.float32),
    )
    inputs = (
        to_groups(queries),
        to_groups(keys),
        to_groups(values),
        to_groups(grad_attn),
        block_table.reshape(turns, group, KB),
    )
    (grad_ck, grad_cv), outputs = lax.scan(one_group, start_carry, inputs)
    grad_q = outputs[0].reshape(tok_rows, local_width)
    grad_k = outputs[1].reshape(tok_rows, local_width)
    grad_v = outputs[2].reshape(tok_rows, local_width)
    attn_out = outputs[3].reshape(tok_rows, local_width)
    grad_cache_k, grad_cache_v = (
        lax.psum_scatter(
            grad_ck.reshape(CACHE, local_width).astype(jnp.bfloat16),
            "col",
            scatter_dimension=0,
            tiled=True,
        ).astype(jnp.float32),
        lax.psum_scatter(
            grad_cv.reshape(CACHE, local_width).astype(jnp.bfloat16),
            "col",
            scatter_dimension=0,
            tiled=True,
        ).astype(jnp.float32),
    )
    columns = full_grads
    grad_weight = lax.psum_scatter(
        lax.dot_general(
            columns, attn_out, (((0,), (0,)), ((), ())), preferred_element_type=jnp.float32
        ).astype(jnp.bfloat16),
        "col",
        scatter_dimension=0,
        tiled=True,
    )
    return (grad_q, grad_k, grad_v, grad_cache_k, grad_cache_v, grad_weight)


def solution(mesh):
    in_specs = (
        P("col", "row"),
        P("col", "row"),
        P("col", "row"),
        P("col", "row"),
        P("col", "row"),
        P("col", "row"),
        P("col", "row"),
        P("col", None),
    )
    out_specs = (
        P("col", "row"),
        P("col", "row"),
        P("col", "row"),
        P("col", "row"),
        P("col", "row"),
        P("col", "row"),
    )
    return jax.shard_map(
        per_device, mesh=mesh, in_specs=in_specs, out_specs=out_specs, check_vma=False
    )
```

profile of v0, /device:TPU:6, one launch (start us, length us, event | category | flops | bytes accessed | tf_op | source)
XLA Modules:
  0.0 711.0 jit_solution(17376013707526476103)
XLA Ops:
  13.6 30.9 %all-gather.5.cloned.1.call-done = bf16[1024,512]{1,0:T(8,128)(2,1)} async-done(((bf16[64,512]{1,0:T(8,128)(2,1)}), bf16[1024,512]{1,0:T(8,128)(2,1)}) %all-gather.5.cloned.1.call-update) | async-done | bytes 1048592 | tf_op jit(solution)/shard_map/all_gather | solution.py:29
  47.1 31.7 %all-gather.11.cloned.1.call-done = bf16[1024,512]{1,0:T(8,128)(2,1)} async-done(((bf16[64,512]{1,0:T(8,128)(2,1)}), bf16[1024,512]{1,0:T(8,128)(2,1)}) %all-gather.11.cloned.1.call-update) | async-done | bytes 1048592 | tf_op jit(solution)/shard_map/all_gather | solution.py:30
  81.4 51.4 %all-gather.9.cloned.1.call-done = bf16[8192,512]{1,0:T(8,128)(2,1)} async-done(((bf16[512,512]{1,0:T(8,128)(2,1)}), bf16[8192,512]{1,0:T(8,128)(2,1)}) %all-gather.9.cloned.1.call-update) | async-done | bytes 8388624 | tf_op jit(solution)/shard_map/all_gather | solution.py:24
  132.8 184.4 %all-gather.7.cloned.1.call-done = bf16[1024,8192]{1,0:T(8,128)(2,1)} async-done(((bf16[1024,1024]{1,0:T(8,128)(2,1)}), bf16[1024,8192]{1,0:T(8,128)(2,1)}) %all-gather.7.cloned.1.call-update) | async-done | bytes 16777232 | tf_op jit(solution)/shard_map/all_gather | solution.py:20
  317.1 14.8 %convolution_convert_fusion.1 = bf16[1024,512]{1,0:T(8,128)(2,1)S(1)} fusion(bf16[1024,8192]{1,0:T(8,128)(2,1)} %all-gather.7.cloned.1.call-done, bf16[8192,512]{1,0:T(8,128)(2,1)} %all-gather.9.cloned.1.call-done), kind=kOutput, calls=%fused_computation.58 | convolution fusion | flops 8590458880 | bytes 26214400 | tf_op jit(solution)/shard_map/dot_general | solution.py:22
  333.0 146.8 %while.21 = (s32[]{:T(128)}, f32[8,65536]{1,0:T(8,128)}, f32[8,65536]{1,0:T(8,128)}, bf16[2,4,128,4,128]{4,3,2,1,0:T(4,128)(2,1)}, bf16[2,4,128,4,128]{4,3,2,1,0...) while((s32[]{:T(128)}, f32[8,65536]{1,0:T(8,128)}, ...), condition=%wide.region_4.5_spmd.clone, body=%wide.region_0.4_spmd.clone.sunk | while | flops 2256273408 | bytes 212464848 | solution.py:105
  365.9 5.3 copy.184
  371.3 4.9 reshape.151
  376.1 4.5 convolution_add_fusion.4
  388.9 5.2 copy.185
  394.1 5.1 reshape.152
  399.3 3.6 convolution_add_fusion.5
  403.2 3.0 copy_dynamic-update-slice_fusion.2
  439.2 5.3 copy.184
  444.5 4.9 reshape.151
  449.4 4.7 convolution_add_fusion.4
  462.4 5.2 copy.185
  467.7 5.1 reshape.152
  472.8 3.6 convolution_add_fusion.5
  476.8 3.0 copy_dynamic-update-slice_fusion.2
  485.0 17.0 %fusion.25 = bf16[8192,512]{0,1:T(8,128)(2,1)} fusion(bf16[1024,8192]{1,0:T(8,128)(2,1)} %all-gather.7.cloned.1.call-done, bf16[128,8,4,128]{3,2,1,0:T(4,128)(2,1)S(1)} %bitcast.130), kind=kOutput, calls=%fused_computation.57 | convolution fusion | flops 8594128896 | bytes 26214400 | tf_op jit(solution)/shard_map/dot_general | solution.py:126
  506.1 34.5 %reduce-scatter.4.cloned.1.call-done = bf16[64,512]{1,0:T(8,128)(2,1)} async-done(((bf16[1024,512]{1,0:T(8,128)(2,1)}), bf16[64,512]{1,0:T(8,128)(2,1)}) %reduce-scatter.4.cloned.1.call-update) | async-done | bytes 65552 | tf_op jit(solution)/shard_map/reduce_scatter | solution.py:111
  542.2 61.1 %reduce-scatter.6.cloned.1.call-done = bf16[64,512]{1,0:T(8,128)(2,1)} async-done(((bf16[1024,512]{1,0:T(8,128)(2,1)}), bf16[64,512]{1,0:T(8,128)(2,1)}) %reduce-scatter.6.cloned.1.call-update) | async-done | bytes 65552 | tf_op jit(solution)/shard_map/reduce_scatter | solution.py:117
  604.7 97.4 %reduce-scatter.8.cloned.1.call-done = bf16[512,512]{0,1:T(8,128)(2,1)} async-done(((bf16[8192,512]{0,1:T(8,128)(2,1)}), bf16[512,512]{0,1:T(8,128)(2,1)}) %reduce-scatter.8.cloned.1.call-update) | async-done | bytes 524304 | tf_op jit(solution)/shard_map/reduce_scatter | solution.py:125
  (154 shorter events, 109.5 us)
Async XLA Ops:
  7.2 2.9 copy-start.16
  7.2 3.0 copy-start.10
  7.2 4.2 copy-start.11
  7.2 37.3 %all-gather.5.cloned.1.call-start = ((), (), s32[]{:S(2)}) async-start(), calls=%async_computation.3 | async-start | bytes 1114112 | tf_op jit(solution)/shard_map/all_gather | solution.py:29
  7.9 70.9 %all-gather.11.cloned.1.call-start = ((), (), s32[]{:S(2)}) async-start(), calls=%async_computation.6 | async-start | bytes 1114112 | tf_op jit(solution)/shard_map/all_gather | solution.py:30
  8.7 124.1 %all-gather.9.cloned.1.call-start = ((), (), s32[]{:S(2)}) async-start(), calls=%async_computation.5 | async-start | bytes 8912896 | tf_op jit(solution)/shard_map/all_gather | solution.py:24
  9.4 307.7 %all-gather.7.cloned.1.call-start = ((), (), s32[]{:S(2)}) async-start(), calls=%async_computation.4 | async-start | bytes 18874368 | tf_op jit(solution)/shard_map/all_gather | solution.py:20
  10.0 2.5 copy-start.12
  10.0 530.7 %reduce-scatter.4.cloned.1.call-start = ((), (), s32[]{:S(2)}) async-start(), calls=%async_computation.7 | async-start | bytes 1114112 | tf_op jit(solution)/shard_map/reduce_scatter | solution.py:111
  339.9 6.2 copy-start.6
  353.1 2.8 copy-start.7
  380.6 4.7 copy-start.2
  394.1 5.1 copy-start.3
  402.9 3.4 copy-start.4
  413.2 6.2 copy-start.6
  426.3 2.8 copy-start.7
  454.1 4.7 copy-start.2
  467.7 5.1 copy-start.3
  476.4 3.4 copy-start.4
  479.8 3.5 copy-start.5
  483.2 120.0 %reduce-scatter.6.cloned.1.call-start = ((), (), s32[]{:S(2)}) async-start(), calls=%async_computation.8 | async-start | bytes 1114112 | tf_op jit(solution)/shard_map/reduce_scatter | solution.py:117
  484.9 217.2 %reduce-scatter.8.cloned.1.call-start = ((), (), s32[]{:S(2)}) async-start(), calls=%async_computation.9 | async-start | bytes 8912896 | tf_op jit(solution)/shard_map/reduce_scatter | solution.py:125
  502.0 2.4 copy-start.14
  502.0 2.4 copy-start.15
  (10 other events, 15.1 us)
Sparse Core Ops, SparseCore 0:
  9.7 34.7 all-gather.4
  46.2 32.5 all-gather.10
  80.5 52.2 all-gather.8
  134.9 182.1 all-gather.6
  483.3 57.2 reduce-scatter.3
  543.0 60.1 reduce-scatter.5
  605.6 96.4 reduce-scatter.7
where the time goes:
time: 717 us; the launch traced here: 711 us
  waiting for transfers between devices  494 us (69%)
  local copies, waits for them, and re-layouts  124 us (17%)
  matrix products  67.2 us (9%)
  between operations  14.3 us (2%)
  other arithmetic  10.5 us (1%)
    all_gather x1, waiting for transfers between devices, per_device(): full_grads = lax.all_gather(grad_out, 'row', axis=1, tiled=True)  184 us
    reduce_scatter x1, waiting for transfers between devices, per_device(): lax.psum_scatter(lax.dot_general(columns, attn_out, (((0,), (0,)), ((), (...  97.4 us
    reduce_scatter x1, waiting for transfers between devices, per_device(): lax.psum_scatter(grad_cv.reshape(CACHE, local_width).astype(jnp.bfloat16)...  61.1 us
    all_gather x1, waiting for transfers between devices, per_device(): lax.all_gather(proj_weight, 'col', axis=0, tiled=True)  51.4 us
    reduce_scatter x1, waiting for transfers between devices, per_device(): lax.psum_scatter(grad_ck.reshape(CACHE, local_width).astype(jnp.bfloat16)...  34.5 us
    all_gather x1, waiting for transfers between devices, per_device(): lax.all_gather(cache_values, 'col', axis=0, tiled=True)  31.7 us
    all_gather x1, waiting for transfers between devices, per_device(): lax.all_gather(cache_keys, 'col', axis=0, tiled=True)  30.9 us
    dynamic_update_slice x10, local copies, waits for them, and re-layouts, per_device(): (grad_ck, grad_cv), outputs = lax.scan(one_group, start_carry, inputs)  20.3 us
  transfers between devices with their start and end apart: 7, of which 7 were waited for; matrix products, arithmetic and copies ran while one was open for 5% of the time, Pallas kernels for 0%

commit v1 on v0

v1 whole, which is shorter than its diff:
```python
import functools
import math

import jax
import jax.numpy as jnp
from jax import lax
from jax.experimental import pallas as pl
from jax.experimental.pallas import tpu as pltpu
from jax.sharding import PartitionSpec as P

HD=128; BLK=128; KB=4; CB=8
SCALE=1.0/math.sqrt(HD); EXPSCALE=SCALE*math.log2(math.e)
NT=(((1,),(1,)),((),())); TN=(((0,),(0,)),((),())); NN=(((1,),(0,)),((),()))
def dg(a,b,dims): return lax.dot_general(a,b,dims,preferred_element_type=jnp.float32)

def fwd_kernel(heads,table,q_ref,k_ref,v_ref,c_ref,o_ref,p_ref):
    b=pl.program_id(0); width=heads*HD
    keyp=lax.broadcasted_iota(jnp.int32,(BLK,BLK),0); qp=lax.broadcasted_iota(jnp.int32,(BLK,BLK),1)
    rows=[pl.ds(pl.multiple_of(table[b,j]*BLK,BLK),BLK) for j in range(KB)]
    for h in range(heads):
        cols=slice(h*HD,(h+1)*HD); vcols=slice(width+h*HD,width+(h+1)*HD)
        q=q_ref[:,cols]
        s=[dg(c_ref[r,cols],q,NT) for r in rows]
        s.append(jnp.where(keyp<=qp,dg(k_ref[:,cols],q,NT),-jnp.inf))
        m=functools.reduce(jnp.maximum,[jnp.max(t,axis=0,keepdims=True) for t in s])
        e=[jnp.exp2((t-m)*EXPSCALE) for t in s]
        l=functools.reduce(jnp.add,[jnp.sum(t,axis=0,keepdims=True) for t in e])
        r=1.0/l
        p=[(t*r).astype(jnp.bfloat16) for t in e]
        o=dg(p[KB],v_ref[:,cols],TN)
        for j in range(KB): o=o+dg(p[j],c_ref[rows[j],vcols],TN)
        o_ref[:,cols]=o.astype(jnp.bfloat16)
        for j in range(KB+1): p_ref[0,h,j*BLK:(j+1)*BLK,:]=p[j]

def fwd(table,q,k,v,cache):
    T,W=q.shape; heads=W//HD; nb=T//BLK
    blk=pl.BlockSpec((BLK,W),lambda b,t:(b,0))
    return pl.pallas_call(functools.partial(fwd_kernel,heads),
        grid_spec=pltpu.PrefetchScalarGridSpec(num_scalar_prefetch=1,grid=(nb,),
            in_specs=[blk,blk,blk,pl.BlockSpec(cache.shape,lambda b,t:(0,0))],
            out_specs=[blk,pl.BlockSpec((1,heads,(KB+1)*BLK,BLK),lambda b,t:(b,0,0,0))]),
        out_shape=[jax.ShapeDtypeStruct((T,W),jnp.bfloat16),jax.ShapeDtypeStruct((nb,heads,(KB+1)*BLK,BLK),jnp.bfloat16)],
        compiler_params=pltpu.CompilerParams(vmem_limit_bytes=40<<20),
        cost_estimate=pl.CostEstimate(flops=int(2*2*T*W*(KB+1)*BLK),bytes_accessed=12<<20,transcendentals=T*heads*(KB+1)*BLK),
        name="attn_fwd")(table,q,k,v,cache)

def bwd_kernel(heads,table,q_ref,k_ref,v_ref,c_ref,p_ref,ga_ref,gb_ref,dq_ref,dk_ref,dv_ref,dc_ref,acc):
    b=pl.program_id(0); width=heads*HD
    @pl.when(b==0)
    def _(): acc[...]=jnp.zeros_like(acc)
    rows=[pl.ds(pl.multiple_of(table[b,j]*BLK,BLK),BLK) for j in range(KB)]
    for h in range(heads):
        cols=slice(h*HD,(h+1)*HD); vcols=slice(width+h*HD,width+(h+1)*HD)
        q=q_ref[:,cols]
        do=(ga_ref[:,cols]+gb_ref[:,cols].astype(jnp.float32)).astype(jnp.bfloat16)
        kk=[c_ref[r,cols] for r in rows]+[k_ref[:,cols]]
        vv=[c_ref[r,vcols] for r in rows]+[v_ref[:,cols]]
        pb=[p_ref[0,h,j*BLK:(j+1)*BLK,:] for j in range(KB+1)]
        pf=[t.astype(jnp.float32) for t in pb]
        dp=[dg(t,do,NT) for t in vv]
        delta=functools.reduce(jnp.add,[jnp.sum(a*c,axis=0,keepdims=True) for a,c in zip(pf,dp)])
        ds=[(a*(c-delta)).astype(jnp.bfloat16) for a,c in zip(pf,dp)]
        dq=functools.reduce(jnp.add,[dg(a,c,TN) for a,c in zip(ds,kk)])
        dq_ref[:,cols]=(dq*SCALE).astype(jnp.bfloat16)
        dk_ref[:,cols]=(dg(ds[KB],q,NN)*SCALE).astype(jnp.bfloat16)
        dv_ref[:,cols]=dg(pb[KB],do,NN).astype(jnp.bfloat16)
        for j in range(KB):
            acc[rows[j],cols]+=dg(ds[j],q,NN)
            acc[rows[j],vcols]+=dg(pb[j],do,NN)
    @pl.when(b==pl.num_programs(0)-1)
    def _():
        dc_ref[:,:width]=(acc[:,:width]*SCALE).astype(jnp.bfloat16)
        dc_ref[:,width:]=acc[:,width:].astype(jnp.bfloat16)

def bwd(table,q,k,v,cache,p,ga,gb):
    T,W=q.shape; heads=W//HD; nb=T//BLK
    blk=pl.BlockSpec((BLK,W),lambda b,t:(b,0))
    full=pl.BlockSpec(cache.shape,lambda b,t:(0,0))
    return pl.pallas_call(functools.partial(bwd_kernel,heads),
        grid_spec=pltpu.PrefetchScalarGridSpec(num_scalar_prefetch=1,grid=(nb,),
            in_specs=[blk,blk,blk,full,pl.BlockSpec((1,heads,(KB+1)*BLK,BLK),lambda b,t:(b,0,0,0)),blk,blk],
            out_specs=[blk,blk,blk,full],
            scratch_shapes=[pltpu.VMEM(cache.shape,jnp.float32)]),
        out_shape=[jax.ShapeDtypeStruct((T,W),jnp.bfloat16)]*3+[jax.ShapeDtypeStruct(cache.shape,jnp.bfloat16)],
        compiler_params=pltpu.CompilerParams(vmem_limit_bytes=40<<20),
        cost_estimate=pl.CostEstimate(flops=int(4*2*T*W*(KB+1)*BLK),bytes_accessed=20<<20,transcendentals=0),
        name="attn_bwd")(table,q,k,v,cache,p,ga,gb)


AXES = ("row", "col")
PLACE = {0: 0, 3: 1, 1: 2, 2: 3}


def device(xh, y, z, xl, core):
    return (xh * 4 + y) * 16 + (z * 2 + xl) * 2 + core


def every():
    for xh in range(2):
        for y in range(4):
            for z in range(4):
                for xl in range(2):
                    for core in range(2):
                        yield xh, y, z, xl, core


def shifted(xh=0, y=0, z=0, xl=0, core=0):
    return [
        (device(*d), device(d[0] ^ xh, (d[1] + y) % 4, (d[2] + z) % 4, d[3] ^ xl, d[4] ^ core)) for d in every()
    ]


def swap_pairs():
    pairs = []
    for d in every():
        xh, y, z, xl, core = d
        owner = z // 2
        place = PLACE[((z % 2) * 2 + xl - y) % 4]
        pairs.append((device(*d), device(owner, y, (xh ^ owner) * 2 + place // 2, place % 2, core)))
    return pairs


def send(array, pairs):
    return lax.ppermute(array, AXES, pairs)


def f32(array):
    return array.astype(jnp.float32)


def per_device(grad_out, proj_weight, queries, keys, values, cache_keys, cache_values, block_table):
    bf16 = jnp.bfloat16
    tokens, width = queries.shape
    depth = grad_out.shape[1]
    swap = swap_pairs()
    back = [(b, a) for a, b in swap]
    col = lax.axis_index("col")
    z, xl = col // 4, (col // 2) % 2

    mine = jnp.concatenate([cache_keys, cache_values], axis=1)
    pair = jnp.concatenate([mine, send(mine, shifted(xl=1))], axis=0)
    own_core = jnp.concatenate(
        [pair, send(pair, shifted(z=1)), send(pair, shifted(z=3)), send(pair, shifted(z=2))], axis=0
    )
    other_core = send(own_core, shifted(core=1))
    rows = mine.shape[0]
    cache = jnp.stack(
        [own_core.reshape(CB, rows, 2 * width), other_core.reshape(CB, rows, 2 * width)], axis=1
    ).reshape(CB * 2 * rows, 2 * width)
    far = (block_table // 2 - z) % 4
    table = jnp.where(far == 0, 0, jnp.where(far == 3, 1, jnp.where(far == 1, 2, 3))) * 2 + ((block_table % 2) ^ xl)

    weight = lax.all_gather(send(proj_weight, swap), "col", axis=0, tiled=True)
    half = weight.shape[0] // 2

    before = send(grad_out, shifted(y=1))
    after = send(grad_out, shifted(y=3))
    across = jnp.concatenate(
        [send(before[: tokens // 2], shifted(y=1)), send(after[tokens // 2 :], shifted(y=3))], axis=0
    )
    columns = jnp.concatenate([grad_out, before, after, across], axis=1)

    attn_out, probs = fwd(table, queries, keys, values, cache)
    attn_other = send(attn_out, shifted(xh=1))

    other_part = jnp.dot(columns, weight[half:], preferred_element_type=jnp.float32).astype(bf16)
    from_other = send(other_part, shifted(xh=1))
    own_part = jnp.dot(columns, weight[:half], preferred_element_type=jnp.float32)

    def weight_part(attn):
        return lax.dot_general(
            columns, attn, (((0,), (0,)), ((), ())), preferred_element_type=jnp.float32
        ).astype(bf16)

    partial = jnp.concatenate([weight_part(attn_out), weight_part(attn_other)], axis=0)
    grad_weight = send(lax.psum_scatter(partial, "col", scatter_dimension=0, tiled=True), back)

    grad_q, grad_k, grad_v, grad_cache = bwd(table, queries, keys, values, cache, probs, own_part, from_other)

    parts = grad_cache.reshape(CB, 2, rows, 2 * width)
    total = (f32(parts[:, 0]) + f32(send(parts[:, 1], shifted(core=1)))).astype(bf16)
    total = total.reshape(4, 2, rows, 2 * width)
    total = (
        f32(total[0]) + f32(send(total[1], shifted(z=3))) + f32(send(total[2], shifted(z=1))) + f32(send(total[3], shifted(z=2)))
    ).astype(bf16)
    total = f32(total[0]) + f32(send(total[1], shifted(xl=1)))
    return (grad_q, grad_k, grad_v, total[:, :width], total[:, width:], grad_weight)


def solution(mesh):
    both = P("col", "row")
    return jax.shard_map(
        per_device, mesh=mesh, in_specs=(both,) * 7 + (P("col", None),), out_specs=(both,) * 6, check_vma=False
    )
```

time: 717 us -> 309 us (0.43)
  waiting for transfers between devices: 494 us -> 155 us
  local copies, waits for them, and re-layouts: 124 us -> 14.6 us
  Pallas kernels: 0 us -> 35.1 us
  starting transfers between devices: 0.27 us -> 33.6 us
  matrix products: 67.2 us -> 43.9 us
    all_gather x4 -> x1, waiting for transfers between devices: 298 us -> 0.02 us  [per_device(): weight = lax.all_gather(send(proj_weight, swap), 'col', axis=0, tiled=True)]
    reduce_scatter x3 -> x1, waiting for transfers between devices: 193 us -> 5.74 us  [per_device(): lax.psum_scatter(partial, 'col', scatter_dimension=0, tiled=True)]
    ppermute x0 -> x18, waiting for transfers between devices: none -> 149 us  [send(): return lax.ppermute(array, AXES, pairs)]
    pallas_call x0 -> x2, Pallas kernels: none -> 35.1 us  [the longest x1 19.4 us: bwd(): pl.pallas_call(functools.partial(bwd_kernel, heads), grid_spec=pltpu.Pref...]
    ppermute x0 -> x18, starting transfers between devices: none -> 33.5 us  [send(): return lax.ppermute(array, AXES, pairs)]
    reshape x11 -> x0, local copies, waits for them, and re-layouts: 28.9 us -> none  [the longest x2 10.2 us: one_group(): grad_value_list[:, :KB * BLOCK].reshape(group * KB, BLOCK * local_width)]
    slice x8 -> x4, local copies, waits for them, and re-layouts: 31.3 us -> 2.87 us  [the longest x1 1.04 us: per_device(): before[:tokens // 2]]
    dot_general x18 -> x4, matrix products: 67.2 us -> 43.9 us  [the longest x2 25.1 us: weight_part(): lax.dot_general(columns, attn, (((0,), (0,)), ((), ())), preferred_elemen...]
  transfers between devices with their start and end apart: 7 -> 20, of which waited for: 7 -> 12; matrix products, arithmetic and copies ran while one was open for 5% -> 19% of each run, Pallas kernels for 0% -> 11%
where the time goes in v1:
time: 309 us; the launch traced here: 306 us
  waiting for transfers between devices  155 us (50%)
  matrix products  43.9 us (14%)
  Pallas kernels  35.1 us (11%)
  starting transfers between devices  33.6 us (11%)
  local copies, waits for them, and re-layouts  14.6 us (5%)
  between operations  14.3 us (5%)
  other arithmetic  9.69 us (3%)
    ppermute x18, waiting for transfers between devices, send(): return lax.ppermute(array, AXES, pairs)  149 us
    ppermute x18, starting transfers between devices, send(): return lax.ppermute(array, AXES, pairs)  33.5 us
    dot_general x2, matrix products, weight_part(): lax.dot_general(columns, attn, (((0,), (0,)), ((), ())), preferred_elemen...  25.1 us
    pallas_call x1, Pallas kernels, bwd(): pl.pallas_call(functools.partial(bwd_kernel, heads), grid_spec=pltpu.Pref...  19.4 us
    pallas_call x1, Pallas kernels, fwd(): pl.pallas_call(functools.partial(fwd_kernel, heads), grid_spec=pltpu.Pref...  15.7 us
    unnamed x36, local copies, waits for them, and re-layouts  10.7 us
    dot_general x1, matrix products, per_device(): jnp.dot(columns, weight[half:], preferred_element_type=jnp.float32)  10.7 us
    dot_general x1, matrix products, per_device(): jnp.dot(columns, weight[:half], preferred_element_type=jnp.float32)  8.16 us
  transfers between devices with their start and end apart: 20, of which 12 were waited for; matrix products, arithmetic and copies ran while one was open for 19% of the time, Pallas kernels for 11%

profile of v1, /device:TPU:6, one launch (start us, length us, event | category | flops | bytes accessed | tf_op | source)
XLA Modules:
  0.0 306.2 jit_solution(3911056057652047113)
XLA Ops:
  7.2 6.0 %collective-permute-start.9 = (bf16[512,512]{1,0:T(8,128)(2,1)}, bf16[512,512]{1,0:T(8,128)(2,1)S(1)}, u32[]{:S(2)}, u32[]{:S(2)}) collective-permute-start(bf16[512,512]{1,0:T(8,128)(2,1)} %param.9), channel_id=1, source_target_pairs={{0,0},{1,1},{2,4},{3,5},{4,6},{5,7},{6,2},{7,3},{8,72},{9,73},{10,... | collective-permute-start | bytes 1572872 | tf_op jit(solution)/shard_map/ppermute | solution.py:124
  13.2 22.7 %collective-permute-done.9 = bf16[512,512]{1,0:T(8,128)(2,1)S(1)} collective-permute-done((bf16[512,512]{1,0:T(8,128)(2,1)}, bf16[512,512]{1,0:T(8,128)(2,1)S(1)}, u32[]{:S(2)}, u32[]{:S(2)}) %collective-permute-start.9) | collective-permute-done | bytes 524320 | tf_op jit(solution)/shard_map/ppermute | solution.py:124
  36.9 3.2 %collective-permute-start.6 = (bf16[1024,1024]{1,0:T(8,128)(2,1)}, bf16[1024,1024]{1,0:T(8,128)(2,1)S(1)}, u32[]{:S(2)}, u32[]{:S(2)}) collective-permute-start(bf16[1024,1024]{1,0:T(8,128)(2,1)} %param.8), channel_id=1, source_target_pairs={{0,48},{1,49},{2,50},{3,51},{4,52},{5,53},{6,54},{7,55},{8,56},{9,... | collective-permute-start | bytes 6291464 | tf_op jit(solution)/shard_map/ppermute | solution.py:124
  41.9 5.0 %collective-permute-done = bf16[64,1024]{1,0:T(8,128)(2,1)S(1)} collective-permute-done((bf16[64,1024]{1,0:T(8,128)(2,1)S(1)}, bf16[64,1024]{1,0:T(8,128)(2,1)S(1)}, u32[]{:S(2)}, u32[]{:S(2)}) %collective-permute-start) | collective-permute-done | bytes 131104 | tf_op jit(solution)/shard_map/ppermute | solution.py:124
  46.9 2.8 collective-permute-start.1
  52.1 9.9 %collective-permute-done.1 = bf16[128,1024]{1,0:T(8,128)(2,1)S(1)} collective-permute-done((bf16[128,1024]{1,0:T(8,128)(2,1)S(1)}, bf16[128,1024]{1,0:T(8,128)(2,1)S(1)}, u32[]{:S(2)}, u32[]{:S(2)}) %collective-permute-start.1) | collective-permute-done | bytes 262176 | tf_op jit(solution)/shard_map/ppermute | solution.py:124
  64.5 10.5 %collective-permute-done.3 = bf16[128,1024]{1,0:T(8,128)(2,1)S(1)} collective-permute-done((bf16[128,1024]{1,0:T(8,128)(2,1)S(1)}, bf16[128,1024]{1,0:T(8,128)(2,1)S(1)}, u32[]{:S(2)}, u32[]{:S(2)}) %collective-permute-start.3) | collective-permute-done | bytes 262176 | tf_op jit(solution)/shard_map/ppermute | solution.py:124
  75.1 10.6 %collective-permute-done.5 = bf16[1024,1024]{1,0:T(8,128)(2,1)S(1)} collective-permute-done((bf16[1024,1024]{1,0:T(8,128)(2,1)}, bf16[1024,1024]{1,0:T(8,128)(2,1)S(1)}, u32[]{:S(2)}, u32[]{:S(2)}) %collective-permute-start.5) | collective-permute-done | bytes 2097184 | tf_op jit(solution)/shard_map/ppermute | solution.py:124
  90.4 3.2 %collective-permute-start.8 = (bf16[512,1024]{1,0:T(8,128)(2,1)}, bf16[512,1024]{1,0:T(8,128)(2,1)}, u32[]{:S(2)}, u32[]{:S(2)}) collective-permute-start(bf16[512,1024]{1,0:T(8,128)(2,1)} %slice.61), channel_id=1, source_target_pairs={{0,48},{1,49},{2,50},{3,51},{4,52},{5,53},{6,54},{7,55},{8,56},{9,... | collective-permute-start | bytes 3145736 | tf_op jit(solution)/shard_map/ppermute | solution.py:124
  98.8 15.7 %attn_fwd.1 = (bf16[1024,512]{1,0:T(8,128)(2,1)S(1)}, bf16[8,4,640,128]{3,2,1,0:T(8,128)(2,1)S(1)}) custom-call(s32[8,4]{1,0:T(8,128)S(1)} %fusion.11.table, bf16[1024,512]{1,0:T(8,128)(2,1)S(1)} %copy-done.1, bf16[1024,512]{1,0:T(8,128)(2,1)S(1)} %copy-done.2, bf16[1024,512]{1,0:T(8,128)(2,1)S(1)} %copy-done.4, bf16[1024,1024]{1,0:T(8,128)(2,1)S(1)} %bitcast.28), custom_call_target="tpu_custom_call" | custom-call | flops 1342177280 | bytes 12582912 | tf_op jit(solution)/shard_map/attn_fwd/pallas_call | solution.py:38
  116.8 13.6 %convolution_convert_fusion.1 = bf16[4096,512]{1,0:T(8,128)(2,1)} fusion(bf16[1024,512]{1,0:T(8,128)(2,1)S(1)} %get-tuple-element.17, bf16[512,1024]{1,0:T(8,128)(2,1)} %collective-permute-done.8, bf16[512,1024]{1,0:T(8,128)(2,1)} %collective-permute-done.7, bf16[1024,1024]{1,0:T(8,128)(2,1)} %copy-done.10, bf16[1024,1024]{1,0:T(8,128)(2,1)} %copy-done.7, ...), kind=kOutput, calls=%fused_computation.3 | convolution fusion | flops 4339007488 | bytes 13631488 | tf_op jit(solution)/shard_map/dot_general | solution.py:171
  130.4 11.4 %collective-permute-done.16 = bf16[1024,512]{1,0:T(8,128)(2,1)S(1)} collective-permute-done((bf16[1024,512]{1,0:T(8,128)(2,1)S(1)}, bf16[1024,512]{1,0:T(8,128)(2,1)S(1)}, u32[]{:S(2)}, u32[]{:S(2)}) %collective-permute-start.16) | collective-permute-done | bytes 1048608 | tf_op jit(solution)/shard_map/ppermute | solution.py:124
  141.8 11.5 %convolution_convert_fusion = bf16[4096,512]{1,0:T(8,128)(2,1)} fusion(bf16[1024,512]{1,0:T(8,128)(2,1)S(1)} %collective-permute-done.16, bf16[512,1024]{1,0:T(8,128)(2,1)} %collective-permute-done.8, bf16[512,1024]{1,0:T(8,128)(2,1)} %collective-permute-done.7, bf16[1024,1024]{1,0:T(8,128)(2,1)S(1)} %copy-done.11, bf16[1024,1024]{1,0:T(8,128)(2,1)S(1)} %copy-done.8, ...), kind=kOutput, calls=%fused_computation.2 | convolution fusion | flops 4339007488 | bytes 13631488 | tf_op jit(solution)/shard_map/dot_general | solution.py:171
  153.3 7.3 %pad_maximum_fusion = bf16[8192,512]{1,0:T(8,128)(2,1)} fusion(bf16[4096,512]{1,0:T(8,128)(2,1)} %convolution_convert_fusion, bf16[4096,512]{1,0:T(8,128)(2,1)} %convolution_convert_fusion.1), kind=kLoop, calls=%fused_computation.1 | loop fusion | flops 16777216 | bytes 16777216 | tf_op jit(solution)/shard_map/concatenate | solution.py:175
  160.6 10.7 %fusion.5 = bf16[1024,512]{1,0:T(8,128)(2,1)} fusion(bf16[8192,512]{1,0:T(8,128)(2,1)} %all-gather.2.cloned.1.call-done, bf16[512,1024]{1,0:T(8,128)(2,1)} %collective-permute-done.8, bf16[512,1024]{1,0:T(8,128)(2,1)} %collective-permute-done.7, bf16[1024,1024]{1,0:T(8,128)(2,1)} %copy-done.10, bf16[1024,1024]{1,0:T(8,128)(2,1)} %copy-done.7, ...), kind=kOutput, calls=%fused_computation.11 | convolution fusion | flops 4337434624 | bytes 13631488 | tf_op jit(solution)/shard_map/dot_general | solution.py:166
  171.7 8.2 %fusion.2.ga_ref = f32[1024,512]{1,0:T(8,128)S(1)} fusion(bf16[8192,512]{1,0:T(8,128)(2,1)} %all-gather.2.cloned.1.call-done, bf16[512,1024]{1,0:T(8,128)(2,1)} %collective-permute-done.8, bf16[512,1024]{1,0:T(8,128)(2,1)} %collective-permute-done.7, bf16[1024,1024]{1,0:T(8,128)(2,1)S(1)} %copy-done.12, bf16[1024,1024]{1,0:T(8,128)(2,1)S(1)} %copy-done.9, ...), kind=kOutput, calls=%fused_computation.6 | convolution fusion | flops 4336910336 | bytes 14680064 | tf_op jit(solution)/shard_map/dot_general | solution.py:168
  179.8 40.6 %collective-permute-done.10.gb_ref = bf16[1024,512]{1,0:T(8,128)(2,1)S(1)} collective-permute-done((bf16[1024,512]{1,0:T(8,128)(2,1)}, bf16[1024,512]{1,0:T(8,128)(2,1)S(1)}, u32[]{:S(2)}, u32[]{:S(2)}) %collective-permute-start.10) | collective-permute-done | bytes 1048608 | tf_op jit(solution)/shard_map/ppermute | solution.py:124
  220.4 19.4 %attn_bwd.1 = (bf16[1024,512]{1,0:T(8,128)(2,1)}, bf16[1024,512]{1,0:T(8,128)(2,1)}, bf16[1024,512]{1,0:T(8,128)(2,1)}, bf16[1024,1024]{1,0:T(8,128)(2,1)S(1)}) custom-call(s32[8,4]{1,0:T(8,128)S(1)} %fusion.11.table, bf16[1024,512]{1,0:T(8,128)(2,1)S(1)} %copy-done.1, bf16[1024,512]{1,0:T(8,128)(2,1)S(1)} %copy-done.3, bf16[1024,512]{1,0:T(8,128)(2,1)S(1)} %copy-done.5, ...), custom_call_target="tpu_custom_call" | custom-call | flops 2684354560 | bytes 20971520 | tf_op jit(solution)/shard_map/attn_bwd/pallas_call | solution.py:79
  243.1 3.9 %collective-permute-start.12 = (bf16[2,64,1024]{2,1,0:T(8,128)(2,1)S(1)}, bf16[2,64,1024]{2,1,0:T(8,128)(2,1)S(1)}, u32[]{:S(2)}, u32[]{:S(2)}) collective-permute-start(bf16[2,64,1024]{2,1,0:T(8,128)(2,1)S(1)} %get-tuple-element.18), channel_id=1, source_target_pairs={{0,12},{1,13},{2,14},{3,15},{4,0},{5,1},{6,2},{7,3},{8,4},{9,5},{1... | collective-permute-start | bytes 786440 | tf_op jit(solution)/shard_map/ppermute | solution.py:124
  247.9 21.4 %collective-permute-done.12 = bf16[2,64,1024]{2,1,0:T(8,128)(2,1)S(1)} collective-permute-done((bf16[2,64,1024]{2,1,0:T(8,128)(2,1)S(1)}, bf16[2,64,1024]{2,1,0:T(8,128)(2,1)S(1)}, u32[]{:S(2)}, u32[]{:S(2)}) %collective-permute-start.12) | collective-permute-done | bytes 262176 | tf_op jit(solution)/shard_map/ppermute | solution.py:124
  269.5 3.9 %collective-permute-start.15 = (bf16[64,1024]{1,0:T(8,128)(2,1)S(1)}, bf16[64,1024]{1,0:T(8,128)(2,1)S(1)}, u32[]{:S(2)}, u32[]{:S(2)}) collective-permute-start(bf16[64,1024]{1,0:T(8,128)(2,1)S(1)} %slice_bitcast_fusion.2), channel_id=1, source_target_pairs={{0,2},{1,3},{2,0},{3,1},{4,6},{5,7},{6,4},{7,5},{8,10},{9,11},{10,... | collective-permute-start | bytes 393224 | tf_op jit(solution)/shard_map/ppermute | solution.py:124
  273.4 5.7 %reduce-scatter.2.cloned.1.call-done = bf16[512,512]{1,0:T(8,128)(2,1)} async-done(((bf16[8192,512]{1,0:T(8,128)(2,1)}), bf16[512,512]{1,0:T(8,128)(2,1)}) %reduce-scatter.2.cloned.1.call-update) | async-done | bytes 524304 | tf_op jit(solution)/shard_map/reduce_scatter | solution.py:176
  279.2 6.5 %collective-permute-start.17 = (bf16[512,512]{1,0:T(8,128)(2,1)}, bf16[512,512]{1,0:T(8,128)(2,1)S(1)}, u32[]{:S(2)}, u32[]{:S(2)}) collective-permute-start(bf16[512,512]{1,0:T(8,128)(2,1)} %reduce-scatter.2.cloned.1.call-done), channel_id=1, source_target_pairs={{0,0},{1,1},{4,2},{5,3},{6,4},{7,5},{2,6},{3,7},{72,8},{73,9},{76,... | collective-permute-start | bytes 1572872 | tf_op jit(solution)/shard_map/ppermute | solution.py:124
  286.4 12.2 %collective-permute-done.17 = bf16[512,512]{1,0:T(8,128)(2,1)S(1)} collective-permute-done((bf16[512,512]{1,0:T(8,128)(2,1)}, bf16[512,512]{1,0:T(8,128)(2,1)S(1)}, u32[]{:S(2)}, u32[]{:S(2)}) %collective-permute-start.17) | collective-permute-done | bytes 524320 | tf_op jit(solution)/shard_map/ppermute | solution.py:124
  (75 shorter events, 26.3 us)
Async XLA Ops:
  7.2 89.1 %copy-start.1 = (bf16[1024,512]{1,0:T(8,128)(2,1)S(1)}, bf16[1024,512]{1,0:T(8,128)(2,1)}, u32[]{:S(2)}) copy-start(bf16[1024,512]{1,0:T(8,128)(2,1)} %q_ref.3) | copy-start | bytes 3145732
  7.2 153.4 %all-gather.2.cloned.1.call-start = ((), (), s32[]{:S(2)}) async-start(), calls=%async_computation.1 | async-start | bytes 8912896 | tf_op jit(solution)/shard_map/all_gather | solution.py:153
  7.2 28.7 %collective-permute-start.9 = (bf16[512,512]{1,0:T(8,128)(2,1)}, bf16[512,512]{1,0:T(8,128)(2,1)S(1)}, u32[]{:S(2)}, u32[]{:S(2)}) collective-permute-start(bf16[512,512]{1,0:T(8,128)(2,1)} %param.9), channel_id=1, source_target_pairs={{0,0},{1,1},{2,4},{3,5},{4,6},{5,7},{6,2},{7,3},{8,72},{9,73},{10,... | collective-permute-start | bytes 1572872 | tf_op jit(solution)/shard_map/ppermute | solution.py:124
  36.8 242.4 %reduce-scatter.2.cloned.1.call-start = ((), (), s32[]{:S(2)}) async-start(), calls=%async_computation.2 | async-start | bytes 8912896 | tf_op jit(solution)/shard_map/reduce_scatter | solution.py:176
  36.8 48.9 %collective-permute-start.5 = (bf16[1024,1024]{1,0:T(8,128)(2,1)}, bf16[1024,1024]{1,0:T(8,128)(2,1)S(1)}, u32[]{:S(2)}, u32[]{:S(2)}) collective-permute-start(bf16[1024,1024]{1,0:T(8,128)(2,1)} %param.8), channel_id=1, source_target_pairs={{0,16},{1,17},{2,18},{3,19},{4,20},{5,21},{6,22},{7,23},{8,24},{9,... | collective-permute-start | bytes 6291464 | tf_op jit(solution)/shard_map/ppermute | solution.py:124
  36.9 51.2 %collective-permute-start.6 = (bf16[1024,1024]{1,0:T(8,128)(2,1)}, bf16[1024,1024]{1,0:T(8,128)(2,1)S(1)}, u32[]{:S(2)}, u32[]{:S(2)}) collective-permute-start(bf16[1024,1024]{1,0:T(8,128)(2,1)} %param.8), channel_id=1, source_target_pairs={{0,48},{1,49},{2,50},{3,51},{4,52},{5,53},{6,54},{7,55},{8,56},{9,... | collective-permute-start | bytes 6291464 | tf_op jit(solution)/shard_map/ppermute | solution.py:124
  41.8 5.0 %collective-permute-start = (bf16[64,1024]{1,0:T(8,128)(2,1)S(1)}, bf16[64,1024]{1,0:T(8,128)(2,1)S(1)}, u32[]{:S(2)}, u32[]{:S(2)}) collective-permute-start(bf16[64,1024]{1,0:T(8,128)(2,1)S(1)} %get-tuple-element.23), channel_id=1, source_target_pairs={{0,2},{1,3},{2,0},{3,1},{4,6},{5,7},{6,4},{7,5},{8,10},{9,11},{10,... | collective-permute-start | bytes 393224 | tf_op jit(solution)/shard_map/ppermute | solution.py:124
  46.9 15.1 %collective-permute-start.1 = (bf16[128,1024]{1,0:T(8,128)(2,1)S(1)}, bf16[128,1024]{1,0:T(8,128)(2,1)S(1)}, u32[]{:S(2)}, u32[]{:S(2)}) collective-permute-start(bf16[128,1024]{1,0:T(8,128)(2,1)S(1)} %pad_maximum_fusion.2), channel_id=1, source_target_pairs={{0,4},{1,5},{2,6},{3,7},{4,8},{5,9},{6,10},{7,11},{8,12},{9,13},{1... | collective-permute-start | bytes 786440 | tf_op jit(solution)/shard_map/ppermute | solution.py:124
  49.7 14.8 %collective-permute-start.2 = (bf16[128,1024]{1,0:T(8,128)(2,1)S(1)}, bf16[128,1024]{1,0:T(8,128)(2,1)S(1)}, u32[]{:S(2)}, u32[]{:S(2)}) collective-permute-start(bf16[128,1024]{1,0:T(8,128)(2,1)S(1)} %pad_maximum_fusion.2), channel_id=1, source_target_pairs={{0,12},{1,13},{2,14},{3,15},{4,0},{5,1},{6,2},{7,3},{8,4},{9,5},{1... | collective-permute-start | bytes 786440 | tf_op jit(solution)/shard_map/ppermute | solution.py:124
  50.7 24.3 %collective-permute-start.3 = (bf16[128,1024]{1,0:T(8,128)(2,1)S(1)}, bf16[128,1024]{1,0:T(8,128)(2,1)S(1)}, u32[]{:S(2)}, u32[]{:S(2)}) collective-permute-start(bf16[128,1024]{1,0:T(8,128)(2,1)S(1)} %pad_maximum_fusion.2), channel_id=1, source_target_pairs={{0,8},{1,9},{2,10},{3,11},{4,12},{5,13},{6,14},{7,15},{8,0},{9,1},... | collective-permute-start | bytes 786440 | tf_op jit(solution)/shard_map/ppermute | solution.py:124
  75.0 19.4 %collective-permute-start.4 = (bf16[512,1024]{1,0:T(8,128)(2,1)S(1)}, bf16[512,1024]{1,0:T(8,128)(2,1)}, u32[]{:S(2)}, u32[]{:S(2)}) collective-permute-start(bf16[512,1024]{1,0:T(8,128)(2,1)S(1)} %constant_dynamic-update-slice_fusion.2), channel_id=1, source_target_pairs={{0,1},{1,0},{2,3},{3,2},{4,5},{5,4},{6,7},{7,6},{8,9},{9,8},{10,11... | collective-permute-start | bytes 3145736 | tf_op jit(solution)/shard_map/ppermute | solution.py:124
  88.1 28.8 %collective-permute-start.7 = (bf16[512,1024]{1,0:T(8,128)(2,1)}, bf16[512,1024]{1,0:T(8,128)(2,1)}, u32[]{:S(2)}, u32[]{:S(2)}) collective-permute-start(bf16[512,1024]{1,0:T(8,128)(2,1)} %slice.60), channel_id=1, source_target_pairs={{0,16},{1,17},{2,18},{3,19},{4,20},{5,21},{6,22},{7,23},{8,24},{9,... | collective-permute-start | bytes 3145736 | tf_op jit(solution)/shard_map/ppermute | solution.py:124
  90.4 26.4 %collective-permute-start.8 = (bf16[512,1024]{1,0:T(8,128)(2,1)}, bf16[512,1024]{1,0:T(8,128)(2,1)}, u32[]{:S(2)}, u32[]{:S(2)}) collective-permute-start(bf16[512,1024]{1,0:T(8,128)(2,1)} %slice.61), channel_id=1, source_target_pairs={{0,48},{1,49},{2,50},{3,51},{4,52},{5,53},{6,54},{7,55},{8,56},{9,... | collective-permute-start | bytes 3145736 | tf_op jit(solution)/shard_map/ppermute | solution.py:124
  116.8 25.0 %copy-start.14 = (bf16[1024,1024]{1,0:T(8,128)(2,1)S(1)}, bf16[1024,1024]{1,0:T(8,128)(2,1)}, u32[]{:S(2)}) copy-start(bf16[1024,1024]{1,0:T(8,128)(2,1)} %param.8) | copy-start | bytes 6291460
  116.8 25.0 %collective-permute-start.16 = (bf16[1024,512]{1,0:T(8,128)(2,1)S(1)}, bf16[1024,512]{1,0:T(8,128)(2,1)S(1)}, u32[]{:S(2)}, u32[]{:S(2)}) collective-permute-start(bf16[1024,512]{1,0:T(8,128)(2,1)S(1)} %get-tuple-element.17), channel_id=1, source_target_pairs={{0,64},{1,65},{2,66},{3,67},{4,68},{5,69},{6,70},{7,71},{8,72},{9,... | collective-permute-start | bytes 3145736 | tf_op jit(solution)/shard_map/ppermute | solution.py:124
  171.3 49.1 %copy-start.3 = (bf16[1024,512]{1,0:T(8,128)(2,1)S(1)}, bf16[1024,512]{1,0:T(8,128)(2,1)}, u32[]{:S(2)}) copy-start(bf16[1024,512]{1,0:T(8,128)(2,1)} %k_ref.3) | copy-start | bytes 3145732
  171.3 49.1 %copy-start.5 = (bf16[1024,512]{1,0:T(8,128)(2,1)S(1)}, bf16[1024,512]{1,0:T(8,128)(2,1)}, u32[]{:S(2)}) copy-start(bf16[1024,512]{1,0:T(8,128)(2,1)} %v_ref.3) | copy-start | bytes 3145732
  171.3 49.1 %collective-permute-start.10 = (bf16[1024,512]{1,0:T(8,128)(2,1)}, bf16[1024,512]{1,0:T(8,128)(2,1)S(1)}, u32[]{:S(2)}, u32[]{:S(2)}) collective-permute-start(bf16[1024,512]{1,0:T(8,128)(2,1)} %fusion.5), channel_id=1, source_target_pairs={{0,64},{1,65},{2,66},{3,67},{4,68},{5,69},{6,70},{7,71},{8,72},{9,... | collective-permute-start | bytes 3145736 | tf_op jit(solution)/shard_map/ppermute | solution.py:124
  239.9 2.7 collective-permute-start.11
  243.1 26.2 %collective-permute-start.12 = (bf16[2,64,1024]{2,1,0:T(8,128)(2,1)S(1)}, bf16[2,64,1024]{2,1,0:T(8,128)(2,1)S(1)}, u32[]{:S(2)}, u32[]{:S(2)}) collective-permute-start(bf16[2,64,1024]{2,1,0:T(8,128)(2,1)S(1)} %get-tuple-element.18), channel_id=1, source_target_pairs={{0,12},{1,13},{2,14},{3,15},{4,0},{5,1},{6,2},{7,3},{8,4},{9,5},{1... | collective-permute-start | bytes 786440 | tf_op jit(solution)/shard_map/ppermute | solution.py:124
  247.0 22.4 %collective-permute-start.14 = (bf16[2,64,1024]{2,1,0:T(8,128)(2,1)S(1)}, bf16[2,64,1024]{2,1,0:T(8,128)(2,1)S(1)}, u32[]{:S(2)}, u32[]{:S(2)}) collective-permute-start(bf16[2,64,1024]{2,1,0:T(8,128)(2,1)S(1)} %get-tuple-element.19), channel_id=1, source_target_pairs={{0,8},{1,9},{2,10},{3,11},{4,12},{5,13},{6,14},{7,15},{8,0},{9,1},... | collective-permute-start | bytes 786440 | tf_op jit(solution)/shard_map/ppermute | solution.py:124
  247.0 22.4 %collective-permute-start.13 = (bf16[2,64,1024]{2,1,0:T(8,128)(2,1)S(1)}, bf16[2,64,1024]{2,1,0:T(8,128)(2,1)S(1)}, u32[]{:S(2)}, u32[]{:S(2)}) collective-permute-start(bf16[2,64,1024]{2,1,0:T(8,128)(2,1)S(1)} %get-tuple-element.20), channel_id=1, source_target_pairs={{0,4},{1,5},{2,6},{3,7},{4,8},{5,9},{6,10},{7,11},{8,12},{9,13},{1... | collective-permute-start | bytes 786440 | tf_op jit(solution)/shard_map/ppermute | solution.py:124
  269.5 16.1 %collective-permute-start.15 = (bf16[64,1024]{1,0:T(8,128)(2,1)S(1)}, bf16[64,1024]{1,0:T(8,128)(2,1)S(1)}, u32[]{:S(2)}, u32[]{:S(2)}) collective-permute-start(bf16[64,1024]{1,0:T(8,128)(2,1)S(1)} %slice_bitcast_fusion.2), channel_id=1, source_target_pairs={{0,2},{1,3},{2,0},{3,1},{4,6},{5,7},{6,4},{7,5},{8,10},{9,11},{10,... | collective-permute-start | bytes 393224 | tf_op jit(solution)/shard_map/ppermute | solution.py:124
  279.2 19.4 %collective-permute-start.17 = (bf16[512,512]{1,0:T(8,128)(2,1)}, bf16[512,512]{1,0:T(8,128)(2,1)S(1)}, u32[]{:S(2)}, u32[]{:S(2)}) collective-permute-start(bf16[512,512]{1,0:T(8,128)(2,1)} %reduce-scatter.2.cloned.1.call-done), channel_id=1, source_target_pairs={{0,0},{1,1},{4,2},{5,3},{6,4},{7,5},{2,6},{3,7},{72,8},{73,9},{76,... | collective-permute-start | bytes 1572872 | tf_op jit(solution)/shard_map/ppermute | solution.py:124
  (11 other events, 99.8 us)
Sparse Core Ops, SparseCore 0:
  36.9 64.7 all-gather.1
  160.7 118.4 reduce-scatter.1

commit v2 on v1

v2 whole, which is shorter than its diff:
```python
import functools
import math

import jax
import jax.numpy as jnp
import numpy as np
from jax import lax
from jax.experimental import pallas as pl
from jax.experimental.pallas import tpu as pltpu
from jax.sharding import PartitionSpec as P

HD=128; BLK=128; KB=4; CB=8
SCALE=1.0/math.sqrt(HD); EXPSCALE=SCALE*math.log2(math.e)
HALF, CHUNKS, CORE, SLOTS, KEPT = 0, 2, 10, 12, 16
STEPS = (0, 3, 1, 2)
NT=(((1,),(1,)),((),())); TN=(((0,),(0,)),((),())); NN=(((1,),(0,)),((),()))
def dg(a,b,dims): return lax.dot_general(a,b,dims,preferred_element_type=jnp.float32)

def fwd_kernel(heads,table,q_ref,k_ref,v_ref,c_ref,o_ref,p_ref):
    b=pl.program_id(0); width=heads*HD
    keyp=lax.broadcasted_iota(jnp.int32,(BLK,BLK),0); qp=lax.broadcasted_iota(jnp.int32,(BLK,BLK),1)
    rows=[pl.ds(pl.multiple_of(table[b,j]*BLK,BLK),BLK) for j in range(KB)]
    for h in range(heads):
        cols=slice(h*HD,(h+1)*HD); vcols=slice(width+h*HD,width+(h+1)*HD)
        q=q_ref[:,cols]
        s=[dg(c_ref[r,cols],q,NT) for r in rows]
        s.append(jnp.where(keyp<=qp,dg(k_ref[:,cols],q,NT),-jnp.inf))
        m=functools.reduce(jnp.maximum,[jnp.max(t,axis=0,keepdims=True) for t in s])
        e=[jnp.exp2((t-m)*EXPSCALE) for t in s]
        l=functools.reduce(jnp.add,[jnp.sum(t,axis=0,keepdims=True) for t in e])
        r=1.0/l
        p=[(t*r).astype(jnp.bfloat16) for t in e]
        o=dg(p[KB],v_ref[:,cols],TN)
        for j in range(KB): o=o+dg(p[j],c_ref[rows[j],vcols],TN)
        o_ref[:,cols]=o.astype(jnp.bfloat16)
        for j in range(KB+1): p_ref[0,h,j*BLK:(j+1)*BLK,:]=p[j]

def fwd(table,q,k,v,cache):
    T,W=q.shape; heads=W//HD; nb=T//BLK
    blk=pl.BlockSpec((BLK,W),lambda b,t:(b,0))
    return pl.pallas_call(functools.partial(fwd_kernel,heads),
        grid_spec=pltpu.PrefetchScalarGridSpec(num_scalar_prefetch=1,grid=(nb,),
            in_specs=[blk,blk,blk,pl.BlockSpec(cache.shape,lambda b,t:(0,0))],
            out_specs=[blk,pl.BlockSpec((1,heads,(KB+1)*BLK,BLK),lambda b,t:(b,0,0,0))]),
        out_shape=[jax.ShapeDtypeStruct((T,W),jnp.bfloat16),jax.ShapeDtypeStruct((nb,heads,(KB+1)*BLK,BLK),jnp.bfloat16)],
        compiler_params=pltpu.CompilerParams(vmem_limit_bytes=40<<20),
        cost_estimate=pl.CostEstimate(flops=int(2*2*T*W*(KB+1)*BLK),bytes_accessed=12<<20,transcendentals=T*heads*(KB+1)*BLK),
        name="attn_fwd")(table,q,k,v,cache)

def bwd_kernel(heads,table,place,q_ref,k_ref,v_ref,c_ref,p_ref,ga_ref,gb_ref,dq_ref,dk_ref,dv_ref,keep_ref,away_ref,acc):
    b=pl.program_id(0); width=heads*HD
    @pl.when(b==0)
    def _(): acc[...]=jnp.zeros_like(acc)
    rows=[pl.ds(pl.multiple_of(table[b,j]*BLK,BLK),BLK) for j in range(KB)]
    kept=[pl.ds(pl.multiple_of(place[KEPT+table[b,j]]*BLK,BLK),BLK) for j in range(KB)]
    for h in range(heads):
        cols=slice(h*HD,(h+1)*HD); vcols=slice(width+h*HD,width+(h+1)*HD)
        q=q_ref[:,cols]
        do=(ga_ref[:,cols]+gb_ref[:,cols].astype(jnp.float32)).astype(jnp.bfloat16)
        kk=[c_ref[r,cols] for r in rows]+[k_ref[:,cols]]
        vv=[c_ref[r,vcols] for r in rows]+[v_ref[:,cols]]
        pb=[p_ref[0,h,j*BLK:(j+1)*BLK,:] for j in range(KB+1)]
        pf=[t.astype(jnp.float32) for t in pb]
        dp=[dg(t,do,NT) for t in vv]
        delta=functools.reduce(jnp.add,[jnp.sum(a*c,axis=0,keepdims=True) for a,c in zip(pf,dp)])
        ds=[(a*(c-delta)).astype(jnp.bfloat16) for a,c in zip(pf,dp)]
        dq=functools.reduce(jnp.add,[dg(a,c,TN) for a,c in zip(ds,kk)])
        dq_ref[:,cols]=(dq*SCALE).astype(jnp.bfloat16)
        dk_ref[:,cols]=(dg(ds[KB],q,NN)*SCALE).astype(jnp.bfloat16)
        dv_ref[:,cols]=dg(pb[KB],do,NN).astype(jnp.bfloat16)
        for j in range(KB):
            acc[kept[j],cols]+=dg(ds[j],q,NN)
            acc[kept[j],vcols]+=dg(pb[j],do,NN)
    @pl.when(b==pl.num_programs(0)-1)
    def _():
        half=BLK//2
        for ref,core in ((keep_ref,place[CORE]),(away_ref,place[CORE+1])):
            for c in range(CB):
                at=pl.ds(pl.multiple_of(c*BLK+core*half,half),half)
                ref[c*half:(c+1)*half,:width]=(acc[at,:width]*SCALE).astype(jnp.bfloat16)
                ref[c*half:(c+1)*half,width:]=acc[at,width:].astype(jnp.bfloat16)

def bwd(table,place,q,k,v,cache,p,ga,gb):
    T,W=q.shape; heads=W//HD; nb=T//BLK
    blk=pl.BlockSpec((BLK,W),lambda b,t,w:(b,0))
    full=pl.BlockSpec(cache.shape,lambda b,t,w:(0,0))
    part=pl.BlockSpec((cache.shape[0]//2,cache.shape[1]),lambda b,t,w:(0,0))
    return pl.pallas_call(functools.partial(bwd_kernel,heads),
        grid_spec=pltpu.PrefetchScalarGridSpec(num_scalar_prefetch=2,grid=(nb,),
            in_specs=[blk,blk,blk,full,pl.BlockSpec((1,heads,(KB+1)*BLK,BLK),lambda b,t,w:(b,0,0,0)),blk,blk],
            out_specs=[blk,blk,blk,part,part],
            scratch_shapes=[pltpu.VMEM(cache.shape,jnp.float32)]),
        out_shape=[jax.ShapeDtypeStruct((T,W),jnp.bfloat16)]*3+[jax.ShapeDtypeStruct((cache.shape[0]//2,cache.shape[1]),jnp.bfloat16)]*2,
        compiler_params=pltpu.CompilerParams(vmem_limit_bytes=40<<20),
        cost_estimate=pl.CostEstimate(flops=int(4*2*T*W*(KB+1)*BLK),bytes_accessed=20<<20,transcendentals=0),
        name="attn_bwd")(table,place,q,k,v,cache,p,ga,gb)


VMEM_LIMIT = 56 << 20


def project_kernel(other, place, *refs):
    w_ref, o_ref = refs[-2:]
    depth = refs[0].shape[1]

    def total(half):
        parts = []
        for j in range(4):
            rows = pl.ds(pl.multiple_of(place[CHUNKS + 4 * other + j] * depth, depth), depth)
            parts.append(dg(refs[2 * j + half][...], w_ref[rows, :], NN))
        return functools.reduce(jnp.add, parts).astype(o_ref.dtype)

    first = pl.program_id(0) < pl.num_programs(0) // 2

    @pl.when(first)
    def _():
        o_ref[...] = total(0)

    @pl.when(jnp.logical_not(first))
    def _():
        o_ref[...] = total(1)


def project(other, place, columns, weight, dtype):
    half, depth = columns[0].shape
    width = weight.shape[1]
    steps = 4
    block = 2 * half // steps
    upper = pl.BlockSpec((block, depth), lambda i, p: (jnp.minimum(i, steps // 2 - 1), 0))
    lower = pl.BlockSpec((block, depth), lambda i, p: (jnp.maximum(i - steps // 2, 0), 0))
    return pl.pallas_call(
        functools.partial(project_kernel, other),
        grid_spec=pltpu.PrefetchScalarGridSpec(
            num_scalar_prefetch=1,
            grid=(steps,),
            in_specs=[upper, lower] * 4 + [pl.BlockSpec((4 * depth, width), lambda i, p: (p[HALF + other], 0))],
            out_specs=pl.BlockSpec((block, width), lambda i, p: (i, 0)),
        ),
        out_shape=jax.ShapeDtypeStruct((2 * half, width), dtype),
        compiler_params=pltpu.CompilerParams(vmem_limit_bytes=VMEM_LIMIT),
        cost_estimate=pl.CostEstimate(flops=16 * half * depth * width, bytes_accessed=14 << 20, transcendentals=0),
        name="project",
    )(place, *columns, weight)


def outer_kernel(place, *refs):
    chunks, own, other, rest = refs[:8], refs[8], refs[9], refs[10:]
    picked, attn = rest[-2:]
    half = chunks[0].shape[0]
    width = own.shape[1]
    upper = place[HALF]

    @pl.when(upper == 0)
    def _():
        attn[:, :width] = own[...]
        attn[:, width:] = other[...]

    @pl.when(upper != 0)
    def _():
        attn[:, :width] = other[...]
        attn[:, width:] = own[...]

    for slot in range(4):
        for j in range(4):

            @pl.when(place[SLOTS + slot] == j)
            def _():
                picked[:half, :] = chunks[2 * j][...]
                picked[half:, :] = chunks[2 * j + 1][...]

        out = dg(picked[...], attn[...], TN)
        size = out.shape[0]
        here = slice(slot * size, (slot + 1) * size)
        if len(rest) == 3:
            rest[0][here, :] = out.astype(jnp.bfloat16)
        else:
            out = (out + rest[0][here, :].astype(jnp.float32)).astype(jnp.bfloat16)
            for f in range(2):
                away = f + upper - 2 * f * upper
                to = 4 * f + slot + away * (3 - 2 * slot)
                rest[1][pl.ds(pl.multiple_of(to * size, size), size), :] = out[:, f * width : (f + 1) * width]


def outer(place, columns, own, other, added=None):
    half, depth = columns[0].shape
    width = own.shape[1]
    size = depth // 2
    core = CORE + int(added is None)
    full = pl.BlockSpec(own.shape, lambda i, p: (0, 0))
    both = pl.BlockSpec((4 * size, 2 * width), lambda i, p: (0, 0))
    shape = (4 * size, 2 * width) if added is None else (8 * size, width)
    return pl.pallas_call(
        outer_kernel,
        grid_spec=pltpu.PrefetchScalarGridSpec(
            num_scalar_prefetch=1,
            grid=(1,),
            in_specs=[pl.BlockSpec((half, size), lambda i, p: (0, p[core]))] * 8
            + [full, full]
            + ([] if added is None else [both]),
            out_specs=pl.BlockSpec(shape, lambda i, p: (0, 0)),
            scratch_shapes=[pltpu.VMEM((2 * half, size), jnp.bfloat16), pltpu.VMEM((2 * half, 2 * width), jnp.bfloat16)],
        ),
        out_shape=jax.ShapeDtypeStruct(shape, jnp.bfloat16),
        compiler_params=pltpu.CompilerParams(vmem_limit_bytes=VMEM_LIMIT),
        cost_estimate=pl.CostEstimate(flops=32 * half * size * width, bytes_accessed=12 << 20, transcendentals=0),
        name="outer",
    )(place, *columns, own, other, *([] if added is None else [added]))


AXES = ("row", "col")

def device(xh, y, z, xl, core):
    return (xh * 4 + y) * 16 + (z * 2 + xl) * 2 + core


def every():
    for xh in range(2):
        for y in range(4):
            for z in range(4):
                for xl in range(2):
                    for core in range(2):
                        yield xh, y, z, xl, core


def shifted(xh=0, y=0, z=0, xl=0, core=0):
    return [
        (device(*d), device(d[0] ^ xh, (d[1] + y) % 4, (d[2] + z) % 4, d[3] ^ xl, d[4] ^ core)) for d in every()
    ]


def swap_pairs():
    pairs = []
    for d in every():
        xh, y, z, xl, core = d
        upper, lower = z // 2, z % 2
        away = int(upper != xh)
        pairs.append((device(*d), device(upper, y, xh * 2 + (lower ^ away), xl ^ away, core)))
    return pairs


def place_table():
    rows = []
    for xh, y, z, xl, core in every():
        owners = [(y + step) % 4 for step in STEPS]
        rows.append(
            [xh, 1 - xh, *owners, *(3 - o for o in owners), core, 1 - core, *(owners.index(t) for t in range(4))]
            + [STEPS.index((c // 2 - z) % 4) * 2 + (c % 2 ^ xl) for c in range(CB)]
        )
    return np.array(rows, np.int32)


def send(array, pairs):
    return lax.ppermute(array, AXES, pairs)


def f32(array):
    return array.astype(jnp.float32)


def per_device(grad_out, proj_weight, queries, keys, values, cache_keys, cache_values, block_table):
    bf16 = jnp.bfloat16
    tokens, width = queries.shape
    depth = grad_out.shape[1]
    place = lax.dynamic_index_in_dim(
        jnp.asarray(place_table()), lax.axis_index("row") * 16 + lax.axis_index("col"), keepdims=False
    )
    swap = swap_pairs()
    half = tokens // 2

    rows = cache_keys.shape[0]
    mine = jnp.concatenate([cache_keys, cache_values], axis=1)
    cache = lax.all_gather(mine, "col", axis=0, tiled=True)

    upper, lower = grad_out[:half], grad_out[half:]
    before_upper, after_lower = send(upper, shifted(y=1)), send(lower, shifted(y=3))
    before_lower, after_upper = send(lower, shifted(y=1)), send(upper, shifted(y=3))
    swapped, before_upper, after_lower = lax.optimization_barrier((send(proj_weight, swap), before_upper, after_lower))
    weight = lax.all_gather(swapped, "col", axis=0, tiled=True)
    columns = (
        upper,
        lower,
        before_upper,
        before_lower,
        after_upper,
        after_lower,
        send(before_upper, shifted(y=1)),
        send(after_lower, shifted(y=3)),
    )

    attn_out, probs = fwd(block_table, queries, keys, values, cache)
    attn_other = send(attn_out, shifted(xh=1))

    theirs = outer(place, columns, attn_out, attn_other)
    theirs, other_part = lax.optimization_barrier((theirs, project(1, place, columns, weight, bf16)))
    from_other = send(other_part, shifted(xh=1))
    own_part = project(0, place, columns, weight, jnp.float32)
    pieces = outer(place, columns, attn_out, attn_other, send(theirs, shifted(core=1)))
    pieces, from_other, own_part = lax.optimization_barrier((pieces, from_other, own_part))
    groups = [[2 * i + c for i in range(8)] for c in range(2)]
    pieces = lax.all_to_all(pieces, "col", split_axis=0, concat_axis=0, axis_index_groups=groups, tiled=True)
    total = jnp.sum(f32(pieces.reshape(8, -1, width)), axis=0).astype(bf16)
    grad_weight = send(total, swap)

    grad_q, grad_k, grad_v, keep, away = bwd(
        block_table, place, queries, keys, values, cache, probs, own_part, from_other
    )
    parts = (f32(keep) + f32(send(away, shifted(core=1)))).astype(bf16).reshape(4, 2 * rows, 2 * width)
    parts = sum([f32(parts[0])] + [f32(send(parts[i], shifted(z=STEPS[i]))) for i in range(1, 4)]).astype(bf16)
    total = f32(parts[:rows]) + f32(send(parts[rows:], shifted(xl=1)))
    return (grad_q, grad_k, grad_v, total[:, :width], total[:, width:], grad_weight)


def solution(mesh):
    both = P("col", "row")
    return jax.shard_map(
        per_device, mesh=mesh, in_specs=(both,) * 7 + (P("col", None),), out_specs=(both,) * 6, check_vma=False
    )
```

time: 309 us -> 272 us (0.88)
  Pallas kernels: 35.1 us -> 80.1 us
  matrix products: 43.9 us -> 0 us
  waiting for transfers between devices: 155 us -> 117 us
  other arithmetic: 9.69 us -> 5.19 us
  starting transfers between devices: 33.6 us -> 37.8 us
    pallas_call x0 -> x4, Pallas kernels: none -> 44.3 us  [the longest x2 23.5 us: outer(): pl.pallas_call(outer_kernel, grid_spec=pltpu.PrefetchScalarGridSpec(num_s...]
    dot_general x4 -> x0, matrix products: 43.9 us -> none  [the longest x2 25.1 us: weight_part(): lax.dot_general(columns, attn, (((0,), (0,)), ((), ())), preferred_elemen...]
    ppermute x18 -> x16, waiting for transfers between devices: 149 us -> 111 us  [send(): return lax.ppermute(array, AXES, pairs)]
    all_to_all x0 -> x1, starting transfers between devices: none -> 6.8 us  [per_device(): lax.all_to_all(pieces, 'col', split_axis=0, concat_axis=0, axis_index_gro...]
    all_gather x1 -> x2, waiting for transfers between devices: 0.02 us -> 5.83 us  [the longest x1 5.83 us: per_device(): cache = lax.all_gather(mine, 'col', axis=0, tiled=True)]
    reduce_scatter x1 -> x0, waiting for transfers between devices: 5.74 us -> none  [per_device(): lax.psum_scatter(partial, 'col', scatter_dimension=0, tiled=True)]
    concatenate x2 -> x1, other arithmetic: 7.27 us -> 1.54 us  [per_device(): mine = jnp.concatenate([cache_keys, cache_values], axis=1)]
    ppermute x18 -> x16, starting transfers between devices: 33.5 us -> 30.9 us  [send(): return lax.ppermute(array, AXES, pairs)]
  transfers between devices with their start and end apart: 20 -> 19, of which waited for: 12 -> 12; matrix products, arithmetic and copies ran while one was open for 19% -> 3% of each run, Pallas kernels for 11% -> 26%
where the time goes in v2:
time: 272 us; the launch traced here: 271 us
  waiting for transfers between devices  117 us (43%)
  Pallas kernels  80.1 us (29%)
  starting transfers between devices  37.8 us (14%)
  local copies, waits for them, and re-layouts  17.3 us (6%)
  between operations  14.2 us (5%)
  other arithmetic  5.19 us (2%)
    ppermute x16, waiting for transfers between devices, send(): return lax.ppermute(array, AXES, pairs)  111 us
    ppermute x16, starting transfers between devices, send(): return lax.ppermute(array, AXES, pairs)  30.9 us
    pallas_call x2, Pallas kernels, outer(): pl.pallas_call(outer_kernel, grid_spec=pltpu.PrefetchScalarGridSpec(num_s...  23.5 us
    pallas_call x2, Pallas kernels, project(): pl.pallas_call(functools.partial(project_kernel, other), grid_spec=pltpu....  20.8 us
    pallas_call x1, Pallas kernels, bwd(): pl.pallas_call(functools.partial(bwd_kernel, heads), grid_spec=pltpu.Pref...  19.4 us
    pallas_call x1, Pallas kernels, fwd(): pl.pallas_call(functools.partial(fwd_kernel, heads), grid_spec=pltpu.Pref...  16.4 us
    unnamed x32, local copies, waits for them, and re-layouts  12.1 us
    all_to_all x1, starting transfers between devices, per_device(): lax.all_to_all(pieces, 'col', split_axis=0, concat_axis=0, axis_index_gro...  6.8 us
  transfers between devices with their start and end apart: 19, of which 12 were waited for; matrix products, arithmetic and copies ran while one was open for 3% of the time, Pallas kernels for 26%

profile of v2, /device:TPU:6, one launch (start us, length us, event | category | flops | bytes accessed | tf_op | source)
XLA Modules:
  0.0 271.3 jit_solution(6748171947630980780)
XLA Ops:
  8.9 3.2 %fusion = (bf16[512,1024]{1,0:T(8,128)(2,1)}, bf16[512,1024]{1,0:T(8,128)(2,1)}) fusion(bf16[1024,1024]{1,0:T(8,128)(2,1)} %param.9), kind=kLoop, calls=%fused_computation.5 | loop fusion | bytes 4194304 | tf_op jit(solution)/shard_map/slice | solution.py:274
  12.1 3.0 %collective-permute-start.2 = (bf16[512,1024]{1,0:T(8,128)(2,1)}, bf16[512,1024]{1,0:T(8,128)(2,1)}, u32[]{:S(2)}, u32[]{:S(2)}) collective-permute-start(bf16[512,1024]{1,0:T(8,128)(2,1)} %get-tuple-element.36.refs_1_), channel_id=1, source_target_pairs={{0,48},{1,49},{2,50},{3,51},{4,52},{5,53},{6,54},{7,55},{8,56},{9,... | collective-permute-start | bytes 3145736 | tf_op jit(solution)/shard_map/ppermute | solution.py:253
  15.1 5.9 %collective-permute-start = (bf16[512,512]{1,0:T(8,128)(2,1)S(1)}, bf16[512,512]{1,0:T(8,128)(2,1)}, u32[]{:S(2)}, u32[]{:S(2)}) collective-permute-start(bf16[512,512]{1,0:T(8,128)(2,1)S(1)} %copy-done.14), channel_id=1, source_target_pairs={{0,0},{1,1},{2,2},{3,3},{4,4},{5,5},{6,6},{7,7},{8,70},{9,71},{10,... | collective-permute-start | bytes 1572872 | tf_op jit(solution)/shard_map/ppermute | solution.py:253
  21.0 12.8 %collective-permute-done = bf16[512,512]{1,0:T(8,128)(2,1)} collective-permute-done((bf16[512,512]{1,0:T(8,128)(2,1)S(1)}, bf16[512,512]{1,0:T(8,128)(2,1)}, u32[]{:S(2)}, u32[]{:S(2)}) %collective-permute-start) | collective-permute-done | bytes 524320 | tf_op jit(solution)/shard_map/ppermute | solution.py:253
  33.8 4.0 %collective-permute-done.2.refs_5_ = bf16[512,1024]{1,0:T(8,128)(2,1)} collective-permute-done((bf16[512,1024]{1,0:T(8,128)(2,1)}, bf16[512,1024]{1,0:T(8,128)(2,1)}, u32[]{:S(2)}, u32[]{:S(2)}) %collective-permute-start.2) | collective-permute-done | bytes 1048608 | tf_op jit(solution)/shard_map/ppermute | solution.py:253
  37.8 3.4 %collective-permute-done.1.refs_2_ = bf16[512,1024]{1,0:T(8,128)(2,1)} collective-permute-done((bf16[512,1024]{1,0:T(8,128)(2,1)}, bf16[512,1024]{1,0:T(8,128)(2,1)}, u32[]{:S(2)}, u32[]{:S(2)}) %collective-permute-start.1) | collective-permute-done | bytes 1048608 | tf_op jit(solution)/shard_map/ppermute | solution.py:253
  41.3 3.2 %collective-permute-start.4 = (bf16[512,1024]{1,0:T(8,128)(2,1)}, bf16[512,1024]{1,0:T(8,128)(2,1)}, u32[]{:S(2)}, u32[]{:S(2)}) collective-permute-start(bf16[512,1024]{1,0:T(8,128)(2,1)} %get-tuple-element.37.refs_0_), channel_id=1, source_target_pairs={{0,48},{1,49},{2,50},{3,51},{4,52},{5,53},{6,54},{7,55},{8,56},{9,... | collective-permute-start | bytes 3145736 | tf_op jit(solution)/shard_map/ppermute | solution.py:253
  44.7 3.2 %collective-permute-start.6 = (bf16[512,1024]{1,0:T(8,128)(2,1)}, bf16[512,1024]{1,0:T(8,128)(2,1)}, u32[]{:S(2)}, u32[]{:S(2)}) collective-permute-start(bf16[512,1024]{1,0:T(8,128)(2,1)} %collective-permute-done.2.refs_5_), channel_id=1, source_target_pairs={{0,48},{1,49},{2,50},{3,51},{4,52},{5,53},{6,54},{7,55},{8,56},{9,... | collective-permute-start | bytes 3145736 | tf_op jit(solution)/shard_map/ppermute | solution.py:253
  47.9 5.8 %all-gather.3.cloned.1.call-done.c_ref = bf16[1024,1024]{1,0:T(8,128)(2,1)} async-done(((bf16[64,1024]{1,0:T(8,128)(2,1)}), bf16[1024,1024]{1,0:T(8,128)(2,1)}) %all-gather.3.cloned.1.call-update) | async-done | bytes 2097168 | tf_op jit(solution)/shard_map/all_gather | solution.py:272
  55.3 16.4 %attn_fwd.1 = (bf16[1024,512]{1,0:T(8,128)(2,1)}, bf16[8,4,640,128]{3,2,1,0:T(8,128)(2,1)S(1)}) custom-call(s32[8,4]{1,0:T(8,128)S(1)} %copy.16.table, bf16[1024,512]{1,0:T(8,128)(2,1)S(1)} %copy-done.4, bf16[1024,512]{1,0:T(8,128)(2,1)S(1)} %copy-done.5, bf16[1024,512]{1,0:T(8,128)(2,1)S(1)} %copy-done.7, bf16[1024,1024]{1,0:T(8,128)(2,1)S(1)} %copy-done), custom_call_target="tpu_custom_call" | custom-call | flops 1342177280 | bytes 12582912 | tf_op jit(solution)/shard_map/attn_fwd/pallas_call | solution.py:41
  77.9 11.2 %collective-permute-done.5.refs_6_ = bf16[512,1024]{1,0:T(8,128)(2,1)} collective-permute-done((bf16[512,1024]{1,0:T(8,128)(2,1)}, bf16[512,1024]{1,0:T(8,128)(2,1)}, u32[]{:S(2)}, u32[]{:S(2)}) %collective-permute-start.5) | collective-permute-done | bytes 1048608 | tf_op jit(solution)/shard_map/ppermute | solution.py:253
  89.0 35.0 %collective-permute-done.7.refs_9_ = bf16[1024,512]{1,0:T(8,128)(2,1)S(1)} collective-permute-done((bf16[1024,512]{1,0:T(8,128)(2,1)}, bf16[1024,512]{1,0:T(8,128)(2,1)S(1)}, u32[]{:S(2)}, u32[]{:S(2)}) %collective-permute-start.7) | collective-permute-done | bytes 1048608 | tf_op jit(solution)/shard_map/ppermute | solution.py:253
  125.0 11.1 %outer.2 = bf16[2048,1024]{1,0:T(8,128)(2,1)} custom-call(s32[24]{0:T(128)} %dynamic-slice_bitcast_fusion.place, bf16[512,1024]{1,0:T(8,128)(2,1)} %get-tuple-element.37.refs_0_, bf16[512,1024]{1,0:T(8,128)(2,1)} %get-tuple-element.36.refs_1_, bf16[512,1024]{1,0:T(8,128)(2,1)} %collective-permute-done.1.refs_2_, ...), custom_call_target="tpu_custom_call" | custom-call | flops 4294967296 | bytes 12582912 | tf_op jit(solution)/shard_map/outer/pallas_call | solution.py:192
  136.1 10.3 %project.2 = bf16[1024,512]{1,0:T(8,128)(2,1)} custom-call(s32[24]{0:T(128)} %dynamic-slice_bitcast_fusion.place, bf16[512,1024]{1,0:T(8,128)(2,1)} %get-tuple-element.37.refs_0_, bf16[512,1024]{1,0:T(8,128)(2,1)} %get-tuple-element.36.refs_1_, bf16[512,1024]{1,0:T(8,128)(2,1)} %collective-permute-done.1.refs_2_, ...), custom_call_target="tpu_custom_call" | custom-call | flops 4294967296 | bytes 14680064 | tf_op jit(solution)/shard_map/project/pallas_call | solution.py:131
  149.3 10.5 %project.3.ga_ref = f32[1024,512]{1,0:T(8,128)} custom-call(s32[24]{0:T(128)} %dynamic-slice_bitcast_fusion.place, bf16[512,1024]{1,0:T(8,128)(2,1)} %get-tuple-element.37.refs_0_, bf16[512,1024]{1,0:T(8,128)(2,1)} %get-tuple-element.36.refs_1_, bf16[512,1024]{1,0:T(8,128)(2,1)} %collective-permute-done.1.refs_2_, ...), custom_call_target="tpu_custom_call" | custom-call | flops 4294967296 | bytes 14680064 | tf_op jit(solution)/shard_map/project/pallas_call | solution.py:131
  159.9 12.4 %outer.3 = bf16[4096,512]{1,0:T(8,128)(2,1)} custom-call(s32[24]{0:T(128)} %dynamic-slice_bitcast_fusion.place, bf16[512,1024]{1,0:T(8,128)(2,1)} %get-tuple-element.37.refs_0_, bf16[512,1024]{1,0:T(8,128)(2,1)} %get-tuple-element.36.refs_1_, bf16[512,1024]{1,0:T(8,128)(2,1)} %collective-permute-done.1.refs_2_, ...), custom_call_target="tpu_custom_call" | custom-call | flops 4294967296 | bytes 12582912 | tf_op jit(solution)/shard_map/outer/pallas_call | solution.py:192
  174.7 6.8 %all-to-all-start = ((bf16[8,512,512]{2,1,0:T(8,128)(2,1)}), bf16[8,512,512]{2,1,0:T(8,128)(2,1)}, u32[]{:S(2)}, u32[]{:S(2)}) async-start(bf16[8,512,512]{2,1,0:T(8,128)(2,1)} %bitcast.3), calls=%async_computation | async-start | bytes 8388608 | tf_op jit(solution)/shard_map/all_to_all | solution.py:300
  186.8 19.4 %attn_bwd.1 = (bf16[1024,512]{1,0:T(8,128)(2,1)}, bf16[1024,512]{1,0:T(8,128)(2,1)}, bf16[1024,512]{1,0:T(8,128)(2,1)}, bf16[512,1024]{1,0:T(8,128)(2,1)S(1)}, bf16[512,1024]{1,0:T(8,128)(2,1)S(1)}) custom-call(s32[8,4]{1,0:T(8,128)S(1)} %copy.16.table, s32[24]{0:T(128)S(1)} %copy-done.11, bf16[1024,512]{1,0:T(8,128)(2,1)S(1)} %copy-done.4, ...), custom_call_target="tpu_custom_call" | custom-call | flops 2684354560 | bytes 20971520 | tf_op jit(solution)/shard_map/attn_bwd/pallas_call | solution.py:88
  213.9 20.0 %collective-permute-done.11 = bf16[128,1024]{1,0:T(8,128)(2,1)S(1)} collective-permute-done((bf16[128,1024]{1,0:T(8,128)(2,1)S(1)}, bf16[128,1024]{1,0:T(8,128)(2,1)S(1)}, u32[]{:S(2)}, u32[]{:S(2)}) %collective-permute-start.11) | collective-permute-done | bytes 262176 | tf_op jit(solution)/shard_map/ppermute | solution.py:253
  233.9 3.0 %collective-permute-done.13 = bf16[128,1024]{1,0:T(8,128)(2,1)S(1)} collective-permute-done((bf16[128,1024]{1,0:T(8,128)(2,1)S(1)}, bf16[128,1024]{1,0:T(8,128)(2,1)S(1)}, u32[]{:S(2)}, u32[]{:S(2)}) %collective-permute-start.13) | collective-permute-done | bytes 262176 | tf_op jit(solution)/shard_map/ppermute | solution.py:253
  236.9 3.7 %collective-permute-done.12 = bf16[128,1024]{1,0:T(8,128)(2,1)S(1)} collective-permute-done((bf16[128,1024]{1,0:T(8,128)(2,1)S(1)}, bf16[128,1024]{1,0:T(8,128)(2,1)S(1)}, u32[]{:S(2)}, u32[]{:S(2)}) %collective-permute-start.12) | collective-permute-done | bytes 262176 | tf_op jit(solution)/shard_map/ppermute | solution.py:253
  241.7 3.1 %reduce_sum.12 = bf16[512,512]{1,0:T(8,128)(2,1)S(1)} reduce(bf16[8,512,512]{2,1,0:T(8,128)(2,1)} %all-to-all-done, bf16[]{:T(256)} %constant.21.clone.1), dimensions={0}, to_apply=%region_0.1 | reduce | flops 1835008 | bytes 4718594 | tf_op jit(solution)/shard_map/reduce_sum | solution.py:301
  244.8 4.6 %collective-permute-start.15 = (bf16[512,512]{1,0:T(8,128)(2,1)S(1)}, bf16[512,512]{1,0:T(8,128)(2,1)S(1)}, u32[]{:S(2)}, u32[]{:S(2)}) collective-permute-start(bf16[512,512]{1,0:T(8,128)(2,1)S(1)} %reduce_sum.12), channel_id=1, source_target_pairs={{0,0},{1,1},{2,2},{3,3},{4,4},{5,5},{6,6},{7,7},{8,70},{9,71},{10,... | collective-permute-start | bytes 1572872 | tf_op jit(solution)/shard_map/ppermute | solution.py:253
  250.2 13.4 %collective-permute-done.15 = bf16[512,512]{1,0:T(8,128)(2,1)S(1)} collective-permute-done((bf16[512,512]{1,0:T(8,128)(2,1)S(1)}, bf16[512,512]{1,0:T(8,128)(2,1)S(1)}, u32[]{:S(2)}, u32[]{:S(2)}) %collective-permute-start.15) | collective-permute-done | bytes 524320 | tf_op jit(solution)/shard_map/ppermute | solution.py:253
  (64 shorter events, 31.5 us)
Async XLA Ops:
  7.2 46.6 %all-gather.3.cloned.1.call-start = ((), (), s32[]{:S(2)}) async-start(), calls=%async_computation.1 | async-start | bytes 2228224 | tf_op jit(solution)/shard_map/all_gather | solution.py:272
  8.8 35.8 %copy-start.13 = (s32[8,4]{0,1:T(4,128)S(1)}, s32[8,4]{0,1:T(4,128)}, u32[]{:S(2)}) copy-start(s32[8,4]{0,1:T(4,128)} %param.16) | copy-start | bytes 388
  8.8 44.9 %copy-start.4 = (bf16[1024,512]{1,0:T(8,128)(2,1)S(1)}, bf16[1024,512]{1,0:T(8,128)(2,1)}, u32[]{:S(2)}) copy-start(bf16[1024,512]{1,0:T(8,128)(2,1)} %q_ref.3) | copy-start | bytes 3145732
  8.8 44.9 %copy-start.5 = (bf16[1024,512]{1,0:T(8,128)(2,1)S(1)}, bf16[1024,512]{1,0:T(8,128)(2,1)}, u32[]{:S(2)}) copy-start(bf16[1024,512]{1,0:T(8,128)(2,1)} %k_ref.3) | copy-start | bytes 3145732
  8.8 44.9 %copy-start.7 = (bf16[1024,512]{1,0:T(8,128)(2,1)S(1)}, bf16[1024,512]{1,0:T(8,128)(2,1)}, u32[]{:S(2)}) copy-start(bf16[1024,512]{1,0:T(8,128)(2,1)} %v_ref.3) | copy-start | bytes 3145732
  8.8 127.3 %all-gather.5.cloned.1.call-start = ((), (), s32[]{:S(2)}) async-start(), calls=%async_computation.2 | async-start | bytes 8912896 | tf_op jit(solution)/shard_map/all_gather | solution.py:278
  12.1 25.7 %collective-permute-start.2 = (bf16[512,1024]{1,0:T(8,128)(2,1)}, bf16[512,1024]{1,0:T(8,128)(2,1)}, u32[]{:S(2)}, u32[]{:S(2)}) collective-permute-start(bf16[512,1024]{1,0:T(8,128)(2,1)} %get-tuple-element.36.refs_1_), channel_id=1, source_target_pairs={{0,48},{1,49},{2,50},{3,51},{4,52},{5,53},{6,54},{7,55},{8,56},{9,... | collective-permute-start | bytes 3145736 | tf_op jit(solution)/shard_map/ppermute | solution.py:253
  15.1 26.1 %collective-permute-start.1 = (bf16[512,1024]{1,0:T(8,128)(2,1)}, bf16[512,1024]{1,0:T(8,128)(2,1)}, u32[]{:S(2)}, u32[]{:S(2)}) collective-permute-start(bf16[512,1024]{1,0:T(8,128)(2,1)} %get-tuple-element.37.refs_0_), channel_id=1, source_target_pairs={{0,16},{1,17},{2,18},{3,19},{4,20},{5,21},{6,22},{7,23},{8,24},{9,... | collective-permute-start | bytes 3145736 | tf_op jit(solution)/shard_map/ppermute | solution.py:253
  15.1 18.7 %collective-permute-start = (bf16[512,512]{1,0:T(8,128)(2,1)S(1)}, bf16[512,512]{1,0:T(8,128)(2,1)}, u32[]{:S(2)}, u32[]{:S(2)}) collective-permute-start(bf16[512,512]{1,0:T(8,128)(2,1)S(1)} %copy-done.14), channel_id=1, source_target_pairs={{0,0},{1,1},{2,2},{3,3},{4,4},{5,5},{6,6},{7,7},{8,70},{9,71},{10,... | collective-permute-start | bytes 1572872 | tf_op jit(solution)/shard_map/ppermute | solution.py:253
  41.3 36.6 %collective-permute-start.3 = (bf16[512,1024]{1,0:T(8,128)(2,1)}, bf16[512,1024]{1,0:T(8,128)(2,1)}, u32[]{:S(2)}, u32[]{:S(2)}) collective-permute-start(bf16[512,1024]{1,0:T(8,128)(2,1)} %get-tuple-element.36.refs_1_), channel_id=1, source_target_pairs={{0,16},{1,17},{2,18},{3,19},{4,20},{5,21},{6,22},{7,23},{8,24},{9,... | collective-permute-start | bytes 3145736 | tf_op jit(solution)/shard_map/ppermute | solution.py:253
  41.3 36.5 %collective-permute-start.4 = (bf16[512,1024]{1,0:T(8,128)(2,1)}, bf16[512,1024]{1,0:T(8,128)(2,1)}, u32[]{:S(2)}, u32[]{:S(2)}) collective-permute-start(bf16[512,1024]{1,0:T(8,128)(2,1)} %get-tuple-element.37.refs_0_), channel_id=1, source_target_pairs={{0,48},{1,49},{2,50},{3,51},{4,52},{5,53},{6,54},{7,55},{8,56},{9,... | collective-permute-start | bytes 3145736 | tf_op jit(solution)/shard_map/ppermute | solution.py:253
  44.7 44.4 %collective-permute-start.5 = (bf16[512,1024]{1,0:T(8,128)(2,1)}, bf16[512,1024]{1,0:T(8,128)(2,1)}, u32[]{:S(2)}, u32[]{:S(2)}) collective-permute-start(bf16[512,1024]{1,0:T(8,128)(2,1)} %collective-permute-done.1.refs_2_), channel_id=1, source_target_pairs={{0,16},{1,17},{2,18},{3,19},{4,20},{5,21},{6,22},{7,23},{8,24},{9,... | collective-permute-start | bytes 3145736 | tf_op jit(solution)/shard_map/ppermute | solution.py:253
  44.7 44.4 %collective-permute-start.6 = (bf16[512,1024]{1,0:T(8,128)(2,1)}, bf16[512,1024]{1,0:T(8,128)(2,1)}, u32[]{:S(2)}, u32[]{:S(2)}) collective-permute-start(bf16[512,1024]{1,0:T(8,128)(2,1)} %collective-permute-done.2.refs_5_), channel_id=1, source_target_pairs={{0,48},{1,49},{2,50},{3,51},{4,52},{5,53},{6,54},{7,55},{8,56},{9,... | collective-permute-start | bytes 3145736 | tf_op jit(solution)/shard_map/ppermute | solution.py:253
  74.1 49.9 %collective-permute-start.7 = (bf16[1024,512]{1,0:T(8,128)(2,1)}, bf16[1024,512]{1,0:T(8,128)(2,1)S(1)}, u32[]{:S(2)}, u32[]{:S(2)}) collective-permute-start(bf16[1024,512]{1,0:T(8,128)(2,1)} %get-tuple-element.24.refs_8_), channel_id=1, source_target_pairs={{0,64},{1,65},{2,66},{3,67},{4,68},{5,69},{6,70},{7,71},{8,72},{9,... | collective-permute-start | bytes 3145736 | tf_op jit(solution)/shard_map/ppermute | solution.py:253
  146.5 13.4 %collective-permute-start.8 = (bf16[2048,1024]{1,0:T(8,128)(2,1)}, bf16[2048,1024]{1,0:T(8,128)(2,1)}, u32[]{:S(2)}, u32[]{:S(2)}) collective-permute-start(bf16[2048,1024]{1,0:T(8,128)(2,1)} %outer.2), channel_id=1, source_target_pairs={{0,1},{1,0},{2,3},{3,2},{4,5},{5,4},{6,7},{7,6},{8,9},{9,8},{10,11... | collective-permute-start | bytes 12582920 | tf_op jit(solution)/shard_map/ppermute | solution.py:253
  146.5 27.3 %collective-permute-start.9 = (bf16[1024,512]{1,0:T(8,128)(2,1)}, bf16[1024,512]{1,0:T(8,128)(2,1)S(1)}, u32[]{:S(2)}, u32[]{:S(2)}) collective-permute-start(bf16[1024,512]{1,0:T(8,128)(2,1)} %project.2), channel_id=1, source_target_pairs={{0,64},{1,65},{2,66},{3,67},{4,68},{5,69},{6,70},{7,71},{8,72},{9,... | collective-permute-start | bytes 3145736 | tf_op jit(solution)/shard_map/ppermute | solution.py:253
  174.7 6.8 %copy-start.11 = (s32[24]{0:T(128)S(1)}, s32[24]{0:T(128)}, u32[]{:S(2)}) copy-start(s32[24]{0:T(128)} %dynamic-slice_bitcast_fusion.place) | copy-start | bytes 292
  174.7 67.0 %all-to-all-start = ((bf16[8,512,512]{2,1,0:T(8,128)(2,1)}), bf16[8,512,512]{2,1,0:T(8,128)(2,1)}, u32[]{:S(2)}, u32[]{:S(2)}) async-start(bf16[8,512,512]{2,1,0:T(8,128)(2,1)} %bitcast.3), calls=%async_computation | async-start | bytes 8388608 | tf_op jit(solution)/shard_map/all_to_all | solution.py:300
  206.2 2.7 collective-permute-start.10
  209.4 24.5 %collective-permute-start.11 = (bf16[128,1024]{1,0:T(8,128)(2,1)S(1)}, bf16[128,1024]{1,0:T(8,128)(2,1)S(1)}, u32[]{:S(2)}, u32[]{:S(2)}) collective-permute-start(bf16[128,1024]{1,0:T(8,128)(2,1)S(1)} %get-tuple-element.38), channel_id=1, source_target_pairs={{0,12},{1,13},{2,14},{3,15},{4,0},{5,1},{6,2},{7,3},{8,4},{9,5},{1... | collective-permute-start | bytes 786440 | tf_op jit(solution)/shard_map/ppermute | solution.py:253
  212.2 24.7 %collective-permute-start.13 = (bf16[128,1024]{1,0:T(8,128)(2,1)S(1)}, bf16[128,1024]{1,0:T(8,128)(2,1)S(1)}, u32[]{:S(2)}, u32[]{:S(2)}) collective-permute-start(bf16[128,1024]{1,0:T(8,128)(2,1)S(1)} %get-tuple-element.39), channel_id=1, source_target_pairs={{0,8},{1,9},{2,10},{3,11},{4,12},{5,13},{6,14},{7,15},{8,0},{9,1},... | collective-permute-start | bytes 786440 | tf_op jit(solution)/shard_map/ppermute | solution.py:253
  213.0 27.6 %collective-permute-start.12 = (bf16[128,1024]{1,0:T(8,128)(2,1)S(1)}, bf16[128,1024]{1,0:T(8,128)(2,1)S(1)}, u32[]{:S(2)}, u32[]{:S(2)}) collective-permute-start(bf16[128,1024]{1,0:T(8,128)(2,1)S(1)} %get-tuple-element.40), channel_id=1, source_target_pairs={{0,4},{1,5},{2,6},{3,7},{4,8},{5,9},{6,10},{7,11},{8,12},{9,13},{1... | collective-permute-start | bytes 786440 | tf_op jit(solution)/shard_map/ppermute | solution.py:253
  240.8 8.6 %collective-permute-start.14 = (bf16[64,1024]{1,0:T(8,128)(2,1)S(1)}, bf16[64,1024]{1,0:T(8,128)(2,1)S(1)}, u32[]{:S(2)}, u32[]{:S(2)}) collective-permute-start(bf16[64,1024]{1,0:T(8,128)(2,1)S(1)} %slice.49), channel_id=1, source_target_pairs={{0,2},{1,3},{2,0},{3,1},{4,6},{5,7},{6,4},{7,5},{8,10},{9,11},{10,... | collective-permute-start | bytes 393224 | tf_op jit(solution)/shard_map/ppermute | solution.py:253
  244.8 18.8 %collective-permute-start.15 = (bf16[512,512]{1,0:T(8,128)(2,1)S(1)}, bf16[512,512]{1,0:T(8,128)(2,1)S(1)}, u32[]{:S(2)}, u32[]{:S(2)}) collective-permute-start(bf16[512,512]{1,0:T(8,128)(2,1)S(1)} %reduce_sum.12), channel_id=1, source_target_pairs={{0,0},{1,1},{2,2},{3,3},{4,4},{5,5},{6,6},{7,7},{8,70},{9,71},{10,... | collective-permute-start | bytes 1572872 | tf_op jit(solution)/shard_map/ppermute | solution.py:253
  (10 other events, 24.3 us)
Sparse Core Ops, SparseCore 0:
  10.3 43.3 all-gather.2
  55.4 75.3 all-gather.4

commit v3 on v2

--- a/solution.py
+++ b/solution.py
@@ -11,15 +11,16 @@
 
 HD=128; BLK=128; KB=4; CB=8
 SCALE=1.0/math.sqrt(HD); EXPSCALE=SCALE*math.log2(math.e)
+SHORT = pl.CostEstimate(flops=1 << 20, bytes_accessed=1 << 16, transcendentals=0)
 HALF, CHUNKS, CORE, SLOTS, KEPT = 0, 2, 10, 12, 16
 STEPS = (0, 3, 1, 2)
 NT=(((1,),(1,)),((),())); TN=(((0,),(0,)),((),())); NN=(((1,),(0,)),((),()))
 def dg(a,b,dims): return lax.dot_general(a,b,dims,preferred_element_type=jnp.float32)
 
-def fwd_kernel(heads,table,q_ref,k_ref,v_ref,c_ref,o_ref,p_ref):
+def fwd_kernel(heads,table,place,q_ref,k_ref,v_ref,c_ref,o_ref,p_ref):
     b=pl.program_id(0); width=heads*HD
     keyp=lax.broadcasted_iota(jnp.int32,(BLK,BLK),0); qp=lax.broadcasted_iota(jnp.int32,(BLK,BLK),1)
-    rows=[pl.ds(pl.multiple_of(table[b,j]*BLK,BLK),BLK) for j in range(KB)]
+    rows=[pl.ds(pl.multiple_of(place[KEPT+table[b,j]]*BLK,BLK),BLK) for j in range(KB)]
     for h in range(heads):
         cols=slice(h*HD,(h+1)*HD); vcols=slice(width+h*HD,width+(h+1)*HD)
         q=q_ref[:,cols]
@@ -35,24 +36,23 @@
         o_ref[:,cols]=o.astype(jnp.bfloat16)
         for j in range(KB+1): p_ref[0,h,j*BLK:(j+1)*BLK,:]=p[j]
 
-def fwd(table,q,k,v,cache):
+def fwd(table,place,q,k,v,cache):
     T,W=q.shape; heads=W//HD; nb=T//BLK
-    blk=pl.BlockSpec((BLK,W),lambda b,t:(b,0))
+    blk=pl.BlockSpec((BLK,W),lambda b,t,w:(b,0))
     return pl.pallas_call(functools.partial(fwd_kernel,heads),
-        grid_spec=pltpu.PrefetchScalarGridSpec(num_scalar_prefetch=1,grid=(nb,),
-            in_specs=[blk,blk,blk,pl.BlockSpec(cache.shape,lambda b,t:(0,0))],
-            out_specs=[blk,pl.BlockSpec((1,heads,(KB+1)*BLK,BLK),lambda b,t:(b,0,0,0))]),
+        grid_spec=pltpu.PrefetchScalarGridSpec(num_scalar_prefetch=2,grid=(nb,),
+            in_specs=[blk,blk,blk,pl.BlockSpec(cache.shape,lambda b,t,w:(0,0))],
+            out_specs=[blk,pl.BlockSpec((1,heads,(KB+1)*BLK,BLK),lambda b,t,w:(b,0,0,0))]),
         out_shape=[jax.ShapeDtypeStruct((T,W),jnp.bfloat16),jax.ShapeDtypeStruct((nb,heads,(KB+1)*BLK,BLK),jnp.bfloat16)],
         compiler_params=pltpu.CompilerParams(vmem_limit_bytes=40<<20),
-        cost_estimate=pl.CostEstimate(flops=int(2*2*T*W*(KB+1)*BLK),bytes_accessed=12<<20,transcendentals=T*heads*(KB+1)*BLK),
-        name="attn_fwd")(table,q,k,v,cache)
+        cost_estimate=SHORT,
+        name="attn_fwd")(table,place,q,k,v,cache)
 
 def bwd_kernel(heads,table,place,q_ref,k_ref,v_ref,c_ref,p_ref,ga_ref,gb_ref,dq_ref,dk_ref,dv_ref,keep_ref,away_ref,acc):
     b=pl.program_id(0); width=heads*HD
     @pl.when(b==0)
     def _(): acc[...]=jnp.zeros_like(acc)
-    rows=[pl.ds(pl.multiple_of(table[b,j]*BLK,BLK),BLK) for j in range(KB)]
-    kept=[pl.ds(pl.multiple_of(place[KEPT+table[b,j]]*BLK,BLK),BLK) for j in range(KB)]
+    rows=[pl.ds(pl.multiple_of(place[KEPT+table[b,j]]*BLK,BLK),BLK) for j in range(KB)]
     for h in range(heads):
         cols=slice(h*HD,(h+1)*HD); vcols=slice(width+h*HD,width+(h+1)*HD)
         q=q_ref[:,cols]
@@ -69,14 +69,14 @@
         dk_ref[:,cols]=(dg(ds[KB],q,NN)*SCALE).astype(jnp.bfloat16)
         dv_ref[:,cols]=dg(pb[KB],do,NN).astype(jnp.bfloat16)
         for j in range(KB):
-            acc[kept[j],cols]+=dg(ds[j],q,NN)
-            acc[kept[j],vcols]+=dg(pb[j],do,NN)
+            acc[rows[j],cols]+=dg(ds[j],q,NN)
+            acc[rows[j],vcols]+=dg(pb[j],do,NN)
     @pl.when(b==pl.num_programs(0)-1)
     def _():
         half=BLK//2
-        for ref,core in ((keep_ref,place[CORE]),(away_ref,place[CORE+1])):
+        for i,ref in enumerate((keep_ref,away_ref)):
             for c in range(CB):
-                at=pl.ds(pl.multiple_of(c*BLK+core*half,half),half)
+                at=slice(c*BLK+i*half,c*BLK+(i+1)*half)
                 ref[c*half:(c+1)*half,:width]=(acc[at,:width]*SCALE).astype(jnp.bfloat16)
                 ref[c*half:(c+1)*half,width:]=acc[at,width:].astype(jnp.bfloat16)
 
@@ -92,7 +92,7 @@
             scratch_shapes=[pltpu.VMEM(cache.shape,jnp.float32)]),
         out_shape=[jax.ShapeDtypeStruct((T,W),jnp.bfloat16)]*3+[jax.ShapeDtypeStruct((cache.shape[0]//2,cache.shape[1]),jnp.bfloat16)]*2,
         compiler_params=pltpu.CompilerParams(vmem_limit_bytes=40<<20),
-        cost_estimate=pl.CostEstimate(flops=int(4*2*T*W*(KB+1)*BLK),bytes_accessed=20<<20,transcendentals=0),
+        cost_estimate=SHORT,
         name="attn_bwd")(table,place,q,k,v,cache,p,ga,gb)
 
 
@@ -138,7 +138,7 @@
         ),
         out_shape=jax.ShapeDtypeStruct((2 * half, width), dtype),
         compiler_params=pltpu.CompilerParams(vmem_limit_bytes=VMEM_LIMIT),
-        cost_estimate=pl.CostEstimate(flops=16 * half * depth * width, bytes_accessed=14 << 20, transcendentals=0),
+        cost_estimate=SHORT,
         name="project",
     )(place, *columns, weight)
 
@@ -202,7 +202,7 @@
         ),
         out_shape=jax.ShapeDtypeStruct(shape, jnp.bfloat16),
         compiler_params=pltpu.CompilerParams(vmem_limit_bytes=VMEM_LIMIT),
-        cost_estimate=pl.CostEstimate(flops=32 * half * size * width, bytes_accessed=12 << 20, transcendentals=0),
+        cost_estimate=SHORT,
         name="outer",
     )(place, *columns, own, other, *([] if added is None else [added]))
 
@@ -269,12 +269,20 @@
 
     rows = cache_keys.shape[0]
     mine = jnp.concatenate([cache_keys, cache_values], axis=1)
-    cache = lax.all_gather(mine, "col", axis=0, tiled=True)
+    pair = jnp.concatenate([mine, send(mine, shifted(xl=1))], axis=0)
 
     upper, lower = grad_out[:half], grad_out[half:]
     before_upper, after_lower = send(upper, shifted(y=1)), send(lower, shifted(y=3))
     before_lower, after_upper = send(lower, shifted(y=1)), send(upper, shifted(y=3))
-    swapped, before_upper, after_lower = lax.optimization_barrier((send(proj_weight, swap), before_upper, after_lower))
+    swapped, before_upper, after_lower, pair = lax.optimization_barrier(
+        (send(proj_weight, swap), before_upper, after_lower, pair)
+    )
+    near = jnp.concatenate([pair] + [send(pair, shifted(z=4 - STEPS[i])) for i in range(1, 4)], axis=0)
+    near, before_lower, after_upper = lax.optimization_barrier((near, before_lower, after_upper))
+    far = send(near, shifted(core=1))
+    cache = jnp.stack(
+        [near.reshape(CB, rows, 2 * width), far.reshape(CB, rows, 2 * width)], axis=1
+    ).reshape(2 * CB * rows, 2 * width)
     weight = lax.all_gather(swapped, "col", axis=0, tiled=True)
     columns = (
         upper,
@@ -287,13 +295,14 @@
         send(after_lower, shifted(y=3)),
     )
 
-    attn_out, probs = fwd(block_table, queries, keys, values, cache)
+    attn_out, probs = fwd(block_table, place, queries, keys, values, cache)
     attn_other = send(attn_out, shifted(xh=1))
 
+    other_part, weight = lax.optimization_barrier((project(1, place, columns, weight, bf16), weight))
+    own_part = project(0, place, columns, weight, jnp.float32)
+    attn_other, own_part = lax.optimization_barrier((attn_other, own_part))
     theirs = outer(place, columns, attn_out, attn_other)
-    theirs, other_part = lax.optimization_barrier((theirs, project(1, place, columns, weight, bf16)))
     from_other = send(other_part, shifted(xh=1))
-    own_part = project(0, place, columns, weight, jnp.float32)
     pieces = outer(place, columns, attn_out, attn_other, send(theirs, shifted(core=1)))
     pieces, from_other, own_part = lax.optimization_barrier((pieces, from_other, own_part))
     groups = [[2 * i + c for i in range(8)] for c in range(2)]

time: 272 us -> 255 us (0.938)
  waiting for transfers between devices: 117 us -> 99.1 us
    ppermute x16 -> x21, waiting for transfers between devices: 111 us -> 97.2 us  [send(): return lax.ppermute(array, AXES, pairs)]
    all_gather x1 -> x0, waiting for transfers between devices: 5.83 us -> none  [per_device(): cache = lax.all_gather(mine, 'col', axis=0, tiled=True)]
    ppermute x16 -> x21, starting transfers between devices: 30.9 us -> 34.1 us  [send(): return lax.ppermute(array, AXES, pairs)]
    unnamed x32 -> x45, local copies, waits for them, and re-layouts: 12.1 us -> 12.2 us
  transfers between devices with their start and end apart: 19 -> 23, of which waited for: 12 -> 16; matrix products, arithmetic and copies ran while one was open for 3% -> 3% of each run, Pallas kernels for 26% -> 27%
where the time goes in v3:
time: 255 us; the launch traced here: 254 us
  waiting for transfers between devices  99.1 us (39%)
  Pallas kernels  80.2 us (31%)
  starting transfers between devices  39.6 us (16%)
  local copies, waits for them, and re-layouts  15.4 us (6%)
  between operations  14.3 us (6%)
  other arithmetic  5.64 us (2%)
    ppermute x21, waiting for transfers between devices, send(): return lax.ppermute(array, AXES, pairs)  97.2 us
    ppermute x21, starting transfers between devices, send(): return lax.ppermute(array, AXES, pairs)  34.1 us
    pallas_call x2, Pallas kernels, outer(): pl.pallas_call(outer_kernel, grid_spec=pltpu.PrefetchScalarGridSpec(num_s...  23.6 us
    pallas_call x2, Pallas kernels, project(): pl.pallas_call(functools.partial(project_kernel, other), grid_spec=pltpu....  20.9 us
    pallas_call x1, Pallas kernels, bwd(): pl.pallas_call(functools.partial(bwd_kernel, heads), grid_spec=pltpu.Pref...  19.4 us
    pallas_call x1, Pallas kernels, fwd(): pl.pallas_call(functools.partial(fwd_kernel, heads), grid_spec=pltpu.Pref...  16.4 us
    unnamed x45, local copies, waits for them, and re-layouts  12.2 us
    all_to_all x1, starting transfers between devices, per_device(): lax.all_to_all(pieces, 'col', split_axis=0, concat_axis=0, axis_index_gro...  5.38 us
  transfers between devices with their start and end apart: 23, of which 16 were waited for; matrix products, arithmetic and copies ran while one was open for 3% of the time, Pallas kernels for 27%

profile of v3, /device:TPU:6, one launch (start us, length us, event | category | flops | bytes accessed | tf_op | source)
XLA Modules:
  0.0 254.2 jit_solution(14111938630531345590)
XLA Ops:
  9.0 3.1 %collective-permute-start.2 = (bf16[512,1024]{1,0:T(8,128)(2,1)S(1)}, bf16[512,1024]{1,0:T(8,128)(2,1)}, u32[]{:S(2)}, u32[]{:S(2)}) collective-permute-start(bf16[512,1024]{1,0:T(8,128)(2,1)S(1)} %get-tuple-element.48.refs_1_), channel_id=1, source_target_pairs={{0,48},{1,49},{2,50},{3,51},{4,52},{5,53},{6,54},{7,55},{8,56},{9,... | collective-permute-start | bytes 3145736 | tf_op jit(solution)/shard_map/ppermute | solution.py:253
  12.1 5.9 %collective-permute-start = (bf16[512,512]{1,0:T(8,128)(2,1)}, bf16[512,512]{1,0:T(8,128)(2,1)S(1)}, u32[]{:S(2)}, u32[]{:S(2)}) collective-permute-start(bf16[512,512]{1,0:T(8,128)(2,1)} %param.10), channel_id=1, source_target_pairs={{0,0},{1,1},{2,2},{3,3},{4,4},{5,5},{6,6},{7,7},{8,70},{9,71},{10,... | collective-permute-start | bytes 1572872 | tf_op jit(solution)/shard_map/ppermute | solution.py:253
  18.9 4.1 %collective-permute-done.3 = bf16[64,1024]{1,0:T(8,128)(2,1)S(1)} collective-permute-done((bf16[64,1024]{1,0:T(8,128)(2,1)S(1)}, bf16[64,1024]{1,0:T(8,128)(2,1)S(1)}, u32[]{:S(2)}, u32[]{:S(2)}) %collective-permute-start.3) | collective-permute-done | bytes 131104 | tf_op jit(solution)/shard_map/ppermute | solution.py:253
  23.0 7.8 %collective-permute-done = bf16[512,512]{1,0:T(8,128)(2,1)S(1)} collective-permute-done((bf16[512,512]{1,0:T(8,128)(2,1)}, bf16[512,512]{1,0:T(8,128)(2,1)S(1)}, u32[]{:S(2)}, u32[]{:S(2)}) %collective-permute-start) | collective-permute-done | bytes 524320 | tf_op jit(solution)/shard_map/ppermute | solution.py:253
  30.9 3.6 %collective-permute-done.2.refs_5_ = bf16[512,1024]{1,0:T(8,128)(2,1)} collective-permute-done((bf16[512,1024]{1,0:T(8,128)(2,1)S(1)}, bf16[512,1024]{1,0:T(8,128)(2,1)}, u32[]{:S(2)}, u32[]{:S(2)}) %collective-permute-start.2) | collective-permute-done | bytes 1048608 | tf_op jit(solution)/shard_map/ppermute | solution.py:253
  34.5 3.5 %collective-permute-done.1.refs_2_ = bf16[512,1024]{1,0:T(8,128)(2,1)} collective-permute-done((bf16[512,1024]{1,0:T(8,128)(2,1)S(1)}, bf16[512,1024]{1,0:T(8,128)(2,1)}, u32[]{:S(2)}, u32[]{:S(2)}) %collective-permute-start.1) | collective-permute-done | bytes 1048608 | tf_op jit(solution)/shard_map/ppermute | solution.py:253
  38.1 3.2 %collective-permute-start.8 = (bf16[512,1024]{1,0:T(8,128)(2,1)S(1)}, bf16[512,1024]{1,0:T(8,128)(2,1)S(1)}, u32[]{:S(2)}, u32[]{:S(2)}) collective-permute-start(bf16[512,1024]{1,0:T(8,128)(2,1)S(1)} %get-tuple-element.49.refs_0_), channel_id=1, source_target_pairs={{0,48},{1,49},{2,50},{3,51},{4,52},{5,53},{6,54},{7,55},{8,56},{9,... | collective-permute-start | bytes 3145736 | tf_op jit(solution)/shard_map/ppermute | solution.py:253
  41.3 3.9 %collective-permute-start.6 = (bf16[128,1024]{1,0:T(8,128)(2,1)S(1)}, bf16[128,1024]{1,0:T(8,128)(2,1)S(1)}, u32[]{:S(2)}, u32[]{:S(2)}) collective-permute-start(bf16[128,1024]{1,0:T(8,128)(2,1)S(1)} %pad_maximum_fusion.2), channel_id=1, source_target_pairs={{0,8},{1,9},{2,10},{3,11},{4,12},{5,13},{6,14},{7,15},{8,0},{9,1},... | collective-permute-start | bytes 786440 | tf_op jit(solution)/shard_map/ppermute | solution.py:253
  47.2 9.6 %collective-permute-done.6 = bf16[128,1024]{1,0:T(8,128)(2,1)S(1)} collective-permute-done((bf16[128,1024]{1,0:T(8,128)(2,1)S(1)}, bf16[128,1024]{1,0:T(8,128)(2,1)S(1)}, u32[]{:S(2)}, u32[]{:S(2)}) %collective-permute-start.6) | collective-permute-done | bytes 262176 | tf_op jit(solution)/shard_map/ppermute | solution.py:253
  56.9 9.3 %collective-permute-done.5 = bf16[128,1024]{1,0:T(8,128)(2,1)S(1)} collective-permute-done((bf16[128,1024]{1,0:T(8,128)(2,1)S(1)}, bf16[128,1024]{1,0:T(8,128)(2,1)S(1)}, u32[]{:S(2)}, u32[]{:S(2)}) %collective-permute-start.5) | collective-permute-done | bytes 262176 | tf_op jit(solution)/shard_map/ppermute | solution.py:253
  69.1 3.2 %collective-permute-start.11 = (bf16[512,1024]{1,0:T(8,128)(2,1)}, bf16[512,1024]{1,0:T(8,128)(2,1)}, u32[]{:S(2)}, u32[]{:S(2)}) collective-permute-start(bf16[512,1024]{1,0:T(8,128)(2,1)} %collective-permute-done.2.refs_5_), channel_id=1, source_target_pairs={{0,48},{1,49},{2,50},{3,51},{4,52},{5,53},{6,54},{7,55},{8,56},{9,... | collective-permute-start | bytes 3145736 | tf_op jit(solution)/shard_map/ppermute | solution.py:253
  74.9 16.4 %attn_fwd.1 = (bf16[1024,512]{1,0:T(8,128)(2,1)}, bf16[8,4,640,128]{3,2,1,0:T(8,128)(2,1)S(1)}) custom-call(s32[8,4]{1,0:T(8,128)S(1)} %copy.18.table, s32[24]{0:T(128)S(1)} %dynamic-slice_bitcast_fusion.place, bf16[1024,512]{1,0:T(8,128)(2,1)S(1)} %copy-done.2, bf16[1024,512]{1,0:T(8,128)(2,1)S(1)} %copy-done.3, bf16[1024,512]{1,0:T(8,128)(2,1)S(1)} %copy-done.5, ...), custom_call_target="tpu_custom_call" | custom-call | flops 1048576 | bytes 65536 | tf_op jit(solution)/shard_map/attn_fwd/pallas_call | solution.py:42
  97.1 10.3 %project.2 = bf16[1024,512]{1,0:T(8,128)(2,1)} custom-call(s32[24]{0:T(128)} %copy-done.9, bf16[512,1024]{1,0:T(8,128)(2,1)} %copy-done.12, bf16[512,1024]{1,0:T(8,128)(2,1)} %copy-done.11, bf16[512,1024]{1,0:T(8,128)(2,1)} %collective-permute-done.1.refs_2_, bf16[512,1024]{1,0:T(8,128)(2,1)} %copy-done.13, bf16[512,1024]{1,0:T(8,128)(2,1)} %copy-done.14, ...), custom_call_target="tpu_custom_call" | custom-call | flops 1048576 | bytes 65536 | tf_op jit(solution)/shard_map/project/pallas_call | solution.py:131
  107.5 10.5 %project.3.ga_ref = f32[1024,512]{1,0:T(8,128)} custom-call(s32[24]{0:T(128)} %copy-done.9, bf16[512,1024]{1,0:T(8,128)(2,1)} %copy-done.12, bf16[512,1024]{1,0:T(8,128)(2,1)} %copy-done.11, bf16[512,1024]{1,0:T(8,128)(2,1)} %collective-permute-done.1.refs_2_, bf16[512,1024]{1,0:T(8,128)(2,1)} %copy-done.13, bf16[512,1024]{1,0:T(8,128)(2,1)} %copy-done.14, ...), custom_call_target="tpu_custom_call" | custom-call | flops 1048576 | bytes 65536 | tf_op jit(solution)/shard_map/project/pallas_call | solution.py:131
  119.6 11.2 %outer.2 = bf16[2048,1024]{1,0:T(8,128)(2,1)} custom-call(s32[24]{0:T(128)} %copy-done.9, bf16[512,1024]{1,0:T(8,128)(2,1)} %copy-done.12, bf16[512,1024]{1,0:T(8,128)(2,1)} %copy-done.11, bf16[512,1024]{1,0:T(8,128)(2,1)} %collective-permute-done.1.refs_2_, bf16[512,1024]{1,0:T(8,128)(2,1)} %copy-done.13, bf16[512,1024]{1,0:T(8,128)(2,1)} %copy-done.14, ...), custom_call_target="tpu_custom_call" | custom-call | flops 1048576 | bytes 65536 | tf_op jit(solution)/shard_map/outer/pallas_call | solution.py:192
  132.2 6.1 %collective-permute-done.13.refs_10_ = bf16[2048,1024]{1,0:T(8,128)(2,1)} collective-permute-done((bf16[2048,1024]{1,0:T(8,128)(2,1)}, bf16[2048,1024]{1,0:T(8,128)(2,1)}, u32[]{:S(2)}, u32[]{:S(2)}) %collective-permute-start.13) | collective-permute-done | bytes 4194336 | tf_op jit(solution)/shard_map/ppermute | solution.py:253
  138.3 12.3 %outer.3 = bf16[4096,512]{1,0:T(8,128)(2,1)} custom-call(s32[24]{0:T(128)} %copy-done.9, bf16[512,1024]{1,0:T(8,128)(2,1)} %copy-done.12, bf16[512,1024]{1,0:T(8,128)(2,1)} %copy-done.11, bf16[512,1024]{1,0:T(8,128)(2,1)} %collective-permute-done.1.refs_2_, bf16[512,1024]{1,0:T(8,128)(2,1)} %copy-done.13, bf16[512,1024]{1,0:T(8,128)(2,1)} %copy-done.14, ...), custom_call_target="tpu_custom_call" | custom-call | flops 1048576 | bytes 65536 | tf_op jit(solution)/shard_map/outer/pallas_call | solution.py:192
  150.6 7.3 %collective-permute-done.14.gb_ref = bf16[1024,512]{1,0:T(8,128)(2,1)S(1)} collective-permute-done((bf16[1024,512]{1,0:T(8,128)(2,1)S(1)}, bf16[1024,512]{1,0:T(8,128)(2,1)S(1)}, u32[]{:S(2)}, u32[]{:S(2)}) %collective-permute-start.14) | collective-permute-done | bytes 1048608 | tf_op jit(solution)/shard_map/ppermute | solution.py:253
  158.8 5.4 %all-to-all-start = ((bf16[8,512,512]{2,1,0:T(8,128)(2,1)}), bf16[8,512,512]{2,1,0:T(8,128)(2,1)}, u32[]{:S(2)}, u32[]{:S(2)}) async-start(bf16[8,512,512]{2,1,0:T(8,128)(2,1)} %bitcast.12), calls=%async_computation | async-start | bytes 8388608 | tf_op jit(solution)/shard_map/all_to_all | solution.py:309
  169.5 19.4 %attn_bwd.1 = (bf16[1024,512]{1,0:T(8,128)(2,1)}, bf16[1024,512]{1,0:T(8,128)(2,1)}, bf16[1024,512]{1,0:T(8,128)(2,1)}, bf16[512,1024]{1,0:T(8,128)(2,1)S(1)}, bf16[512,1024]{1,0:T(8,128)(2,1)S(1)}) custom-call(s32[8,4]{1,0:T(8,128)S(1)} %copy.18.table, s32[24]{0:T(128)S(1)} %copy-done.10, bf16[1024,512]{1,0:T(8,128)(2,1)S(1)} %copy-done.2, ...), custom_call_target="tpu_custom_call" | custom-call | flops 1048576 | bytes 65536 | tf_op jit(solution)/shard_map/attn_bwd/pallas_call | solution.py:88
  196.5 20.3 %collective-permute-done.16 = bf16[128,1024]{1,0:T(8,128)(2,1)S(1)} collective-permute-done((bf16[128,1024]{1,0:T(8,128)(2,1)S(1)}, bf16[128,1024]{1,0:T(8,128)(2,1)S(1)}, u32[]{:S(2)}, u32[]{:S(2)}) %collective-permute-start.16) | collective-permute-done | bytes 262176 | tf_op jit(solution)/shard_map/ppermute | solution.py:253
  219.6 4.0 %collective-permute-done.17 = bf16[128,1024]{1,0:T(8,128)(2,1)S(1)} collective-permute-done((bf16[128,1024]{1,0:T(8,128)(2,1)S(1)}, bf16[128,1024]{1,0:T(8,128)(2,1)S(1)}, u32[]{:S(2)}, u32[]{:S(2)}) %collective-permute-start.17) | collective-permute-done | bytes 262176 | tf_op jit(solution)/shard_map/ppermute | solution.py:253
  227.7 3.6 %collective-permute-start.20 = (bf16[512,512]{1,0:T(8,128)(2,1)S(1)}, bf16[512,512]{1,0:T(8,128)(2,1)S(1)}, u32[]{:S(2)}, u32[]{:S(2)}) collective-permute-start(bf16[512,512]{1,0:T(8,128)(2,1)S(1)} %reduce_sum.12), channel_id=1, source_target_pairs={{0,0},{1,1},{2,2},{3,3},{4,4},{5,5},{6,6},{7,7},{8,70},{9,71},{10,... | collective-permute-start | bytes 1572872 | tf_op jit(solution)/shard_map/ppermute | solution.py:253
  232.1 14.4 %collective-permute-done.20 = bf16[512,512]{1,0:T(8,128)(2,1)S(1)} collective-permute-done((bf16[512,512]{1,0:T(8,128)(2,1)S(1)}, bf16[512,512]{1,0:T(8,128)(2,1)S(1)}, u32[]{:S(2)}, u32[]{:S(2)}) %collective-permute-start.20) | collective-permute-done | bytes 524320 | tf_op jit(solution)/shard_map/ppermute | solution.py:253
  (87 shorter events, 41.4 us)
Async XLA Ops:
  7.2 89.9 %all-gather.2.cloned.1.call-start = ((), (), s32[]{:S(2)}) async-start(), calls=%async_computation.1 | async-start | bytes 8912896 | tf_op jit(solution)/shard_map/all_gather | solution.py:286
  8.9 63.4 %copy-start.11 = (bf16[512,1024]{1,0:T(8,128)(2,1)}, bf16[512,1024]{1,0:T(8,128)(2,1)S(1)}, u32[]{:S(2)}) copy-start(bf16[512,1024]{1,0:T(8,128)(2,1)S(1)} %get-tuple-element.48.refs_1_) | copy-start | bytes 3145732
  9.0 25.5 %collective-permute-start.2 = (bf16[512,1024]{1,0:T(8,128)(2,1)S(1)}, bf16[512,1024]{1,0:T(8,128)(2,1)}, u32[]{:S(2)}, u32[]{:S(2)}) collective-permute-start(bf16[512,1024]{1,0:T(8,128)(2,1)S(1)} %get-tuple-element.48.refs_1_), channel_id=1, source_target_pairs={{0,48},{1,49},{2,50},{3,51},{4,52},{5,53},{6,54},{7,55},{8,56},{9,... | collective-permute-start | bytes 3145736 | tf_op jit(solution)/shard_map/ppermute | solution.py:253
  12.1 25.9 %collective-permute-start.1 = (bf16[512,1024]{1,0:T(8,128)(2,1)S(1)}, bf16[512,1024]{1,0:T(8,128)(2,1)}, u32[]{:S(2)}, u32[]{:S(2)}) collective-permute-start(bf16[512,1024]{1,0:T(8,128)(2,1)S(1)} %get-tuple-element.49.refs_0_), channel_id=1, source_target_pairs={{0,16},{1,17},{2,18},{3,19},{4,20},{5,21},{6,22},{7,23},{8,24},{9,... | collective-permute-start | bytes 3145736 | tf_op jit(solution)/shard_map/ppermute | solution.py:253
  12.1 18.8 %collective-permute-start = (bf16[512,512]{1,0:T(8,128)(2,1)}, bf16[512,512]{1,0:T(8,128)(2,1)S(1)}, u32[]{:S(2)}, u32[]{:S(2)}) collective-permute-start(bf16[512,512]{1,0:T(8,128)(2,1)} %param.10), channel_id=1, source_target_pairs={{0,0},{1,1},{2,2},{3,3},{4,4},{5,5},{6,6},{7,7},{8,70},{9,71},{10,... | collective-permute-start | bytes 1572872 | tf_op jit(solution)/shard_map/ppermute | solution.py:253
  18.0 5.0 %collective-permute-start.3 = (bf16[64,1024]{1,0:T(8,128)(2,1)S(1)}, bf16[64,1024]{1,0:T(8,128)(2,1)S(1)}, u32[]{:S(2)}, u32[]{:S(2)}) collective-permute-start(bf16[64,1024]{1,0:T(8,128)(2,1)S(1)} %constant_dynamic-update-slice_fusion), channel_id=1, source_target_pairs={{0,2},{1,3},{2,0},{3,1},{4,6},{5,7},{6,4},{7,5},{8,10},{9,11},{10,... | collective-permute-start | bytes 393224 | tf_op jit(solution)/shard_map/ppermute | solution.py:253
  38.0 28.2 %collective-permute-start.7 = (bf16[512,1024]{1,0:T(8,128)(2,1)S(1)}, bf16[512,1024]{1,0:T(8,128)(2,1)S(1)}, u32[]{:S(2)}, u32[]{:S(2)}) collective-permute-start(bf16[512,1024]{1,0:T(8,128)(2,1)S(1)} %get-tuple-element.48.refs_1_), channel_id=1, source_target_pairs={{0,16},{1,17},{2,18},{3,19},{4,20},{5,21},{6,22},{7,23},{8,24},{9,... | collective-permute-start | bytes 3145736 | tf_op jit(solution)/shard_map/ppermute | solution.py:253
  38.1 28.2 %collective-permute-start.8 = (bf16[512,1024]{1,0:T(8,128)(2,1)S(1)}, bf16[512,1024]{1,0:T(8,128)(2,1)S(1)}, u32[]{:S(2)}, u32[]{:S(2)}) collective-permute-start(bf16[512,1024]{1,0:T(8,128)(2,1)S(1)} %get-tuple-element.49.refs_0_), channel_id=1, source_target_pairs={{0,48},{1,49},{2,50},{3,51},{4,52},{5,53},{6,54},{7,55},{8,56},{9,... | collective-permute-start | bytes 3145736 | tf_op jit(solution)/shard_map/ppermute | solution.py:253
  41.3 15.5 %collective-permute-start.6 = (bf16[128,1024]{1,0:T(8,128)(2,1)S(1)}, bf16[128,1024]{1,0:T(8,128)(2,1)S(1)}, u32[]{:S(2)}, u32[]{:S(2)}) collective-permute-start(bf16[128,1024]{1,0:T(8,128)(2,1)S(1)} %pad_maximum_fusion.2), channel_id=1, source_target_pairs={{0,8},{1,9},{2,10},{3,11},{4,12},{5,13},{6,14},{7,15},{8,0},{9,1},... | collective-permute-start | bytes 786440 | tf_op jit(solution)/shard_map/ppermute | solution.py:253
  45.2 21.0 %collective-permute-start.5 = (bf16[128,1024]{1,0:T(8,128)(2,1)S(1)}, bf16[128,1024]{1,0:T(8,128)(2,1)S(1)}, u32[]{:S(2)}, u32[]{:S(2)}) collective-permute-start(bf16[128,1024]{1,0:T(8,128)(2,1)S(1)} %pad_maximum_fusion.2), channel_id=1, source_target_pairs={{0,12},{1,13},{2,14},{3,15},{4,0},{5,1},{6,2},{7,3},{8,4},{9,5},{1... | collective-permute-start | bytes 786440 | tf_op jit(solution)/shard_map/ppermute | solution.py:253
  45.9 20.3 %collective-permute-start.4 = (bf16[128,1024]{1,0:T(8,128)(2,1)S(1)}, bf16[128,1024]{1,0:T(8,128)(2,1)S(1)}, u32[]{:S(2)}, u32[]{:S(2)}) collective-permute-start(bf16[128,1024]{1,0:T(8,128)(2,1)S(1)} %pad_maximum_fusion.2), channel_id=1, source_target_pairs={{0,4},{1,5},{2,6},{3,7},{4,8},{5,9},{6,10},{7,11},{8,12},{9,13},{1... | collective-permute-start | bytes 786440 | tf_op jit(solution)/shard_map/ppermute | solution.py:253
  67.3 5.0 %collective-permute-start.9 = (bf16[512,1024]{1,0:T(8,128)(2,1)S(1)}, bf16[512,1024]{1,0:T(8,128)(2,1)}, u32[]{:S(2)}, u32[]{:S(2)}) collective-permute-start(bf16[512,1024]{1,0:T(8,128)(2,1)S(1)} %pad_maximum_fusion.1), channel_id=1, source_target_pairs={{0,1},{1,0},{2,3},{3,2},{4,5},{5,4},{6,7},{7,6},{8,9},{9,8},{10,11... | collective-permute-start | bytes 3145736 | tf_op jit(solution)/shard_map/ppermute | solution.py:253
  69.1 26.1 %collective-permute-start.10 = (bf16[512,1024]{1,0:T(8,128)(2,1)}, bf16[512,1024]{1,0:T(8,128)(2,1)}, u32[]{:S(2)}, u32[]{:S(2)}) collective-permute-start(bf16[512,1024]{1,0:T(8,128)(2,1)} %collective-permute-done.1.refs_2_), channel_id=1, source_target_pairs={{0,16},{1,17},{2,18},{3,19},{4,20},{5,21},{6,22},{7,23},{8,24},{9,... | collective-permute-start | bytes 3145736 | tf_op jit(solution)/shard_map/ppermute | solution.py:253
  69.1 26.1 %collective-permute-start.11 = (bf16[512,1024]{1,0:T(8,128)(2,1)}, bf16[512,1024]{1,0:T(8,128)(2,1)}, u32[]{:S(2)}, u32[]{:S(2)}) collective-permute-start(bf16[512,1024]{1,0:T(8,128)(2,1)} %collective-permute-done.2.refs_5_), channel_id=1, source_target_pairs={{0,48},{1,49},{2,50},{3,51},{4,52},{5,53},{6,54},{7,55},{8,56},{9,... | collective-permute-start | bytes 3145736 | tf_op jit(solution)/shard_map/ppermute | solution.py:253
  93.7 25.9 %collective-permute-start.12 = (bf16[1024,512]{1,0:T(8,128)(2,1)}, bf16[1024,512]{1,0:T(8,128)(2,1)}, u32[]{:S(2)}, u32[]{:S(2)}) collective-permute-start(bf16[1024,512]{1,0:T(8,128)(2,1)} %get-tuple-element.34.refs_8_), channel_id=1, source_target_pairs={{0,64},{1,65},{2,66},{3,67},{4,68},{5,69},{6,70},{7,71},{8,72},{9,... | collective-permute-start | bytes 3145736 | tf_op jit(solution)/shard_map/ppermute | solution.py:253
  130.8 7.5 %collective-permute-start.13 = (bf16[2048,1024]{1,0:T(8,128)(2,1)}, bf16[2048,1024]{1,0:T(8,128)(2,1)}, u32[]{:S(2)}, u32[]{:S(2)}) collective-permute-start(bf16[2048,1024]{1,0:T(8,128)(2,1)} %outer.2), channel_id=1, source_target_pairs={{0,1},{1,0},{2,3},{3,2},{4,5},{5,4},{6,7},{7,6},{8,9},{9,8},{10,11... | collective-permute-start | bytes 12582920 | tf_op jit(solution)/shard_map/ppermute | solution.py:253
  130.8 27.1 %collective-permute-start.14 = (bf16[1024,512]{1,0:T(8,128)(2,1)S(1)}, bf16[1024,512]{1,0:T(8,128)(2,1)S(1)}, u32[]{:S(2)}, u32[]{:S(2)}) collective-permute-start(bf16[1024,512]{1,0:T(8,128)(2,1)S(1)} %copy-done.16), channel_id=1, source_target_pairs={{0,64},{1,65},{2,66},{3,67},{4,68},{5,69},{6,70},{7,71},{8,72},{9,... | collective-permute-start | bytes 3145736 | tf_op jit(solution)/shard_map/ppermute | solution.py:253
  158.8 65.8 %all-to-all-start = ((bf16[8,512,512]{2,1,0:T(8,128)(2,1)}), bf16[8,512,512]{2,1,0:T(8,128)(2,1)}, u32[]{:S(2)}, u32[]{:S(2)}) async-start(bf16[8,512,512]{2,1,0:T(8,128)(2,1)} %bitcast.12), calls=%async_computation | async-start | bytes 8388608 | tf_op jit(solution)/shard_map/all_to_all | solution.py:309
  188.9 2.7 %collective-permute-start.15 = (bf16[512,1024]{1,0:T(8,128)(2,1)S(1)}, bf16[512,1024]{1,0:T(8,128)(2,1)S(1)}, u32[]{:S(2)}, u32[]{:S(2)}) collective-permute-start(bf16[512,1024]{1,0:T(8,128)(2,1)S(1)} %get-tuple-element.46), channel_id=1, source_target_pairs={{0,1},{1,0},{2,3},{3,2},{4,5},{5,4},{6,7},{7,6},{8,9},{9,8},{10,11... | collective-permute-start | bytes 3145736 | tf_op jit(solution)/shard_map/ppermute | solution.py:253
  192.0 24.8 %collective-permute-start.16 = (bf16[128,1024]{1,0:T(8,128)(2,1)S(1)}, bf16[128,1024]{1,0:T(8,128)(2,1)S(1)}, u32[]{:S(2)}, u32[]{:S(2)}) collective-permute-start(bf16[128,1024]{1,0:T(8,128)(2,1)S(1)} %get-tuple-element.50), channel_id=1, source_target_pairs={{0,12},{1,13},{2,14},{3,15},{4,0},{5,1},{6,2},{7,3},{8,4},{9,5},{1... | collective-permute-start | bytes 786440 | tf_op jit(solution)/shard_map/ppermute | solution.py:253
  194.8 24.8 %collective-permute-start.18 = (bf16[128,1024]{1,0:T(8,128)(2,1)S(1)}, bf16[128,1024]{1,0:T(8,128)(2,1)S(1)}, u32[]{:S(2)}, u32[]{:S(2)}) collective-permute-start(bf16[128,1024]{1,0:T(8,128)(2,1)S(1)} %get-tuple-element.51), channel_id=1, source_target_pairs={{0,8},{1,9},{2,10},{3,11},{4,12},{5,13},{6,14},{7,15},{8,0},{9,1},... | collective-permute-start | bytes 786440 | tf_op jit(solution)/shard_map/ppermute | solution.py:253
  195.6 27.9 %collective-permute-start.17 = (bf16[128,1024]{1,0:T(8,128)(2,1)S(1)}, bf16[128,1024]{1,0:T(8,128)(2,1)S(1)}, u32[]{:S(2)}, u32[]{:S(2)}) collective-permute-start(bf16[128,1024]{1,0:T(8,128)(2,1)S(1)} %get-tuple-element.52), channel_id=1, source_target_pairs={{0,4},{1,5},{2,6},{3,7},{4,8},{5,9},{6,10},{7,11},{8,12},{9,13},{1... | collective-permute-start | bytes 786440 | tf_op jit(solution)/shard_map/ppermute | solution.py:253
  223.7 7.6 %collective-permute-start.19 = (bf16[64,1024]{1,0:T(8,128)(2,1)S(1)}, bf16[64,1024]{1,0:T(8,128)(2,1)S(1)}, u32[]{:S(2)}, u32[]{:S(2)}) collective-permute-start(bf16[64,1024]{1,0:T(8,128)(2,1)S(1)} %slice.49), channel_id=1, source_target_pairs={{0,2},{1,3},{2,0},{3,1},{4,6},{5,7},{6,4},{7,5},{8,10},{9,11},{10,... | collective-permute-start | bytes 393224 | tf_op jit(solution)/shard_map/ppermute | solution.py:253
  227.7 18.8 %collective-permute-start.20 = (bf16[512,512]{1,0:T(8,128)(2,1)S(1)}, bf16[512,512]{1,0:T(8,128)(2,1)S(1)}, u32[]{:S(2)}, u32[]{:S(2)}) collective-permute-start(bf16[512,512]{1,0:T(8,128)(2,1)S(1)} %reduce_sum.12), channel_id=1, source_target_pairs={{0,0},{1,1},{2,2},{3,3},{4,4},{5,5},{6,6},{7,7},{8,70},{9,71},{10,... | collective-permute-start | bytes 1572872 | tf_op jit(solution)/shard_map/ppermute | solution.py:253
  (20 other events, 198.2 us)
Sparse Core Ops, SparseCore 0:
  38.2 58.9 all-gather.1

commit v4 on v3

--- a/solution.py
+++ b/solution.py
@@ -48,7 +48,7 @@
         cost_estimate=SHORT,
         name="attn_fwd")(table,place,q,k,v,cache)
 
-def bwd_kernel(heads,table,place,q_ref,k_ref,v_ref,c_ref,p_ref,ga_ref,gb_ref,dq_ref,dk_ref,dv_ref,keep_ref,away_ref,acc):
+def bwd_kernel(heads,table,place,q_ref,k_ref,v_ref,c_ref,p_ref,ga_ref,gu_ref,gl_ref,dq_ref,dk_ref,dv_ref,keep_ref,away_ref,acc):
     b=pl.program_id(0); width=heads*HD
     @pl.when(b==0)
     def _(): acc[...]=jnp.zeros_like(acc)
@@ -56,7 +56,8 @@
     for h in range(heads):
         cols=slice(h*HD,(h+1)*HD); vcols=slice(width+h*HD,width+(h+1)*HD)
         q=q_ref[:,cols]
-        do=(ga_ref[:,cols]+gb_ref[:,cols].astype(jnp.float32)).astype(jnp.bfloat16)
+        gb=jnp.where(b<pl.num_programs(0)//2,gu_ref[:,cols].astype(jnp.float32),gl_ref[:,cols].astype(jnp.float32))
+        do=(ga_ref[:,cols]+gb).astype(jnp.bfloat16)
         kk=[c_ref[r,cols] for r in rows]+[k_ref[:,cols]]
         vv=[c_ref[r,vcols] for r in rows]+[v_ref[:,cols]]
         pb=[p_ref[0,h,j*BLK:(j+1)*BLK,:] for j in range(KB+1)]
@@ -80,20 +81,22 @@
                 ref[c*half:(c+1)*half,:width]=(acc[at,:width]*SCALE).astype(jnp.bfloat16)
                 ref[c*half:(c+1)*half,width:]=acc[at,width:].astype(jnp.bfloat16)
 
-def bwd(table,place,q,k,v,cache,p,ga,gb):
+def bwd(table,place,q,k,v,cache,p,ga,gu,gl):
     T,W=q.shape; heads=W//HD; nb=T//BLK
     blk=pl.BlockSpec((BLK,W),lambda b,t,w:(b,0))
+    upper=pl.BlockSpec((BLK,W),lambda b,t,w:(jnp.minimum(b,nb//2-1),0))
+    lower=pl.BlockSpec((BLK,W),lambda b,t,w:(jnp.maximum(b-nb//2,0),0))
     full=pl.BlockSpec(cache.shape,lambda b,t,w:(0,0))
     part=pl.BlockSpec((cache.shape[0]//2,cache.shape[1]),lambda b,t,w:(0,0))
     return pl.pallas_call(functools.partial(bwd_kernel,heads),
         grid_spec=pltpu.PrefetchScalarGridSpec(num_scalar_prefetch=2,grid=(nb,),
-            in_specs=[blk,blk,blk,full,pl.BlockSpec((1,heads,(KB+1)*BLK,BLK),lambda b,t,w:(b,0,0,0)),blk,blk],
+            in_specs=[blk,blk,blk,full,pl.BlockSpec((1,heads,(KB+1)*BLK,BLK),lambda b,t,w:(b,0,0,0)),blk,upper,lower],
             out_specs=[blk,blk,blk,part,part],
             scratch_shapes=[pltpu.VMEM(cache.shape,jnp.float32)]),
         out_shape=[jax.ShapeDtypeStruct((T,W),jnp.bfloat16)]*3+[jax.ShapeDtypeStruct((cache.shape[0]//2,cache.shape[1]),jnp.bfloat16)]*2,
         compiler_params=pltpu.CompilerParams(vmem_limit_bytes=40<<20),
         cost_estimate=SHORT,
-        name="attn_bwd")(table,place,q,k,v,cache,p,ga,gb)
+        name="attn_bwd")(table,place,q,k,v,cache,p,ga,gu,gl)
 
 
 VMEM_LIMIT = 56 << 20
@@ -274,10 +277,10 @@
     upper, lower = grad_out[:half], grad_out[half:]
     before_upper, after_lower = send(upper, shifted(y=1)), send(lower, shifted(y=3))
     before_lower, after_upper = send(lower, shifted(y=1)), send(upper, shifted(y=3))
-    swapped, before_upper, after_lower, pair = lax.optimization_barrier(
-        (send(proj_weight, swap), before_upper, after_lower, pair)
-    )
-    near = jnp.concatenate([pair] + [send(pair, shifted(z=4 - STEPS[i])) for i in range(1, 4)], axis=0)
+    swapped, before_upper, after_lower, pair, across = lax.optimization_barrier(
+        (send(proj_weight, swap), before_upper, after_lower, pair, send(pair, shifted(z=2)))
+    )
+    near = jnp.concatenate([pair] + [send(pair, shifted(z=4 - STEPS[i])) for i in range(1, 3)] + [across], axis=0)
     near, before_lower, after_upper = lax.optimization_barrier((near, before_lower, after_upper))
     far = send(near, shifted(core=1))
     cache = jnp.stack(
@@ -301,17 +304,18 @@
     other_part, weight = lax.optimization_barrier((project(1, place, columns, weight, bf16), weight))
     own_part = project(0, place, columns, weight, jnp.float32)
     attn_other, own_part = lax.optimization_barrier((attn_other, own_part))
+    from_upper, from_lower = send(other_part[:half], shifted(xh=1)), send(other_part[half:], shifted(xh=1))
     theirs = outer(place, columns, attn_out, attn_other)
-    from_other = send(other_part, shifted(xh=1))
+    theirs, from_upper = lax.optimization_barrier((theirs, from_upper))
     pieces = outer(place, columns, attn_out, attn_other, send(theirs, shifted(core=1)))
-    pieces, from_other, own_part = lax.optimization_barrier((pieces, from_other, own_part))
+    pieces, from_lower, own_part = lax.optimization_barrier((pieces, from_lower, own_part))
     groups = [[2 * i + c for i in range(8)] for c in range(2)]
     pieces = lax.all_to_all(pieces, "col", split_axis=0, concat_axis=0, axis_index_groups=groups, tiled=True)
     total = jnp.sum(f32(pieces.reshape(8, -1, width)), axis=0).astype(bf16)
     grad_weight = send(total, swap)
 
     grad_q, grad_k, grad_v, keep, away = bwd(
-        block_table, place, queries, keys, values, cache, probs, own_part, from_other
+        block_table, place, queries, keys, values, cache, probs, own_part, from_upper, from_lower
     )
     parts = (f32(keep) + f32(send(away, shifted(core=1)))).astype(bf16).reshape(4, 2 * rows, 2 * width)
     parts = sum([f32(parts[0])] + [f32(send(parts[i], shifted(z=STEPS[i]))) for i in range(1, 4)]).astype(bf16)

time: 255 us -> 248 us (0.973)
  waiting for transfers between devices: 99.1 us -> 86.8 us
    ppermute x21 -> x22, waiting for transfers between devices: 97.2 us -> 86.8 us  [send(): return lax.ppermute(array, AXES, pairs)]
    ppermute x21 -> x22, starting transfers between devices: 34.1 us -> 35.1 us  [send(): return lax.ppermute(array, AXES, pairs)]
    unnamed x45 -> x49, local copies, waits for them, and re-layouts: 12.2 us -> 12.8 us
  transfers between devices with their start and end apart: 23 -> 24, of which waited for: 16 -> 13; matrix products, arithmetic and copies ran while one was open for 3% -> 4% of each run, Pallas kernels for 27% -> 32%
where the time goes in v4:
time: 248 us; the launch traced here: 247 us
  waiting for transfers between devices  86.8 us (35%)
  Pallas kernels  80.2 us (32%)
  starting transfers between devices  42.1 us (17%)
  local copies, waits for them, and re-layouts  17.2 us (7%)
  between operations  14.3 us (6%)
  other arithmetic  6.63 us (3%)
    ppermute x22, waiting for transfers between devices, send(): return lax.ppermute(array, AXES, pairs)  86.8 us
    ppermute x22, starting transfers between devices, send(): return lax.ppermute(array, AXES, pairs)  35.1 us
    pallas_call x2, Pallas kernels, outer(): pl.pallas_call(outer_kernel, grid_spec=pltpu.PrefetchScalarGridSpec(num_s...  23.6 us
    pallas_call x2, Pallas kernels, project(): pl.pallas_call(functools.partial(project_kernel, other), grid_spec=pltpu....  20.8 us
    pallas_call x1, Pallas kernels, bwd(): pl.pallas_call(functools.partial(bwd_kernel, heads), grid_spec=pltpu.Pref...  19.4 us
    pallas_call x1, Pallas kernels, fwd(): pl.pallas_call(functools.partial(fwd_kernel, heads), grid_spec=pltpu.Pref...  16.4 us
    unnamed x49, local copies, waits for them, and re-layouts  12.8 us
    all_to_all x1, starting transfers between devices, per_device(): lax.all_to_all(pieces, 'col', split_axis=0, concat_axis=0, axis_index_gro...  6.91 us
  transfers between devices with their start and end apart: 24, of which 13 were waited for; matrix products, arithmetic and copies ran while one was open for 4% of the time, Pallas kernels for 32%

profile of v4, /device:TPU:6, one launch (start us, length us, event | category | flops | bytes accessed | tf_op | source)
XLA Modules:
  0.0 247.3 jit_solution(5453741515487127269)
XLA Ops:
  9.0 3.1 %collective-permute-start.2 = (bf16[512,1024]{1,0:T(8,128)(2,1)S(1)}, bf16[512,1024]{1,0:T(8,128)(2,1)}, u32[]{:S(2)}, u32[]{:S(2)}) collective-permute-start(bf16[512,1024]{1,0:T(8,128)(2,1)S(1)} %get-tuple-element.54.refs_1_), channel_id=1, source_target_pairs={{0,48},{1,49},{2,50},{3,51},{4,52},{5,53},{6,54},{7,55},{8,56},{9,... | collective-permute-start | bytes 3145736 | tf_op jit(solution)/shard_map/ppermute | solution.py:256
  12.1 5.9 %collective-permute-start = (bf16[512,512]{1,0:T(8,128)(2,1)}, bf16[512,512]{1,0:T(8,128)(2,1)S(1)}, u32[]{:S(2)}, u32[]{:S(2)}) collective-permute-start(bf16[512,512]{1,0:T(8,128)(2,1)} %param.10), channel_id=1, source_target_pairs={{0,0},{1,1},{2,2},{3,3},{4,4},{5,5},{6,6},{7,7},{8,70},{9,71},{10,... | collective-permute-start | bytes 1572872 | tf_op jit(solution)/shard_map/ppermute | solution.py:256
  18.9 4.1 %collective-permute-done.3 = bf16[64,1024]{1,0:T(8,128)(2,1)S(1)} collective-permute-done((bf16[64,1024]{1,0:T(8,128)(2,1)S(1)}, bf16[64,1024]{1,0:T(8,128)(2,1)S(1)}, u32[]{:S(2)}, u32[]{:S(2)}) %collective-permute-start.3) | collective-permute-done | bytes 131104 | tf_op jit(solution)/shard_map/ppermute | solution.py:256
  23.1 13.3 %collective-permute-done.4 = bf16[128,1024]{1,0:T(8,128)(2,1)S(1)} collective-permute-done((bf16[128,1024]{1,0:T(8,128)(2,1)S(1)}, bf16[128,1024]{1,0:T(8,128)(2,1)S(1)}, u32[]{:S(2)}, u32[]{:S(2)}) %collective-permute-start.4) | collective-permute-done | bytes 262176 | tf_op jit(solution)/shard_map/ppermute | solution.py:256
  38.1 3.2 %collective-permute-start.8 = (bf16[512,1024]{1,0:T(8,128)(2,1)S(1)}, bf16[512,1024]{1,0:T(8,128)(2,1)S(1)}, u32[]{:S(2)}, u32[]{:S(2)}) collective-permute-start(bf16[512,1024]{1,0:T(8,128)(2,1)S(1)} %get-tuple-element.55.refs_0_), channel_id=1, source_target_pairs={{0,48},{1,49},{2,50},{3,51},{4,52},{5,53},{6,54},{7,55},{8,56},{9,... | collective-permute-start | bytes 3145736 | tf_op jit(solution)/shard_map/ppermute | solution.py:256
  41.3 4.0 %collective-permute-start.6 = (bf16[128,1024]{1,0:T(8,128)(2,1)S(1)}, bf16[128,1024]{1,0:T(8,128)(2,1)S(1)}, u32[]{:S(2)}, u32[]{:S(2)}) collective-permute-start(bf16[128,1024]{1,0:T(8,128)(2,1)S(1)} %pad_maximum_fusion.2), channel_id=1, source_target_pairs={{0,12},{1,13},{2,14},{3,15},{4,0},{5,1},{6,2},{7,3},{8,4},{9,5},{1... | collective-permute-start | bytes 786440 | tf_op jit(solution)/shard_map/ppermute | solution.py:256
  45.4 3.9 %collective-permute-done.6 = bf16[128,1024]{1,0:T(8,128)(2,1)S(1)} collective-permute-done((bf16[128,1024]{1,0:T(8,128)(2,1)S(1)}, bf16[128,1024]{1,0:T(8,128)(2,1)S(1)}, u32[]{:S(2)}, u32[]{:S(2)}) %collective-permute-start.6) | collective-permute-done | bytes 262176 | tf_op jit(solution)/shard_map/ppermute | solution.py:256
  49.3 4.7 %collective-permute-done.5 = bf16[128,1024]{1,0:T(8,128)(2,1)S(1)} collective-permute-done((bf16[128,1024]{1,0:T(8,128)(2,1)S(1)}, bf16[128,1024]{1,0:T(8,128)(2,1)S(1)}, u32[]{:S(2)}, u32[]{:S(2)}) %collective-permute-start.5) | collective-permute-done | bytes 262176 | tf_op jit(solution)/shard_map/ppermute | solution.py:256
  55.0 8.0 %collective-permute-done.7.refs_3_ = bf16[512,1024]{1,0:T(8,128)(2,1)S(1)} collective-permute-done((bf16[512,1024]{1,0:T(8,128)(2,1)S(1)}, bf16[512,1024]{1,0:T(8,128)(2,1)S(1)}, u32[]{:S(2)}, u32[]{:S(2)}) %collective-permute-start.7) | collective-permute-done | bytes 1048608 | tf_op jit(solution)/shard_map/ppermute | solution.py:256
  65.0 3.2 %collective-permute-start.11 = (bf16[512,1024]{1,0:T(8,128)(2,1)}, bf16[512,1024]{1,0:T(8,128)(2,1)}, u32[]{:S(2)}, u32[]{:S(2)}) collective-permute-start(bf16[512,1024]{1,0:T(8,128)(2,1)} %collective-permute-done.2.refs_5_), channel_id=1, source_target_pairs={{0,48},{1,49},{2,50},{3,51},{4,52},{5,53},{6,54},{7,55},{8,56},{9,... | collective-permute-start | bytes 3145736 | tf_op jit(solution)/shard_map/ppermute | solution.py:256
  71.6 16.4 %attn_fwd.1 = (bf16[1024,512]{1,0:T(8,128)(2,1)}, bf16[8,4,640,128]{3,2,1,0:T(8,128)(2,1)S(1)}) custom-call(s32[8,4]{1,0:T(8,128)S(1)} %copy.18.table, s32[24]{0:T(128)S(1)} %dynamic-slice_bitcast_fusion.place, bf16[1024,512]{1,0:T(8,128)(2,1)S(1)} %copy-done.2, bf16[1024,512]{1,0:T(8,128)(2,1)S(1)} %copy-done.3, bf16[1024,512]{1,0:T(8,128)(2,1)S(1)} %copy-done.5, ...), custom_call_target="tpu_custom_call" | custom-call | flops 1048576 | bytes 65536 | tf_op jit(solution)/shard_map/attn_fwd/pallas_call | solution.py:42
  91.8 10.3 %project.2 = bf16[1024,512]{1,0:T(8,128)(2,1)} custom-call(s32[24]{0:T(128)} %copy-done.11, bf16[512,1024]{1,0:T(8,128)(2,1)} %copy-done.14, bf16[512,1024]{1,0:T(8,128)(2,1)} %copy-done.13, bf16[512,1024]{1,0:T(8,128)(2,1)} %collective-permute-done.1.refs_2_, bf16[512,1024]{1,0:T(8,128)(2,1)} %copy-done.15, bf16[512,1024]{1,0:T(8,128)(2,1)} %copy-done.16, ...), custom_call_target="tpu_custom_call" | custom-call | flops 1048576 | bytes 65536 | tf_op jit(solution)/shard_map/project/pallas_call | solution.py:134
  105.6 10.5 %project.3.ga_ref = f32[1024,512]{1,0:T(8,128)} custom-call(s32[24]{0:T(128)} %copy-done.11, bf16[512,1024]{1,0:T(8,128)(2,1)} %copy-done.14, bf16[512,1024]{1,0:T(8,128)(2,1)} %copy-done.13, bf16[512,1024]{1,0:T(8,128)(2,1)} %collective-permute-done.1.refs_2_, bf16[512,1024]{1,0:T(8,128)(2,1)} %copy-done.15, bf16[512,1024]{1,0:T(8,128)(2,1)} %copy-done.16, ...), custom_call_target="tpu_custom_call" | custom-call | flops 1048576 | bytes 65536 | tf_op jit(solution)/shard_map/project/pallas_call | solution.py:134
  118.3 11.2 %outer.2 = bf16[2048,1024]{1,0:T(8,128)(2,1)} custom-call(s32[24]{0:T(128)} %copy-done.11, bf16[512,1024]{1,0:T(8,128)(2,1)} %copy-done.14, bf16[512,1024]{1,0:T(8,128)(2,1)} %copy-done.13, bf16[512,1024]{1,0:T(8,128)(2,1)} %collective-permute-done.1.refs_2_, bf16[512,1024]{1,0:T(8,128)(2,1)} %copy-done.15, bf16[512,1024]{1,0:T(8,128)(2,1)} %copy-done.16, ...), custom_call_target="tpu_custom_call" | custom-call | flops 1048576 | bytes 65536 | tf_op jit(solution)/shard_map/outer/pallas_call | solution.py:195
  131.1 6.0 %collective-permute-done.14.refs_10_ = bf16[2048,1024]{1,0:T(8,128)(2,1)} collective-permute-done((bf16[2048,1024]{1,0:T(8,128)(2,1)}, bf16[2048,1024]{1,0:T(8,128)(2,1)}, u32[]{:S(2)}, u32[]{:S(2)}) %collective-permute-start.14) | collective-permute-done | bytes 4194336 | tf_op jit(solution)/shard_map/ppermute | solution.py:256
  137.1 12.4 %outer.3 = bf16[4096,512]{1,0:T(8,128)(2,1)} custom-call(s32[24]{0:T(128)} %copy-done.11, bf16[512,1024]{1,0:T(8,128)(2,1)} %copy-done.14, bf16[512,1024]{1,0:T(8,128)(2,1)} %copy-done.13, bf16[512,1024]{1,0:T(8,128)(2,1)} %collective-permute-done.1.refs_2_, bf16[512,1024]{1,0:T(8,128)(2,1)} %copy-done.15, bf16[512,1024]{1,0:T(8,128)(2,1)} %copy-done.16, ...), custom_call_target="tpu_custom_call" | custom-call | flops 1048576 | bytes 65536 | tf_op jit(solution)/shard_map/outer/pallas_call | solution.py:195
  150.3 6.9 %all-to-all-start = ((bf16[8,512,512]{2,1,0:T(8,128)(2,1)}), bf16[8,512,512]{2,1,0:T(8,128)(2,1)}, u32[]{:S(2)}, u32[]{:S(2)}) async-start(bf16[8,512,512]{2,1,0:T(8,128)(2,1)} %bitcast.12), calls=%async_computation | async-start | bytes 8388608 | tf_op jit(solution)/shard_map/all_to_all | solution.py:313
  163.3 19.4 %attn_bwd.1 = (bf16[1024,512]{1,0:T(8,128)(2,1)}, bf16[1024,512]{1,0:T(8,128)(2,1)}, bf16[1024,512]{1,0:T(8,128)(2,1)}, bf16[512,1024]{1,0:T(8,128)(2,1)S(1)}, bf16[512,1024]{1,0:T(8,128)(2,1)S(1)}) custom-call(s32[8,4]{1,0:T(8,128)S(1)} %copy.18.table, s32[24]{0:T(128)S(1)} %copy-done.12, bf16[1024,512]{1,0:T(8,128)(2,1)S(1)} %copy-done.2, ...), custom_call_target="tpu_custom_call" | custom-call | flops 1048576 | bytes 65536 | tf_op jit(solution)/shard_map/attn_bwd/pallas_call | solution.py:91
  185.8 2.7 %collective-permute-start.17 = (bf16[128,1024]{1,0:T(8,128)(2,1)S(1)}, bf16[128,1024]{1,0:T(8,128)(2,1)S(1)}, u32[]{:S(2)}, u32[]{:S(2)}) collective-permute-start(bf16[128,1024]{1,0:T(8,128)(2,1)S(1)} %get-tuple-element.56), channel_id=1, source_target_pairs={{0,12},{1,13},{2,14},{3,15},{4,0},{5,1},{6,2},{7,3},{8,4},{9,5},{1... | collective-permute-start | bytes 786440 | tf_op jit(solution)/shard_map/ppermute | solution.py:256
  190.3 19.6 %collective-permute-done.17 = bf16[128,1024]{1,0:T(8,128)(2,1)S(1)} collective-permute-done((bf16[128,1024]{1,0:T(8,128)(2,1)S(1)}, bf16[128,1024]{1,0:T(8,128)(2,1)S(1)}, u32[]{:S(2)}, u32[]{:S(2)}) %collective-permute-start.17) | collective-permute-done | bytes 262176 | tf_op jit(solution)/shard_map/ppermute | solution.py:256
  212.5 4.2 %collective-permute-done.18 = bf16[128,1024]{1,0:T(8,128)(2,1)S(1)} collective-permute-done((bf16[128,1024]{1,0:T(8,128)(2,1)S(1)}, bf16[128,1024]{1,0:T(8,128)(2,1)S(1)}, u32[]{:S(2)}, u32[]{:S(2)}) %collective-permute-start.18) | collective-permute-done | bytes 262176 | tf_op jit(solution)/shard_map/ppermute | solution.py:256
  217.8 3.1 %reduce_sum.12 = bf16[512,512]{1,0:T(8,128)(2,1)S(1)} reduce(bf16[8,512,512]{2,1,0:T(8,128)(2,1)} %all-to-all-done, bf16[]{:T(256)} %constant.21.clone.1), dimensions={0}, to_apply=%region_0.1 | reduce | flops 1835008 | bytes 4718594 | tf_op jit(solution)/shard_map/reduce_sum | solution.py:314
  220.8 4.0 %collective-permute-start.21 = (bf16[512,512]{1,0:T(8,128)(2,1)S(1)}, bf16[512,512]{1,0:T(8,128)(2,1)S(1)}, u32[]{:S(2)}, u32[]{:S(2)}) collective-permute-start(bf16[512,512]{1,0:T(8,128)(2,1)S(1)} %reduce_sum.12), channel_id=1, source_target_pairs={{0,0},{1,1},{2,2},{3,3},{4,4},{5,5},{6,6},{7,7},{8,70},{9,71},{10,... | collective-permute-start | bytes 1572872 | tf_op jit(solution)/shard_map/ppermute | solution.py:256
  225.6 14.1 %collective-permute-done.21 = bf16[512,512]{1,0:T(8,128)(2,1)S(1)} collective-permute-done((bf16[512,512]{1,0:T(8,128)(2,1)S(1)}, bf16[512,512]{1,0:T(8,128)(2,1)S(1)}, u32[]{:S(2)}, u32[]{:S(2)}) %collective-permute-start.21) | collective-permute-done | bytes 524320 | tf_op jit(solution)/shard_map/ppermute | solution.py:256
  (94 shorter events, 38.7 us)
Async XLA Ops:
  7.2 84.6 %all-gather.2.cloned.1.call-start = ((), (), s32[]{:S(2)}) async-start(), calls=%async_computation.1 | async-start | bytes 8912896 | tf_op jit(solution)/shard_map/all_gather | solution.py:289
  9.0 27.5 %collective-permute-start.2 = (bf16[512,1024]{1,0:T(8,128)(2,1)S(1)}, bf16[512,1024]{1,0:T(8,128)(2,1)}, u32[]{:S(2)}, u32[]{:S(2)}) collective-permute-start(bf16[512,1024]{1,0:T(8,128)(2,1)S(1)} %get-tuple-element.54.refs_1_), channel_id=1, source_target_pairs={{0,48},{1,49},{2,50},{3,51},{4,52},{5,53},{6,54},{7,55},{8,56},{9,... | collective-permute-start | bytes 3145736 | tf_op jit(solution)/shard_map/ppermute | solution.py:256
  12.1 25.9 %collective-permute-start.1 = (bf16[512,1024]{1,0:T(8,128)(2,1)S(1)}, bf16[512,1024]{1,0:T(8,128)(2,1)}, u32[]{:S(2)}, u32[]{:S(2)}) collective-permute-start(bf16[512,1024]{1,0:T(8,128)(2,1)S(1)} %get-tuple-element.55.refs_0_), channel_id=1, source_target_pairs={{0,16},{1,17},{2,18},{3,19},{4,20},{5,21},{6,22},{7,23},{8,24},{9,... | collective-permute-start | bytes 3145736 | tf_op jit(solution)/shard_map/ppermute | solution.py:256
  12.1 24.4 %collective-permute-start = (bf16[512,512]{1,0:T(8,128)(2,1)}, bf16[512,512]{1,0:T(8,128)(2,1)S(1)}, u32[]{:S(2)}, u32[]{:S(2)}) collective-permute-start(bf16[512,512]{1,0:T(8,128)(2,1)} %param.10), channel_id=1, source_target_pairs={{0,0},{1,1},{2,2},{3,3},{4,4},{5,5},{6,6},{7,7},{8,70},{9,71},{10,... | collective-permute-start | bytes 1572872 | tf_op jit(solution)/shard_map/ppermute | solution.py:256
  18.0 5.0 %collective-permute-start.3 = (bf16[64,1024]{1,0:T(8,128)(2,1)S(1)}, bf16[64,1024]{1,0:T(8,128)(2,1)S(1)}, u32[]{:S(2)}, u32[]{:S(2)}) collective-permute-start(bf16[64,1024]{1,0:T(8,128)(2,1)S(1)} %constant_dynamic-update-slice_fusion), channel_id=1, source_target_pairs={{0,2},{1,3},{2,0},{3,1},{4,6},{5,7},{6,4},{7,5},{8,10},{9,11},{10,... | collective-permute-start | bytes 393224 | tf_op jit(solution)/shard_map/ppermute | solution.py:256
  23.0 13.4 %collective-permute-start.4 = (bf16[128,1024]{1,0:T(8,128)(2,1)S(1)}, bf16[128,1024]{1,0:T(8,128)(2,1)S(1)}, u32[]{:S(2)}, u32[]{:S(2)}) collective-permute-start(bf16[128,1024]{1,0:T(8,128)(2,1)S(1)} %pad_maximum_fusion.2), channel_id=1, source_target_pairs={{0,8},{1,9},{2,10},{3,11},{4,12},{5,13},{6,14},{7,15},{8,0},{9,1},... | collective-permute-start | bytes 786440 | tf_op jit(solution)/shard_map/ppermute | solution.py:256
  38.0 25.0 %collective-permute-start.7 = (bf16[512,1024]{1,0:T(8,128)(2,1)S(1)}, bf16[512,1024]{1,0:T(8,128)(2,1)S(1)}, u32[]{:S(2)}, u32[]{:S(2)}) collective-permute-start(bf16[512,1024]{1,0:T(8,128)(2,1)S(1)} %get-tuple-element.54.refs_1_), channel_id=1, source_target_pairs={{0,16},{1,17},{2,18},{3,19},{4,20},{5,21},{6,22},{7,23},{8,24},{9,... | collective-permute-start | bytes 3145736 | tf_op jit(solution)/shard_map/ppermute | solution.py:256
  38.1 24.9 %collective-permute-start.8 = (bf16[512,1024]{1,0:T(8,128)(2,1)S(1)}, bf16[512,1024]{1,0:T(8,128)(2,1)S(1)}, u32[]{:S(2)}, u32[]{:S(2)}) collective-permute-start(bf16[512,1024]{1,0:T(8,128)(2,1)S(1)} %get-tuple-element.55.refs_0_), channel_id=1, source_target_pairs={{0,48},{1,49},{2,50},{3,51},{4,52},{5,53},{6,54},{7,55},{8,56},{9,... | collective-permute-start | bytes 3145736 | tf_op jit(solution)/shard_map/ppermute | solution.py:256
  41.3 7.9 %collective-permute-start.6 = (bf16[128,1024]{1,0:T(8,128)(2,1)S(1)}, bf16[128,1024]{1,0:T(8,128)(2,1)S(1)}, u32[]{:S(2)}, u32[]{:S(2)}) collective-permute-start(bf16[128,1024]{1,0:T(8,128)(2,1)S(1)} %pad_maximum_fusion.2), channel_id=1, source_target_pairs={{0,12},{1,13},{2,14},{3,15},{4,0},{5,1},{6,2},{7,3},{8,4},{9,5},{1... | collective-permute-start | bytes 786440 | tf_op jit(solution)/shard_map/ppermute | solution.py:256
  45.4 8.6 %collective-permute-start.5 = (bf16[128,1024]{1,0:T(8,128)(2,1)S(1)}, bf16[128,1024]{1,0:T(8,128)(2,1)S(1)}, u32[]{:S(2)}, u32[]{:S(2)}) collective-permute-start(bf16[128,1024]{1,0:T(8,128)(2,1)S(1)} %pad_maximum_fusion.2), channel_id=1, source_target_pairs={{0,4},{1,5},{2,6},{3,7},{4,8},{5,9},{6,10},{7,11},{8,12},{9,13},{1... | collective-permute-start | bytes 786440 | tf_op jit(solution)/shard_map/ppermute | solution.py:256
  64.0 5.0 %collective-permute-start.9 = (bf16[512,1024]{1,0:T(8,128)(2,1)S(1)}, bf16[512,1024]{1,0:T(8,128)(2,1)}, u32[]{:S(2)}, u32[]{:S(2)}) collective-permute-start(bf16[512,1024]{1,0:T(8,128)(2,1)S(1)} %pad_maximum_fusion.1), channel_id=1, source_target_pairs={{0,1},{1,0},{2,3},{3,2},{4,5},{5,4},{6,7},{7,6},{8,9},{9,8},{10,11... | collective-permute-start | bytes 3145736 | tf_op jit(solution)/shard_map/ppermute | solution.py:256
  65.0 26.8 %collective-permute-start.10 = (bf16[512,1024]{1,0:T(8,128)(2,1)}, bf16[512,1024]{1,0:T(8,128)(2,1)}, u32[]{:S(2)}, u32[]{:S(2)}) collective-permute-start(bf16[512,1024]{1,0:T(8,128)(2,1)} %collective-permute-done.1.refs_2_), channel_id=1, source_target_pairs={{0,16},{1,17},{2,18},{3,19},{4,20},{5,21},{6,22},{7,23},{8,24},{9,... | collective-permute-start | bytes 3145736 | tf_op jit(solution)/shard_map/ppermute | solution.py:256
  65.0 26.8 %collective-permute-start.11 = (bf16[512,1024]{1,0:T(8,128)(2,1)}, bf16[512,1024]{1,0:T(8,128)(2,1)}, u32[]{:S(2)}, u32[]{:S(2)}) collective-permute-start(bf16[512,1024]{1,0:T(8,128)(2,1)} %collective-permute-done.2.refs_5_), channel_id=1, source_target_pairs={{0,48},{1,49},{2,50},{3,51},{4,52},{5,53},{6,54},{7,55},{8,56},{9,... | collective-permute-start | bytes 3145736 | tf_op jit(solution)/shard_map/ppermute | solution.py:256
  90.4 27.9 %collective-permute-start.12 = (bf16[1024,512]{1,0:T(8,128)(2,1)}, bf16[1024,512]{1,0:T(8,128)(2,1)}, u32[]{:S(2)}, u32[]{:S(2)}) collective-permute-start(bf16[1024,512]{1,0:T(8,128)(2,1)} %get-tuple-element.38.refs_8_), channel_id=1, source_target_pairs={{0,64},{1,65},{2,66},{3,67},{4,68},{5,69},{6,70},{7,71},{8,72},{9,... | collective-permute-start | bytes 3145736 | tf_op jit(solution)/shard_map/ppermute | solution.py:256
  103.4 26.1 %collective-permute-start.13 = (bf16[512,512]{1,0:T(8,128)(2,1)S(1)}, bf16[512,512]{1,0:T(8,128)(2,1)S(1)}, u32[]{:S(2)}, u32[]{:S(2)}) collective-permute-start(bf16[512,512]{1,0:T(8,128)(2,1)S(1)} %get-tuple-element.60), channel_id=1, source_target_pairs={{0,64},{1,65},{2,66},{3,67},{4,68},{5,69},{6,70},{7,71},{8,72},{9,... | collective-permute-start | bytes 1572872 | tf_op jit(solution)/shard_map/ppermute | solution.py:256
  129.5 7.6 %collective-permute-start.14 = (bf16[2048,1024]{1,0:T(8,128)(2,1)}, bf16[2048,1024]{1,0:T(8,128)(2,1)}, u32[]{:S(2)}, u32[]{:S(2)}) collective-permute-start(bf16[2048,1024]{1,0:T(8,128)(2,1)} %outer.2), channel_id=1, source_target_pairs={{0,1},{1,0},{2,3},{3,2},{4,5},{5,4},{6,7},{7,6},{8,9},{9,8},{10,11... | collective-permute-start | bytes 12582920 | tf_op jit(solution)/shard_map/ppermute | solution.py:256
  129.6 19.8 %collective-permute-start.15 = (bf16[512,512]{1,0:T(8,128)(2,1)S(1)}, bf16[512,512]{1,0:T(8,128)(2,1)S(1)}, u32[]{:S(2)}, u32[]{:S(2)}) collective-permute-start(bf16[512,512]{1,0:T(8,128)(2,1)S(1)} %get-tuple-element.59), channel_id=1, source_target_pairs={{0,64},{1,65},{2,66},{3,67},{4,68},{5,69},{6,70},{7,71},{8,72},{9,... | collective-permute-start | bytes 1572872 | tf_op jit(solution)/shard_map/ppermute | solution.py:256
  150.3 67.5 %all-to-all-start = ((bf16[8,512,512]{2,1,0:T(8,128)(2,1)}), bf16[8,512,512]{2,1,0:T(8,128)(2,1)}, u32[]{:S(2)}, u32[]{:S(2)}) async-start(bf16[8,512,512]{2,1,0:T(8,128)(2,1)} %bitcast.12), calls=%async_computation | async-start | bytes 8388608 | tf_op jit(solution)/shard_map/all_to_all | solution.py:313
  182.7 2.7 %collective-permute-start.16 = (bf16[512,1024]{1,0:T(8,128)(2,1)S(1)}, bf16[512,1024]{1,0:T(8,128)(2,1)S(1)}, u32[]{:S(2)}, u32[]{:S(2)}) collective-permute-start(bf16[512,1024]{1,0:T(8,128)(2,1)S(1)} %get-tuple-element.52), channel_id=1, source_target_pairs={{0,1},{1,0},{2,3},{3,2},{4,5},{5,4},{6,7},{7,6},{8,9},{9,8},{10,11... | collective-permute-start | bytes 3145736 | tf_op jit(solution)/shard_map/ppermute | solution.py:256
  185.8 24.1 %collective-permute-start.17 = (bf16[128,1024]{1,0:T(8,128)(2,1)S(1)}, bf16[128,1024]{1,0:T(8,128)(2,1)S(1)}, u32[]{:S(2)}, u32[]{:S(2)}) collective-permute-start(bf16[128,1024]{1,0:T(8,128)(2,1)S(1)} %get-tuple-element.56), channel_id=1, source_target_pairs={{0,12},{1,13},{2,14},{3,15},{4,0},{5,1},{6,2},{7,3},{8,4},{9,5},{1... | collective-permute-start | bytes 786440 | tf_op jit(solution)/shard_map/ppermute | solution.py:256
  188.6 23.9 %collective-permute-start.19 = (bf16[128,1024]{1,0:T(8,128)(2,1)S(1)}, bf16[128,1024]{1,0:T(8,128)(2,1)S(1)}, u32[]{:S(2)}, u32[]{:S(2)}) collective-permute-start(bf16[128,1024]{1,0:T(8,128)(2,1)S(1)} %get-tuple-element.57), channel_id=1, source_target_pairs={{0,8},{1,9},{2,10},{3,11},{4,12},{5,13},{6,14},{7,15},{8,0},{9,1},... | collective-permute-start | bytes 786440 | tf_op jit(solution)/shard_map/ppermute | solution.py:256
  189.4 27.2 %collective-permute-start.18 = (bf16[128,1024]{1,0:T(8,128)(2,1)S(1)}, bf16[128,1024]{1,0:T(8,128)(2,1)S(1)}, u32[]{:S(2)}, u32[]{:S(2)}) collective-permute-start(bf16[128,1024]{1,0:T(8,128)(2,1)S(1)} %get-tuple-element.58), channel_id=1, source_target_pairs={{0,4},{1,5},{2,6},{3,7},{4,8},{5,9},{6,10},{7,11},{8,12},{9,13},{1... | collective-permute-start | bytes 786440 | tf_op jit(solution)/shard_map/ppermute | solution.py:256
  216.8 8.0 %collective-permute-start.20 = (bf16[64,1024]{1,0:T(8,128)(2,1)S(1)}, bf16[64,1024]{1,0:T(8,128)(2,1)S(1)}, u32[]{:S(2)}, u32[]{:S(2)}) collective-permute-start(bf16[64,1024]{1,0:T(8,128)(2,1)S(1)} %slice.57), channel_id=1, source_target_pairs={{0,2},{1,3},{2,0},{3,1},{4,6},{5,7},{6,4},{7,5},{8,10},{9,11},{10,... | collective-permute-start | bytes 393224 | tf_op jit(solution)/shard_map/ppermute | solution.py:256
  220.8 18.8 %collective-permute-start.21 = (bf16[512,512]{1,0:T(8,128)(2,1)S(1)}, bf16[512,512]{1,0:T(8,128)(2,1)S(1)}, u32[]{:S(2)}, u32[]{:S(2)}) collective-permute-start(bf16[512,512]{1,0:T(8,128)(2,1)S(1)} %reduce_sum.12), channel_id=1, source_target_pairs={{0,0},{1,1},{2,2},{3,3},{4,4},{5,5},{6,6},{7,7},{8,70},{9,71},{10,... | collective-permute-start | bytes 1572872 | tf_op jit(solution)/shard_map/ppermute | solution.py:256
  (23 other events, 276.1 us)
Sparse Core Ops, SparseCore 0:
  38.2 51.7 all-gather.1

commit v5 on v4

--- a/solution.py
+++ b/solution.py
@@ -178,10 +178,15 @@
             rest[0][here, :] = out.astype(jnp.bfloat16)
         else:
             out = (out + rest[0][here, :].astype(jnp.float32)).astype(jnp.bfloat16)
+            piece = size // 2
             for f in range(2):
                 away = f + upper - 2 * f * upper
-                to = 4 * f + slot + away * (3 - 2 * slot)
-                rest[1][pl.ds(pl.multiple_of(to * size, size), size), :] = out[:, f * width : (f + 1) * width]
+                for r in range(2):
+                    chunk = slot ^ (2 * r)
+                    to = 4 * (upper + r - 2 * r * upper) + chunk + away * (1 - 2 * (chunk % 2))
+                    rest[1][pl.ds(pl.multiple_of((2 * to + away) * piece, piece), piece), :] = out[
+                        r * piece : (r + 1) * piece, f * width : (f + 1) * width
+                    ]
 
 
 def outer(place, columns, own, other, added=None):
@@ -241,6 +246,15 @@
     return pairs
 
 
+def owner_pairs(other, r):
+    pairs = []
+    for d in every():
+        xh, y, z, xl, core = d
+        if z // 2 == xh ^ r:
+            pairs.append((device(*d), device(xh ^ other, y, xh * 2 + (z % 2 ^ r), xl ^ other, core)))
+    return pairs
+
+
 def place_table():
     rows = []
     for xh, y, z, xl, core in every():
@@ -312,7 +326,15 @@
     groups = [[2 * i + c for i in range(8)] for c in range(2)]
     pieces = lax.all_to_all(pieces, "col", split_axis=0, concat_axis=0, axis_index_groups=groups, tiled=True)
     total = jnp.sum(f32(pieces.reshape(8, -1, width)), axis=0).astype(bf16)
-    grad_weight = send(total, swap)
+    own_sum, other_sum = total[: total.shape[0] // 2], total[total.shape[0] // 2 :]
+    stays = lax.axis_index("row") // 4 == lax.axis_index("col") // 8
+    grad_weight = jnp.concatenate(
+        [
+            jnp.where(stays, own_sum, send(other_sum, owner_pairs(1, 0))),
+            jnp.where(stays, send(own_sum, owner_pairs(0, 1)), send(other_sum, owner_pairs(1, 1))),
+        ],
+        axis=0,
+    )
 
     grad_q, grad_k, grad_v, keep, away = bwd(
         block_table, place, queries, keys, values, cache, probs, own_part, from_upper, from_lower

time: 248 us -> 241 us (0.972)
  waiting for transfers between devices: 86.8 us -> 74.8 us
  starting transfers between devices: 42.1 us -> 44.6 us
    ppermute x22 -> x24, waiting for transfers between devices: 86.8 us -> 58.7 us  [send(): return lax.ppermute(array, AXES, pairs)]
    all_to_all x1, waiting for transfers between devices: 0.01 us -> 16 us  [per_device(): lax.all_to_all(pieces, 'col', split_axis=0, concat_axis=0, axis_index_gro...]
    ppermute x22 -> x24, starting transfers between devices: 35.1 us -> 37.6 us  [send(): return lax.ppermute(array, AXES, pairs)]
    unnamed x49 -> x48, local copies, waits for them, and re-layouts: 12.8 us -> 12 us
  transfers between devices with their start and end apart: 24 -> 26, of which waited for: 13 -> 13; matrix products, arithmetic and copies ran while one was open for 4% -> 4% of each run, Pallas kernels for 32% -> 34%
where the time goes in v5:
time: 241 us; the launch traced here: 239 us
  Pallas kernels  80.2 us (33%)
  waiting for transfers between devices  74.8 us (31%)
  starting transfers between devices  44.6 us (19%)
  local copies, waits for them, and re-layouts  17.2 us (7%)
  between operations  14.4 us (6%)
  other arithmetic  7.53 us (3%)
    ppermute x24, waiting for transfers between devices, send(): return lax.ppermute(array, AXES, pairs)  58.7 us
    ppermute x24, starting transfers between devices, send(): return lax.ppermute(array, AXES, pairs)  37.6 us
    pallas_call x2, Pallas kernels, outer(): pl.pallas_call(outer_kernel, grid_spec=pltpu.PrefetchScalarGridSpec(num_s...  23.6 us
    pallas_call x2, Pallas kernels, project(): pl.pallas_call(functools.partial(project_kernel, other), grid_spec=pltpu....  20.9 us
    pallas_call x1, Pallas kernels, bwd(): pl.pallas_call(functools.partial(bwd_kernel, heads), grid_spec=pltpu.Pref...  19.4 us
    pallas_call x1, Pallas kernels, fwd(): pl.pallas_call(functools.partial(fwd_kernel, heads), grid_spec=pltpu.Pref...  16.4 us
    all_to_all x1, waiting for transfers between devices, per_device(): lax.all_to_all(pieces, 'col', split_axis=0, concat_axis=0, axis_index_gro...  16 us
    unnamed x48, local copies, waits for them, and re-layouts  12 us
  transfers between devices with their start and end apart: 26, of which 13 were waited for; matrix products, arithmetic and copies ran while one was open for 4% of the time, Pallas kernels for 34%

profile of v5, /device:TPU:6, one launch (start us, length us, event | category | flops | bytes accessed | tf_op | source)
XLA Modules:
  0.0 238.7 jit_solution(12211546393230537850)
XLA Ops:
  9.0 3.1 %collective-permute-start.2 = (bf16[512,1024]{1,0:T(8,128)(2,1)S(1)}, bf16[512,1024]{1,0:T(8,128)(2,1)}, u32[]{:S(2)}, u32[]{:S(2)}) collective-permute-start(bf16[512,1024]{1,0:T(8,128)(2,1)S(1)} %get-tuple-element.54.refs_1_), channel_id=1, source_target_pairs={{0,48},{1,49},{2,50},{3,51},{4,52},{5,53},{6,54},{7,55},{8,56},{9,... | collective-permute-start | bytes 3145736 | tf_op jit(solution)/shard_map/ppermute | solution.py:270
  12.1 5.9 %collective-permute-start = (bf16[512,512]{1,0:T(8,128)(2,1)}, bf16[512,512]{1,0:T(8,128)(2,1)S(1)}, u32[]{:S(2)}, u32[]{:S(2)}) collective-permute-start(bf16[512,512]{1,0:T(8,128)(2,1)} %param.10), channel_id=1, source_target_pairs={{0,0},{1,1},{2,2},{3,3},{4,4},{5,5},{6,6},{7,7},{8,70},{9,71},{10,... | collective-permute-start | bytes 1572872 | tf_op jit(solution)/shard_map/ppermute | solution.py:270
  18.9 4.1 %collective-permute-done.3 = bf16[64,1024]{1,0:T(8,128)(2,1)S(1)} collective-permute-done((bf16[64,1024]{1,0:T(8,128)(2,1)S(1)}, bf16[64,1024]{1,0:T(8,128)(2,1)S(1)}, u32[]{:S(2)}, u32[]{:S(2)}) %collective-permute-start.3) | collective-permute-done | bytes 131104 | tf_op jit(solution)/shard_map/ppermute | solution.py:270
  23.1 13.3 %collective-permute-done.4 = bf16[128,1024]{1,0:T(8,128)(2,1)S(1)} collective-permute-done((bf16[128,1024]{1,0:T(8,128)(2,1)S(1)}, bf16[128,1024]{1,0:T(8,128)(2,1)S(1)}, u32[]{:S(2)}, u32[]{:S(2)}) %collective-permute-start.4) | collective-permute-done | bytes 262176 | tf_op jit(solution)/shard_map/ppermute | solution.py:270
  38.1 3.2 %collective-permute-start.8 = (bf16[512,1024]{1,0:T(8,128)(2,1)S(1)}, bf16[512,1024]{1,0:T(8,128)(2,1)S(1)}, u32[]{:S(2)}, u32[]{:S(2)}) collective-permute-start(bf16[512,1024]{1,0:T(8,128)(2,1)S(1)} %get-tuple-element.55.refs_0_), channel_id=1, source_target_pairs={{0,48},{1,49},{2,50},{3,51},{4,52},{5,53},{6,54},{7,55},{8,56},{9,... | collective-permute-start | bytes 3145736 | tf_op jit(solution)/shard_map/ppermute | solution.py:270
  41.3 4.0 %collective-permute-start.6 = (bf16[128,1024]{1,0:T(8,128)(2,1)S(1)}, bf16[128,1024]{1,0:T(8,128)(2,1)S(1)}, u32[]{:S(2)}, u32[]{:S(2)}) collective-permute-start(bf16[128,1024]{1,0:T(8,128)(2,1)S(1)} %pad_maximum_fusion.3), channel_id=1, source_target_pairs={{0,12},{1,13},{2,14},{3,15},{4,0},{5,1},{6,2},{7,3},{8,4},{9,5},{1... | collective-permute-start | bytes 786440 | tf_op jit(solution)/shard_map/ppermute | solution.py:270
  45.4 3.9 %collective-permute-done.6 = bf16[128,1024]{1,0:T(8,128)(2,1)S(1)} collective-permute-done((bf16[128,1024]{1,0:T(8,128)(2,1)S(1)}, bf16[128,1024]{1,0:T(8,128)(2,1)S(1)}, u32[]{:S(2)}, u32[]{:S(2)}) %collective-permute-start.6) | collective-permute-done | bytes 262176 | tf_op jit(solution)/shard_map/ppermute | solution.py:270
  49.3 4.7 %collective-permute-done.5 = bf16[128,1024]{1,0:T(8,128)(2,1)S(1)} collective-permute-done((bf16[128,1024]{1,0:T(8,128)(2,1)S(1)}, bf16[128,1024]{1,0:T(8,128)(2,1)S(1)}, u32[]{:S(2)}, u32[]{:S(2)}) %collective-permute-start.5) | collective-permute-done | bytes 262176 | tf_op jit(solution)/shard_map/ppermute | solution.py:270
  55.0 8.0 %collective-permute-done.7.refs_3_ = bf16[512,1024]{1,0:T(8,128)(2,1)S(1)} collective-permute-done((bf16[512,1024]{1,0:T(8,128)(2,1)S(1)}, bf16[512,1024]{1,0:T(8,128)(2,1)S(1)}, u32[]{:S(2)}, u32[]{:S(2)}) %collective-permute-start.7) | collective-permute-done | bytes 1048608 | tf_op jit(solution)/shard_map/ppermute | solution.py:270
  65.0 3.2 %collective-permute-start.11 = (bf16[512,1024]{1,0:T(8,128)(2,1)}, bf16[512,1024]{1,0:T(8,128)(2,1)}, u32[]{:S(2)}, u32[]{:S(2)}) collective-permute-start(bf16[512,1024]{1,0:T(8,128)(2,1)} %collective-permute-done.2.refs_5_), channel_id=1, source_target_pairs={{0,48},{1,49},{2,50},{3,51},{4,52},{5,53},{6,54},{7,55},{8,56},{9,... | collective-permute-start | bytes 3145736 | tf_op jit(solution)/shard_map/ppermute | solution.py:270
  71.6 16.4 %attn_fwd.1 = (bf16[1024,512]{1,0:T(8,128)(2,1)}, bf16[8,4,640,128]{3,2,1,0:T(8,128)(2,1)S(1)}) custom-call(s32[8,4]{1,0:T(8,128)S(1)} %copy.18.table, s32[24]{0:T(128)S(1)} %dynamic-slice_bitcast_fusion.place, bf16[1024,512]{1,0:T(8,128)(2,1)S(1)} %copy-done.2, bf16[1024,512]{1,0:T(8,128)(2,1)S(1)} %copy-done.3, bf16[1024,512]{1,0:T(8,128)(2,1)S(1)} %copy-done.5, ...), custom_call_target="tpu_custom_call" | custom-call | flops 1048576 | bytes 65536 | tf_op jit(solution)/shard_map/attn_fwd/pallas_call | solution.py:42
  91.8 10.3 %project.2 = bf16[1024,512]{1,0:T(8,128)(2,1)} custom-call(s32[24]{0:T(128)} %copy-done.11, bf16[512,1024]{1,0:T(8,128)(2,1)} %copy-done.14, bf16[512,1024]{1,0:T(8,128)(2,1)} %copy-done.13, bf16[512,1024]{1,0:T(8,128)(2,1)} %collective-permute-done.1.refs_2_, bf16[512,1024]{1,0:T(8,128)(2,1)} %copy-done.15, bf16[512,1024]{1,0:T(8,128)(2,1)} %copy-done.16, ...), custom_call_target="tpu_custom_call" | custom-call | flops 1048576 | bytes 65536 | tf_op jit(solution)/shard_map/project/pallas_call | solution.py:134
  105.6 10.5 %project.3.ga_ref = f32[1024,512]{1,0:T(8,128)} custom-call(s32[24]{0:T(128)} %copy-done.11, bf16[512,1024]{1,0:T(8,128)(2,1)} %copy-done.14, bf16[512,1024]{1,0:T(8,128)(2,1)} %copy-done.13, bf16[512,1024]{1,0:T(8,128)(2,1)} %collective-permute-done.1.refs_2_, bf16[512,1024]{1,0:T(8,128)(2,1)} %copy-done.15, bf16[512,1024]{1,0:T(8,128)(2,1)} %copy-done.16, ...), custom_call_target="tpu_custom_call" | custom-call | flops 1048576 | bytes 65536 | tf_op jit(solution)/shard_map/project/pallas_call | solution.py:134
  118.3 11.2 %outer.2 = bf16[2048,1024]{1,0:T(8,128)(2,1)} custom-call(s32[24]{0:T(128)} %copy-done.11, bf16[512,1024]{1,0:T(8,128)(2,1)} %copy-done.14, bf16[512,1024]{1,0:T(8,128)(2,1)} %copy-done.13, bf16[512,1024]{1,0:T(8,128)(2,1)} %collective-permute-done.1.refs_2_, bf16[512,1024]{1,0:T(8,128)(2,1)} %copy-done.15, bf16[512,1024]{1,0:T(8,128)(2,1)} %copy-done.16, ...), custom_call_target="tpu_custom_call" | custom-call | flops 1048576 | bytes 65536 | tf_op jit(solution)/shard_map/outer/pallas_call | solution.py:200
  131.1 6.0 %collective-permute-done.14.refs_10_ = bf16[2048,1024]{1,0:T(8,128)(2,1)} collective-permute-done((bf16[2048,1024]{1,0:T(8,128)(2,1)}, bf16[2048,1024]{1,0:T(8,128)(2,1)}, u32[]{:S(2)}, u32[]{:S(2)}) %collective-permute-start.14) | collective-permute-done | bytes 4194336 | tf_op jit(solution)/shard_map/ppermute | solution.py:270
  137.1 12.4 %outer.3 = bf16[4096,512]{1,0:T(8,128)(2,1)} custom-call(s32[24]{0:T(128)} %copy-done.11, bf16[512,1024]{1,0:T(8,128)(2,1)} %copy-done.14, bf16[512,1024]{1,0:T(8,128)(2,1)} %copy-done.13, bf16[512,1024]{1,0:T(8,128)(2,1)} %collective-permute-done.1.refs_2_, bf16[512,1024]{1,0:T(8,128)(2,1)} %copy-done.15, bf16[512,1024]{1,0:T(8,128)(2,1)} %copy-done.16, ...), custom_call_target="tpu_custom_call" | custom-call | flops 1048576 | bytes 65536 | tf_op jit(solution)/shard_map/outer/pallas_call | solution.py:200
  150.3 6.9 %all-to-all-start = ((bf16[8,512,512]{2,1,0:T(8,128)(2,1)}), bf16[8,512,512]{2,1,0:T(8,128)(2,1)}, u32[]{:S(2)}, u32[]{:S(2)}) async-start(bf16[8,512,512]{2,1,0:T(8,128)(2,1)} %bitcast.12), calls=%async_computation | async-start | bytes 8388608 | tf_op jit(solution)/shard_map/all_to_all | solution.py:327
  163.3 19.4 %attn_bwd.1 = (bf16[1024,512]{1,0:T(8,128)(2,1)}, bf16[1024,512]{1,0:T(8,128)(2,1)}, bf16[1024,512]{1,0:T(8,128)(2,1)}, bf16[512,1024]{1,0:T(8,128)(2,1)S(1)}, bf16[512,1024]{1,0:T(8,128)(2,1)S(1)}) custom-call(s32[8,4]{1,0:T(8,128)S(1)} %copy.18.table, s32[24]{0:T(128)S(1)} %copy-done.12, bf16[1024,512]{1,0:T(8,128)(2,1)S(1)} %copy-done.2, ...), custom_call_target="tpu_custom_call" | custom-call | flops 1048576 | bytes 65536 | tf_op jit(solution)/shard_map/attn_bwd/pallas_call | solution.py:91
  186.6 2.7 %collective-permute-start.17 = (bf16[128,1024]{1,0:T(8,128)(2,1)}, bf16[128,1024]{1,0:T(8,128)(2,1)S(1)}, u32[]{:S(2)}, u32[]{:S(2)}) collective-permute-start(bf16[128,1024]{1,0:T(8,128)(2,1)} %get-tuple-element.56), channel_id=1, source_target_pairs={{0,12},{1,13},{2,14},{3,15},{4,0},{5,1},{6,2},{7,3},{8,4},{9,5},{1... | collective-permute-start | bytes 786440 | tf_op jit(solution)/shard_map/ppermute | solution.py:270
  191.0 16.0 %all-to-all-done = bf16[8,512,512]{2,1,0:T(8,128)(2,1)} async-done(((bf16[8,512,512]{2,1,0:T(8,128)(2,1)}), bf16[8,512,512]{2,1,0:T(8,128)(2,1)}, u32[]{:S(2)}, u32[]{:S(2)}) %all-to-all-start) | async-done | bytes 4194336 | tf_op jit(solution)/shard_map/all_to_all | solution.py:327
  207.0 3.1 %reduce_sum.12 = bf16[512,512]{1,0:T(8,128)(2,1)S(1)} reduce(bf16[8,512,512]{2,1,0:T(8,128)(2,1)} %all-to-all-done, bf16[]{:T(256)} %constant.46.clone.1), dimensions={0}, to_apply=%region_0.1 | reduce | flops 1835008 | bytes 4718594 | tf_op jit(solution)/shard_map/reduce_sum | solution.py:328
  212.5 4.2 %collective-permute-done.18 = bf16[128,1024]{1,0:T(8,128)(2,1)S(1)} collective-permute-done((bf16[128,1024]{1,0:T(8,128)(2,1)S(1)}, bf16[128,1024]{1,0:T(8,128)(2,1)S(1)}, u32[]{:S(2)}, u32[]{:S(2)}) %collective-permute-start.18) | collective-permute-done | bytes 262176 | tf_op jit(solution)/shard_map/ppermute | solution.py:270
  217.8 4.0 %collective-permute-start.23 = (bf16[256,512]{1,0:T(8,128)(2,1)S(1)}, bf16[256,512]{1,0:T(8,128)(2,1)S(1)}, u32[]{:S(2)}, u32[]{:S(2)}) collective-permute-start(bf16[256,512]{1,0:T(8,128)(2,1)S(1)} %slice.69), channel_id=1, source_target_pairs={{8,70},{9,71},{10,68},{11,69},{12,66},{13,67},{14,64},{15,65},{24,... | collective-permute-start | bytes 786440 | tf_op jit(solution)/shard_map/ppermute | solution.py:270
  223.9 7.1 %collective-permute-done.23 = bf16[256,512]{1,0:T(8,128)(2,1)S(1)} collective-permute-done((bf16[256,512]{1,0:T(8,128)(2,1)S(1)}, bf16[256,512]{1,0:T(8,128)(2,1)S(1)}, u32[]{:S(2)}, u32[]{:S(2)}) %collective-permute-start.23) | collective-permute-done | bytes 262176 | tf_op jit(solution)/shard_map/ppermute | solution.py:270
  (101 shorter events, 40.7 us)
Async XLA Ops:
  7.2 84.6 %all-gather.2.cloned.1.call-start = ((), (), s32[]{:S(2)}) async-start(), calls=%async_computation.1 | async-start | bytes 8912896 | tf_op jit(solution)/shard_map/all_gather | solution.py:303
  9.0 27.5 %collective-permute-start.2 = (bf16[512,1024]{1,0:T(8,128)(2,1)S(1)}, bf16[512,1024]{1,0:T(8,128)(2,1)}, u32[]{:S(2)}, u32[]{:S(2)}) collective-permute-start(bf16[512,1024]{1,0:T(8,128)(2,1)S(1)} %get-tuple-element.54.refs_1_), channel_id=1, source_target_pairs={{0,48},{1,49},{2,50},{3,51},{4,52},{5,53},{6,54},{7,55},{8,56},{9,... | collective-permute-start | bytes 3145736 | tf_op jit(solution)/shard_map/ppermute | solution.py:270
  12.1 25.9 %collective-permute-start.1 = (bf16[512,1024]{1,0:T(8,128)(2,1)S(1)}, bf16[512,1024]{1,0:T(8,128)(2,1)}, u32[]{:S(2)}, u32[]{:S(2)}) collective-permute-start(bf16[512,1024]{1,0:T(8,128)(2,1)S(1)} %get-tuple-element.55.refs_0_), channel_id=1, source_target_pairs={{0,16},{1,17},{2,18},{3,19},{4,20},{5,21},{6,22},{7,23},{8,24},{9,... | collective-permute-start | bytes 3145736 | tf_op jit(solution)/shard_map/ppermute | solution.py:270
  12.1 24.4 %collective-permute-start = (bf16[512,512]{1,0:T(8,128)(2,1)}, bf16[512,512]{1,0:T(8,128)(2,1)S(1)}, u32[]{:S(2)}, u32[]{:S(2)}) collective-permute-start(bf16[512,512]{1,0:T(8,128)(2,1)} %param.10), channel_id=1, source_target_pairs={{0,0},{1,1},{2,2},{3,3},{4,4},{5,5},{6,6},{7,7},{8,70},{9,71},{10,... | collective-permute-start | bytes 1572872 | tf_op jit(solution)/shard_map/ppermute | solution.py:270
  18.0 5.0 %collective-permute-start.3 = (bf16[64,1024]{1,0:T(8,128)(2,1)S(1)}, bf16[64,1024]{1,0:T(8,128)(2,1)S(1)}, u32[]{:S(2)}, u32[]{:S(2)}) collective-permute-start(bf16[64,1024]{1,0:T(8,128)(2,1)S(1)} %constant_dynamic-update-slice_fusion), channel_id=1, source_target_pairs={{0,2},{1,3},{2,0},{3,1},{4,6},{5,7},{6,4},{7,5},{8,10},{9,11},{10,... | collective-permute-start | bytes 393224 | tf_op jit(solution)/shard_map/ppermute | solution.py:270
  23.0 13.4 %collective-permute-start.4 = (bf16[128,1024]{1,0:T(8,128)(2,1)S(1)}, bf16[128,1024]{1,0:T(8,128)(2,1)S(1)}, u32[]{:S(2)}, u32[]{:S(2)}) collective-permute-start(bf16[128,1024]{1,0:T(8,128)(2,1)S(1)} %pad_maximum_fusion.3), channel_id=1, source_target_pairs={{0,8},{1,9},{2,10},{3,11},{4,12},{5,13},{6,14},{7,15},{8,0},{9,1},... | collective-permute-start | bytes 786440 | tf_op jit(solution)/shard_map/ppermute | solution.py:270
  38.0 25.0 %collective-permute-start.7 = (bf16[512,1024]{1,0:T(8,128)(2,1)S(1)}, bf16[512,1024]{1,0:T(8,128)(2,1)S(1)}, u32[]{:S(2)}, u32[]{:S(2)}) collective-permute-start(bf16[512,1024]{1,0:T(8,128)(2,1)S(1)} %get-tuple-element.54.refs_1_), channel_id=1, source_target_pairs={{0,16},{1,17},{2,18},{3,19},{4,20},{5,21},{6,22},{7,23},{8,24},{9,... | collective-permute-start | bytes 3145736 | tf_op jit(solution)/shard_map/ppermute | solution.py:270
  38.1 24.9 %collective-permute-start.8 = (bf16[512,1024]{1,0:T(8,128)(2,1)S(1)}, bf16[512,1024]{1,0:T(8,128)(2,1)S(1)}, u32[]{:S(2)}, u32[]{:S(2)}) collective-permute-start(bf16[512,1024]{1,0:T(8,128)(2,1)S(1)} %get-tuple-element.55.refs_0_), channel_id=1, source_target_pairs={{0,48},{1,49},{2,50},{3,51},{4,52},{5,53},{6,54},{7,55},{8,56},{9,... | collective-permute-start | bytes 3145736 | tf_op jit(solution)/shard_map/ppermute | solution.py:270
  41.3 7.9 %collective-permute-start.6 = (bf16[128,1024]{1,0:T(8,128)(2,1)S(1)}, bf16[128,1024]{1,0:T(8,128)(2,1)S(1)}, u32[]{:S(2)}, u32[]{:S(2)}) collective-permute-start(bf16[128,1024]{1,0:T(8,128)(2,1)S(1)} %pad_maximum_fusion.3), channel_id=1, source_target_pairs={{0,12},{1,13},{2,14},{3,15},{4,0},{5,1},{6,2},{7,3},{8,4},{9,5},{1... | collective-permute-start | bytes 786440 | tf_op jit(solution)/shard_map/ppermute | solution.py:270
  45.4 8.6 %collective-permute-start.5 = (bf16[128,1024]{1,0:T(8,128)(2,1)S(1)}, bf16[128,1024]{1,0:T(8,128)(2,1)S(1)}, u32[]{:S(2)}, u32[]{:S(2)}) collective-permute-start(bf16[128,1024]{1,0:T(8,128)(2,1)S(1)} %pad_maximum_fusion.3), channel_id=1, source_target_pairs={{0,4},{1,5},{2,6},{3,7},{4,8},{5,9},{6,10},{7,11},{8,12},{9,13},{1... | collective-permute-start | bytes 786440 | tf_op jit(solution)/shard_map/ppermute | solution.py:270
  65.0 26.8 %collective-permute-start.10 = (bf16[512,1024]{1,0:T(8,128)(2,1)}, bf16[512,1024]{1,0:T(8,128)(2,1)}, u32[]{:S(2)}, u32[]{:S(2)}) collective-permute-start(bf16[512,1024]{1,0:T(8,128)(2,1)} %collective-permute-done.1.refs_2_), channel_id=1, source_target_pairs={{0,16},{1,17},{2,18},{3,19},{4,20},{5,21},{6,22},{7,23},{8,24},{9,... | collective-permute-start | bytes 3145736 | tf_op jit(solution)/shard_map/ppermute | solution.py:270
  65.0 26.8 %collective-permute-start.11 = (bf16[512,1024]{1,0:T(8,128)(2,1)}, bf16[512,1024]{1,0:T(8,128)(2,1)}, u32[]{:S(2)}, u32[]{:S(2)}) collective-permute-start(bf16[512,1024]{1,0:T(8,128)(2,1)} %collective-permute-done.2.refs_5_), channel_id=1, source_target_pairs={{0,48},{1,49},{2,50},{3,51},{4,52},{5,53},{6,54},{7,55},{8,56},{9,... | collective-permute-start | bytes 3145736 | tf_op jit(solution)/shard_map/ppermute | solution.py:270
  90.4 27.9 %collective-permute-start.12 = (bf16[1024,512]{1,0:T(8,128)(2,1)}, bf16[1024,512]{1,0:T(8,128)(2,1)}, u32[]{:S(2)}, u32[]{:S(2)}) collective-permute-start(bf16[1024,512]{1,0:T(8,128)(2,1)} %get-tuple-element.38.refs_8_), channel_id=1, source_target_pairs={{0,64},{1,65},{2,66},{3,67},{4,68},{5,69},{6,70},{7,71},{8,72},{9,... | collective-permute-start | bytes 3145736 | tf_op jit(solution)/shard_map/ppermute | solution.py:270
  103.4 26.1 %collective-permute-start.13 = (bf16[512,512]{1,0:T(8,128)(2,1)S(1)}, bf16[512,512]{1,0:T(8,128)(2,1)S(1)}, u32[]{:S(2)}, u32[]{:S(2)}) collective-permute-start(bf16[512,512]{1,0:T(8,128)(2,1)S(1)} %get-tuple-element.60), channel_id=1, source_target_pairs={{0,64},{1,65},{2,66},{3,67},{4,68},{5,69},{6,70},{7,71},{8,72},{9,... | collective-permute-start | bytes 1572872 | tf_op jit(solution)/shard_map/ppermute | solution.py:270
  129.5 7.6 %collective-permute-start.14 = (bf16[2048,1024]{1,0:T(8,128)(2,1)}, bf16[2048,1024]{1,0:T(8,128)(2,1)}, u32[]{:S(2)}, u32[]{:S(2)}) collective-permute-start(bf16[2048,1024]{1,0:T(8,128)(2,1)} %outer.2), channel_id=1, source_target_pairs={{0,1},{1,0},{2,3},{3,2},{4,5},{5,4},{6,7},{7,6},{8,9},{9,8},{10,11... | collective-permute-start | bytes 12582920 | tf_op jit(solution)/shard_map/ppermute | solution.py:270
  129.6 19.8 %collective-permute-start.15 = (bf16[512,512]{1,0:T(8,128)(2,1)S(1)}, bf16[512,512]{1,0:T(8,128)(2,1)S(1)}, u32[]{:S(2)}, u32[]{:S(2)}) collective-permute-start(bf16[512,512]{1,0:T(8,128)(2,1)S(1)} %get-tuple-element.59), channel_id=1, source_target_pairs={{0,64},{1,65},{2,66},{3,67},{4,68},{5,69},{6,70},{7,71},{8,72},{9,... | collective-permute-start | bytes 1572872 | tf_op jit(solution)/shard_map/ppermute | solution.py:270
  150.3 56.7 %all-to-all-start = ((bf16[8,512,512]{2,1,0:T(8,128)(2,1)}), bf16[8,512,512]{2,1,0:T(8,128)(2,1)}, u32[]{:S(2)}, u32[]{:S(2)}) async-start(bf16[8,512,512]{2,1,0:T(8,128)(2,1)} %bitcast.12), calls=%async_computation | async-start | bytes 8388608 | tf_op jit(solution)/shard_map/all_to_all | solution.py:327
  186.6 24.9 %collective-permute-start.17 = (bf16[128,1024]{1,0:T(8,128)(2,1)}, bf16[128,1024]{1,0:T(8,128)(2,1)S(1)}, u32[]{:S(2)}, u32[]{:S(2)}) collective-permute-start(bf16[128,1024]{1,0:T(8,128)(2,1)} %get-tuple-element.56), channel_id=1, source_target_pairs={{0,12},{1,13},{2,14},{3,15},{4,0},{5,1},{6,2},{7,3},{8,4},{9,5},{1... | collective-permute-start | bytes 786440 | tf_op jit(solution)/shard_map/ppermute | solution.py:270
  189.3 23.2 %collective-permute-start.19 = (bf16[128,1024]{1,0:T(8,128)(2,1)S(1)}, bf16[128,1024]{1,0:T(8,128)(2,1)S(1)}, u32[]{:S(2)}, u32[]{:S(2)}) collective-permute-start(bf16[128,1024]{1,0:T(8,128)(2,1)S(1)} %get-tuple-element.57), channel_id=1, source_target_pairs={{0,8},{1,9},{2,10},{3,11},{4,12},{5,13},{6,14},{7,15},{8,0},{9,1},... | collective-permute-start | bytes 786440 | tf_op jit(solution)/shard_map/ppermute | solution.py:270
  190.1 26.6 %collective-permute-start.18 = (bf16[128,1024]{1,0:T(8,128)(2,1)S(1)}, bf16[128,1024]{1,0:T(8,128)(2,1)S(1)}, u32[]{:S(2)}, u32[]{:S(2)}) collective-permute-start(bf16[128,1024]{1,0:T(8,128)(2,1)S(1)} %get-tuple-element.58), channel_id=1, source_target_pairs={{0,4},{1,5},{2,6},{3,7},{4,8},{5,9},{6,10},{7,11},{8,12},{9,13},{1... | collective-permute-start | bytes 786440 | tf_op jit(solution)/shard_map/ppermute | solution.py:270
  210.1 11.7 %collective-permute-start.21 = (bf16[256,512]{1,0:T(8,128)(2,1)S(1)}, bf16[256,512]{1,0:T(8,128)(2,1)S(1)}, u32[]{:S(2)}, u32[]{:S(2)}) collective-permute-start(bf16[256,512]{1,0:T(8,128)(2,1)S(1)} %slice.69), channel_id=1, source_target_pairs={{0,66},{1,67},{2,64},{3,65},{4,70},{5,71},{6,68},{7,69},{16,82},{1... | collective-permute-start | bytes 786440 | tf_op jit(solution)/shard_map/ppermute | solution.py:270
  216.9 6.3 %collective-permute-start.20 = (bf16[64,1024]{1,0:T(8,128)(2,1)S(1)}, bf16[64,1024]{1,0:T(8,128)(2,1)S(1)}, u32[]{:S(2)}, u32[]{:S(2)}) collective-permute-start(bf16[64,1024]{1,0:T(8,128)(2,1)S(1)} %slice.65), channel_id=1, source_target_pairs={{0,2},{1,3},{2,0},{3,1},{4,6},{5,7},{6,4},{7,5},{8,10},{9,11},{10,... | collective-permute-start | bytes 393224 | tf_op jit(solution)/shard_map/ppermute | solution.py:270
  217.8 13.2 %collective-permute-start.23 = (bf16[256,512]{1,0:T(8,128)(2,1)S(1)}, bf16[256,512]{1,0:T(8,128)(2,1)S(1)}, u32[]{:S(2)}, u32[]{:S(2)}) collective-permute-start(bf16[256,512]{1,0:T(8,128)(2,1)S(1)} %slice.69), channel_id=1, source_target_pairs={{8,70},{9,71},{10,68},{11,69},{12,66},{13,67},{14,64},{15,65},{24,... | collective-permute-start | bytes 786440 | tf_op jit(solution)/shard_map/ppermute | solution.py:270
  221.8 9.2 %collective-permute-start.22 = (bf16[256,512]{1,0:T(8,128)(2,1)S(1)}, bf16[256,512]{1,0:T(8,128)(2,1)S(1)}, u32[]{:S(2)}, u32[]{:S(2)}) collective-permute-start(bf16[256,512]{1,0:T(8,128)(2,1)S(1)} %get-tuple-element.62), channel_id=1, source_target_pairs={{8,4},{9,5},{10,6},{11,7},{12,0},{13,1},{14,2},{15,3},{24,20},{25,... | collective-permute-start | bytes 786440 | tf_op jit(solution)/shard_map/ppermute | solution.py:270
  (25 other events, 283.9 us)
Sparse Core Ops, SparseCore 0:
  38.2 51.7 all-gather.1

commit v6 on v5

--- a/solution.py
+++ b/solution.py
@@ -44,7 +44,7 @@
             in_specs=[blk,blk,blk,pl.BlockSpec(cache.shape,lambda b,t,w:(0,0))],
             out_specs=[blk,pl.BlockSpec((1,heads,(KB+1)*BLK,BLK),lambda b,t,w:(b,0,0,0))]),
         out_shape=[jax.ShapeDtypeStruct((T,W),jnp.bfloat16),jax.ShapeDtypeStruct((nb,heads,(KB+1)*BLK,BLK),jnp.bfloat16)],
-        compiler_params=pltpu.CompilerParams(vmem_limit_bytes=40<<20),
+        compiler_params=pltpu.CompilerParams(vmem_limit_bytes=56<<20),
         cost_estimate=SHORT,
         name="attn_fwd")(table,place,q,k,v,cache)
 
@@ -94,7 +94,7 @@
             out_specs=[blk,blk,blk,part,part],
             scratch_shapes=[pltpu.VMEM(cache.shape,jnp.float32)]),
         out_shape=[jax.ShapeDtypeStruct((T,W),jnp.bfloat16)]*3+[jax.ShapeDtypeStruct((cache.shape[0]//2,cache.shape[1]),jnp.bfloat16)]*2,
-        compiler_params=pltpu.CompilerParams(vmem_limit_bytes=40<<20),
+        compiler_params=pltpu.CompilerParams(vmem_limit_bytes=56<<20),
         cost_estimate=SHORT,
         name="attn_bwd")(table,place,q,k,v,cache,p,ga,gu,gl)
 

time: 241 us -> 244 us (1.012)
  local copies, waits for them, and re-layouts: 17.2 us -> 11.6 us
  Pallas kernels: 80.2 us -> 84.9 us
  other arithmetic: 7.53 us -> 10.9 us
    unnamed x48 -> x28, local copies, waits for them, and re-layouts: 12 us -> 5.82 us
  transfers between devices with their start and end apart: 26 -> 26, of which waited for: 13 -> 13; matrix products, arithmetic and copies ran while one was open for 4% -> 6% of each run, Pallas kernels for 34% -> 35%
where the time goes in v6:
time: 244 us; the launch traced here: 242 us
  Pallas kernels  84.9 us (35%)
  waiting for transfers between devices  75.9 us (31%)
  starting transfers between devices  44.3 us (18%)
  between operations  14.4 us (6%)
  local copies, waits for them, and re-layouts  11.6 us (5%)
  other arithmetic  10.9 us (4%)
    ppermute x24, waiting for transfers between devices, send(): return lax.ppermute(array, AXES, pairs)  57.6 us
    ppermute x24, starting transfers between devices, send(): return lax.ppermute(array, AXES, pairs)  37.5 us
    pallas_call x2, Pallas kernels, outer(): pl.pallas_call(outer_kernel, grid_spec=pltpu.PrefetchScalarGridSpec(num_s...  23.5 us
    pallas_call x1, Pallas kernels, bwd(): pl.pallas_call(functools.partial(bwd_kernel, heads), grid_spec=pltpu.Pref...  21.8 us
    pallas_call x2, Pallas kernels, project(): pl.pallas_call(functools.partial(project_kernel, other), grid_spec=pltpu....  20.9 us
    pallas_call x1, Pallas kernels, fwd(): pl.pallas_call(functools.partial(fwd_kernel, heads), grid_spec=pltpu.Pref...  18.6 us
    all_to_all x1, waiting for transfers between devices, per_device(): lax.all_to_all(pieces, 'col', split_axis=0, concat_axis=0, axis_index_gro...  18.3 us
    all_to_all x1, starting transfers between devices, per_device(): lax.all_to_all(pieces, 'col', split_axis=0, concat_axis=0, axis_index_gro...  6.79 us
  transfers between devices with their start and end apart: 26, of which 13 were waited for; matrix products, arithmetic and copies ran while one was open for 6% of the time, Pallas kernels for 35%

profile of v6, /device:TPU:6, one launch (start us, length us, event | category | flops | bytes accessed | tf_op | source)
XLA Modules:
  0.0 241.9 jit_solution(8516064459865985403)
XLA Ops:
  9.1 3.1 %collective-permute-start.2 = (bf16[512,1024]{1,0:T(8,128)(2,1)S(1)}, bf16[512,1024]{1,0:T(8,128)(2,1)S(1)}, u32[]{:S(2)}, u32[]{:S(2)}) collective-permute-start(bf16[512,1024]{1,0:T(8,128)(2,1)S(1)} %get-tuple-element.54.refs_1_), channel_id=1, source_target_pairs={{0,48},{1,49},{2,50},{3,51},{4,52},{5,53},{6,54},{7,55},{8,56},{9,... | collective-permute-start | bytes 3145736 | tf_op jit(solution)/shard_map/ppermute | solution.py:270
  12.1 5.8 %collective-permute-start = (bf16[512,512]{1,0:T(8,128)(2,1)S(1)}, bf16[512,512]{1,0:T(8,128)(2,1)}, u32[]{:S(2)}, u32[]{:S(2)}) collective-permute-start(bf16[512,512]{1,0:T(8,128)(2,1)S(1)} %copy-done.12), channel_id=1, source_target_pairs={{0,0},{1,1},{2,2},{3,3},{4,4},{5,5},{6,6},{7,7},{8,70},{9,71},{10,... | collective-permute-start | bytes 1572872 | tf_op jit(solution)/shard_map/ppermute | solution.py:270
  19.0 4.1 %collective-permute-done.3 = bf16[64,1024]{1,0:T(8,128)(2,1)S(1)} collective-permute-done((bf16[64,1024]{1,0:T(8,128)(2,1)S(1)}, bf16[64,1024]{1,0:T(8,128)(2,1)S(1)}, u32[]{:S(2)}, u32[]{:S(2)}) %collective-permute-start.3) | collective-permute-done | bytes 131104 | tf_op jit(solution)/shard_map/ppermute | solution.py:270
  23.2 13.2 %collective-permute-done.4 = bf16[128,1024]{1,0:T(8,128)(2,1)} collective-permute-done((bf16[128,1024]{1,0:T(8,128)(2,1)S(1)}, bf16[128,1024]{1,0:T(8,128)(2,1)}, u32[]{:S(2)}, u32[]{:S(2)}) %collective-permute-start.4) | collective-permute-done | bytes 262176 | tf_op jit(solution)/shard_map/ppermute | solution.py:270
  38.2 3.2 %collective-permute-start.8 = (bf16[512,1024]{1,0:T(8,128)(2,1)S(1)}, bf16[512,1024]{1,0:T(8,128)(2,1)S(1)}, u32[]{:S(2)}, u32[]{:S(2)}) collective-permute-start(bf16[512,1024]{1,0:T(8,128)(2,1)S(1)} %get-tuple-element.55.refs_0_), channel_id=1, source_target_pairs={{0,48},{1,49},{2,50},{3,51},{4,52},{5,53},{6,54},{7,55},{8,56},{9,... | collective-permute-start | bytes 3145736 | tf_op jit(solution)/shard_map/ppermute | solution.py:270
  41.4 4.0 %collective-permute-start.6 = (bf16[128,1024]{1,0:T(8,128)(2,1)S(1)}, bf16[128,1024]{1,0:T(8,128)(2,1)S(1)}, u32[]{:S(2)}, u32[]{:S(2)}) collective-permute-start(bf16[128,1024]{1,0:T(8,128)(2,1)S(1)} %pad_maximum_fusion.3), channel_id=1, source_target_pairs={{0,12},{1,13},{2,14},{3,15},{4,0},{5,1},{6,2},{7,3},{8,4},{9,5},{1... | collective-permute-start | bytes 786440 | tf_op jit(solution)/shard_map/ppermute | solution.py:270
  45.4 3.9 %collective-permute-done.6 = bf16[128,1024]{1,0:T(8,128)(2,1)S(1)} collective-permute-done((bf16[128,1024]{1,0:T(8,128)(2,1)S(1)}, bf16[128,1024]{1,0:T(8,128)(2,1)S(1)}, u32[]{:S(2)}, u32[]{:S(2)}) %collective-permute-start.6) | collective-permute-done | bytes 262176 | tf_op jit(solution)/shard_map/ppermute | solution.py:270
  49.3 4.7 %collective-permute-done.5 = bf16[128,1024]{1,0:T(8,128)(2,1)S(1)} collective-permute-done((bf16[128,1024]{1,0:T(8,128)(2,1)S(1)}, bf16[128,1024]{1,0:T(8,128)(2,1)S(1)}, u32[]{:S(2)}, u32[]{:S(2)}) %collective-permute-start.5) | collective-permute-done | bytes 262176 | tf_op jit(solution)/shard_map/ppermute | solution.py:270
  56.0 7.1 %collective-permute-done.7.refs_3_ = bf16[512,1024]{1,0:T(8,128)(2,1)S(1)} collective-permute-done((bf16[512,1024]{1,0:T(8,128)(2,1)S(1)}, bf16[512,1024]{1,0:T(8,128)(2,1)S(1)}, u32[]{:S(2)}, u32[]{:S(2)}) %collective-permute-start.7) | collective-permute-done | bytes 1048608 | tf_op jit(solution)/shard_map/ppermute | solution.py:270
  69.2 3.1 %pad_maximum_fusion = bf16[8,2,64,1024]{3,2,1,0:T(8,128)(2,1)} fusion(bf16[8,1,64,1024]{3,2,1,0:T(8,128)(2,1)} %bitcast.4, bf16[8,1,64,1024]{3,2,1,0:T(8,128)(2,1)} %bitcast.2), kind=kLoop, calls=%fused_computation | loop fusion | flops 1048576 | bytes 4194304 | tf_op jit(solution)/shard_map/stack | solution.py:300
  72.3 18.6 %attn_fwd.1 = (bf16[1024,512]{1,0:T(8,128)(2,1)}, bf16[8,4,640,128]{3,2,1,0:T(8,128)(2,1)}) custom-call(s32[8,4]{1,0:T(8,128)} %copy.18.table, s32[24]{0:T(128)} %dynamic-slice_bitcast_fusion.place, bf16[1024,512]{1,0:T(8,128)(2,1)} %q_ref.3, bf16[1024,512]{1,0:T(8,128)(2,1)} %k_ref.3, bf16[1024,512]{1,0:T(8,128)(2,1)} %v_ref.3, bf16[1024,1024]{1,0:T(8,128)(2,1)} %bitcast.10), custom_call_target="tpu_custom_call" | custom-call | flops 1048576 | bytes 65536 | tf_op jit(solution)/shard_map/attn_fwd/pallas_call | solution.py:42
  92.3 10.3 %project.2 = bf16[1024,512]{1,0:T(8,128)(2,1)} custom-call(s32[24]{0:T(128)} %dynamic-slice_bitcast_fusion.place, bf16[512,1024]{1,0:T(8,128)(2,1)} %copy-done.1, bf16[512,1024]{1,0:T(8,128)(2,1)} %copy-done, bf16[512,1024]{1,0:T(8,128)(2,1)} %collective-permute-done.1.refs_2_, bf16[512,1024]{1,0:T(8,128)(2,1)} %copy-done.3, bf16[512,1024]{1,0:T(8,128)(2,1)} %copy-done.4, ...), custom_call_target="tpu_custom_call" | custom-call | flops 1048576 | bytes 65536 | tf_op jit(solution)/shard_map/project/pallas_call | solution.py:134
  106.1 10.5 %project.3.ga_ref = f32[1024,512]{1,0:T(8,128)} custom-call(s32[24]{0:T(128)} %dynamic-slice_bitcast_fusion.place, bf16[512,1024]{1,0:T(8,128)(2,1)} %copy-done.1, bf16[512,1024]{1,0:T(8,128)(2,1)} %copy-done, bf16[512,1024]{1,0:T(8,128)(2,1)} %collective-permute-done.1.refs_2_, bf16[512,1024]{1,0:T(8,128)(2,1)} %copy-done.3, bf16[512,1024]{1,0:T(8,128)(2,1)} %copy-done.4, ...), custom_call_target="tpu_custom_call" | custom-call | flops 1048576 | bytes 65536 | tf_op jit(solution)/shard_map/project/pallas_call | solution.py:134
  119.7 11.2 %outer.2 = bf16[2048,1024]{1,0:T(8,128)(2,1)} custom-call(s32[24]{0:T(128)} %dynamic-slice_bitcast_fusion.place, bf16[512,1024]{1,0:T(8,128)(2,1)} %copy-done.1, bf16[512,1024]{1,0:T(8,128)(2,1)} %copy-done, bf16[512,1024]{1,0:T(8,128)(2,1)} %collective-permute-done.1.refs_2_, bf16[512,1024]{1,0:T(8,128)(2,1)} %copy-done.3, bf16[512,1024]{1,0:T(8,128)(2,1)} %copy-done.4, ...), custom_call_target="tpu_custom_call" | custom-call | flops 1048576 | bytes 65536 | tf_op jit(solution)/shard_map/outer/pallas_call | solution.py:200
  132.6 5.8 %collective-permute-done.14.refs_10_ = bf16[2048,1024]{1,0:T(8,128)(2,1)S(1)} collective-permute-done((bf16[2048,1024]{1,0:T(8,128)(2,1)}, bf16[2048,1024]{1,0:T(8,128)(2,1)S(1)}, u32[]{:S(2)}, u32[]{:S(2)}) %collective-permute-start.14) | collective-permute-done | bytes 4194336 | tf_op jit(solution)/shard_map/ppermute | solution.py:270
  140.4 12.3 %outer.3 = bf16[4096,512]{1,0:T(8,128)(2,1)} custom-call(s32[24]{0:T(128)} %dynamic-slice_bitcast_fusion.place, bf16[512,1024]{1,0:T(8,128)(2,1)} %copy-done.1, bf16[512,1024]{1,0:T(8,128)(2,1)} %copy-done, bf16[512,1024]{1,0:T(8,128)(2,1)} %collective-permute-done.1.refs_2_, bf16[512,1024]{1,0:T(8,128)(2,1)} %copy-done.3, bf16[512,1024]{1,0:T(8,128)(2,1)} %copy-done.4, ...), custom_call_target="tpu_custom_call" | custom-call | flops 1048576 | bytes 65536 | tf_op jit(solution)/shard_map/outer/pallas_call | solution.py:200
  153.6 6.8 %all-to-all-start = ((bf16[8,512,512]{2,1,0:T(8,128)(2,1)}), bf16[8,512,512]{2,1,0:T(8,128)(2,1)}, u32[]{:S(2)}, u32[]{:S(2)}) async-start(bf16[8,512,512]{2,1,0:T(8,128)(2,1)} %bitcast.12), calls=%async_computation | async-start | bytes 8388608 | tf_op jit(solution)/shard_map/all_to_all | solution.py:327
  160.4 21.8 %attn_bwd.1 = (bf16[1024,512]{1,0:T(8,128)(2,1)}, bf16[1024,512]{1,0:T(8,128)(2,1)}, bf16[1024,512]{1,0:T(8,128)(2,1)}, bf16[512,1024]{1,0:T(8,128)(2,1)}, bf16[512,1024]{1,0:T(8,128)(2,1)}) custom-call(s32[8,4]{1,0:T(8,128)} %copy.18.table, s32[24]{0:T(128)} %dynamic-slice_bitcast_fusion.place, bf16[1024,512]{1,0:T(8,128)(2,1)} %q_ref.3, ...), custom_call_target="tpu_custom_call" | custom-call | flops 1048576 | bytes 65536 | tf_op jit(solution)/shard_map/attn_bwd/pallas_call | solution.py:91
  182.3 2.9 %collective-permute-done.16 = bf16[512,1024]{1,0:T(8,128)(2,1)S(1)} collective-permute-done((bf16[512,1024]{1,0:T(8,128)(2,1)}, bf16[512,1024]{1,0:T(8,128)(2,1)S(1)}, u32[]{:S(2)}, u32[]{:S(2)}) %collective-permute-start.16) | collective-permute-done | bytes 1048608 | tf_op jit(solution)/shard_map/ppermute | solution.py:270
  191.9 18.3 %all-to-all-done = bf16[8,512,512]{2,1,0:T(8,128)(2,1)} async-done(((bf16[8,512,512]{2,1,0:T(8,128)(2,1)}), bf16[8,512,512]{2,1,0:T(8,128)(2,1)}, u32[]{:S(2)}, u32[]{:S(2)}) %all-to-all-start) | async-done | bytes 4194336 | tf_op jit(solution)/shard_map/all_to_all | solution.py:327
  210.2 3.1 %reduce_sum.12 = bf16[512,512]{1,0:T(8,128)(2,1)S(1)} reduce(bf16[8,512,512]{2,1,0:T(8,128)(2,1)} %all-to-all-done, bf16[]{:T(256)} %constant.46.clone.1), dimensions={0}, to_apply=%region_0.1 | reduce | flops 1835008 | bytes 4718594 | tf_op jit(solution)/shard_map/reduce_sum | solution.py:328
  215.7 4.2 %collective-permute-done.18 = bf16[128,1024]{1,0:T(8,128)(2,1)S(1)} collective-permute-done((bf16[128,1024]{1,0:T(8,128)(2,1)S(1)}, bf16[128,1024]{1,0:T(8,128)(2,1)S(1)}, u32[]{:S(2)}, u32[]{:S(2)}) %collective-permute-start.18) | collective-permute-done | bytes 262176 | tf_op jit(solution)/shard_map/ppermute | solution.py:270
  221.0 4.0 %collective-permute-start.23 = (bf16[256,512]{1,0:T(8,128)(2,1)S(1)}, bf16[256,512]{1,0:T(8,128)(2,1)S(1)}, u32[]{:S(2)}, u32[]{:S(2)}) collective-permute-start(bf16[256,512]{1,0:T(8,128)(2,1)S(1)} %slice.69), channel_id=1, source_target_pairs={{8,70},{9,71},{10,68},{11,69},{12,66},{13,67},{14,64},{15,65},{24,... | collective-permute-start | bytes 786440 | tf_op jit(solution)/shard_map/ppermute | solution.py:270
  227.1 7.1 %collective-permute-done.23 = bf16[256,512]{1,0:T(8,128)(2,1)S(1)} collective-permute-done((bf16[256,512]{1,0:T(8,128)(2,1)S(1)}, bf16[256,512]{1,0:T(8,128)(2,1)S(1)}, u32[]{:S(2)}, u32[]{:S(2)}) %collective-permute-start.23) | collective-permute-done | bytes 262176 | tf_op jit(solution)/shard_map/ppermute | solution.py:270
  (81 shorter events, 38.3 us)
Async XLA Ops:
  7.2 85.2 %all-gather.2.cloned.1.call-start = ((), (), s32[]{:S(2)}) async-start(), calls=%async_computation.1 | async-start | bytes 8912896 | tf_op jit(solution)/shard_map/all_gather | solution.py:303
  9.1 27.4 %collective-permute-start.2 = (bf16[512,1024]{1,0:T(8,128)(2,1)S(1)}, bf16[512,1024]{1,0:T(8,128)(2,1)S(1)}, u32[]{:S(2)}, u32[]{:S(2)}) collective-permute-start(bf16[512,1024]{1,0:T(8,128)(2,1)S(1)} %get-tuple-element.54.refs_1_), channel_id=1, source_target_pairs={{0,48},{1,49},{2,50},{3,51},{4,52},{5,53},{6,54},{7,55},{8,56},{9,... | collective-permute-start | bytes 3145736 | tf_op jit(solution)/shard_map/ppermute | solution.py:270
  12.1 25.9 %collective-permute-start.1 = (bf16[512,1024]{1,0:T(8,128)(2,1)S(1)}, bf16[512,1024]{1,0:T(8,128)(2,1)}, u32[]{:S(2)}, u32[]{:S(2)}) collective-permute-start(bf16[512,1024]{1,0:T(8,128)(2,1)S(1)} %get-tuple-element.55.refs_0_), channel_id=1, source_target_pairs={{0,16},{1,17},{2,18},{3,19},{4,20},{5,21},{6,22},{7,23},{8,24},{9,... | collective-permute-start | bytes 3145736 | tf_op jit(solution)/shard_map/ppermute | solution.py:270
  12.1 24.3 %collective-permute-start = (bf16[512,512]{1,0:T(8,128)(2,1)S(1)}, bf16[512,512]{1,0:T(8,128)(2,1)}, u32[]{:S(2)}, u32[]{:S(2)}) collective-permute-start(bf16[512,512]{1,0:T(8,128)(2,1)S(1)} %copy-done.12), channel_id=1, source_target_pairs={{0,0},{1,1},{2,2},{3,3},{4,4},{5,5},{6,6},{7,7},{8,70},{9,71},{10,... | collective-permute-start | bytes 1572872 | tf_op jit(solution)/shard_map/ppermute | solution.py:270
  23.1 13.3 %collective-permute-start.4 = (bf16[128,1024]{1,0:T(8,128)(2,1)S(1)}, bf16[128,1024]{1,0:T(8,128)(2,1)}, u32[]{:S(2)}, u32[]{:S(2)}) collective-permute-start(bf16[128,1024]{1,0:T(8,128)(2,1)S(1)} %pad_maximum_fusion.3), channel_id=1, source_target_pairs={{0,8},{1,9},{2,10},{3,11},{4,12},{5,13},{6,14},{7,15},{8,0},{9,1},... | collective-permute-start | bytes 786440 | tf_op jit(solution)/shard_map/ppermute | solution.py:270
  38.1 25.0 %collective-permute-start.7 = (bf16[512,1024]{1,0:T(8,128)(2,1)S(1)}, bf16[512,1024]{1,0:T(8,128)(2,1)S(1)}, u32[]{:S(2)}, u32[]{:S(2)}) collective-permute-start(bf16[512,1024]{1,0:T(8,128)(2,1)S(1)} %get-tuple-element.54.refs_1_), channel_id=1, source_target_pairs={{0,16},{1,17},{2,18},{3,19},{4,20},{5,21},{6,22},{7,23},{8,24},{9,... | collective-permute-start | bytes 3145736 | tf_op jit(solution)/shard_map/ppermute | solution.py:270
  38.2 24.9 %collective-permute-start.8 = (bf16[512,1024]{1,0:T(8,128)(2,1)S(1)}, bf16[512,1024]{1,0:T(8,128)(2,1)S(1)}, u32[]{:S(2)}, u32[]{:S(2)}) collective-permute-start(bf16[512,1024]{1,0:T(8,128)(2,1)S(1)} %get-tuple-element.55.refs_0_), channel_id=1, source_target_pairs={{0,48},{1,49},{2,50},{3,51},{4,52},{5,53},{6,54},{7,55},{8,56},{9,... | collective-permute-start | bytes 3145736 | tf_op jit(solution)/shard_map/ppermute | solution.py:270
  41.4 7.9 %collective-permute-start.6 = (bf16[128,1024]{1,0:T(8,128)(2,1)S(1)}, bf16[128,1024]{1,0:T(8,128)(2,1)S(1)}, u32[]{:S(2)}, u32[]{:S(2)}) collective-permute-start(bf16[128,1024]{1,0:T(8,128)(2,1)S(1)} %pad_maximum_fusion.3), channel_id=1, source_target_pairs={{0,12},{1,13},{2,14},{3,15},{4,0},{5,1},{6,2},{7,3},{8,4},{9,5},{1... | collective-permute-start | bytes 786440 | tf_op jit(solution)/shard_map/ppermute | solution.py:270
  45.4 8.6 %collective-permute-start.5 = (bf16[128,1024]{1,0:T(8,128)(2,1)S(1)}, bf16[128,1024]{1,0:T(8,128)(2,1)S(1)}, u32[]{:S(2)}, u32[]{:S(2)}) collective-permute-start(bf16[128,1024]{1,0:T(8,128)(2,1)S(1)} %pad_maximum_fusion.3), channel_id=1, source_target_pairs={{0,4},{1,5},{2,6},{3,7},{4,8},{5,9},{6,10},{7,11},{8,12},{9,13},{1... | collective-permute-start | bytes 786440 | tf_op jit(solution)/shard_map/ppermute | solution.py:270
  63.1 6.1 %collective-permute-start.9 = (bf16[512,1024]{1,0:T(8,128)(2,1)}, bf16[512,1024]{1,0:T(8,128)(2,1)}, u32[]{:S(2)}, u32[]{:S(2)}) collective-permute-start(bf16[512,1024]{1,0:T(8,128)(2,1)} %pad_maximum_fusion.1), channel_id=1, source_target_pairs={{0,1},{1,0},{2,3},{3,2},{4,5},{5,4},{6,7},{7,6},{8,9},{9,8},{10,11... | collective-permute-start | bytes 3145736 | tf_op jit(solution)/shard_map/ppermute | solution.py:270
  64.1 28.3 %collective-permute-start.10 = (bf16[512,1024]{1,0:T(8,128)(2,1)}, bf16[512,1024]{1,0:T(8,128)(2,1)}, u32[]{:S(2)}, u32[]{:S(2)}) collective-permute-start(bf16[512,1024]{1,0:T(8,128)(2,1)} %collective-permute-done.1.refs_2_), channel_id=1, source_target_pairs={{0,16},{1,17},{2,18},{3,19},{4,20},{5,21},{6,22},{7,23},{8,24},{9,... | collective-permute-start | bytes 3145736 | tf_op jit(solution)/shard_map/ppermute | solution.py:270
  64.5 27.9 %collective-permute-start.11 = (bf16[512,1024]{1,0:T(8,128)(2,1)S(1)}, bf16[512,1024]{1,0:T(8,128)(2,1)}, u32[]{:S(2)}, u32[]{:S(2)}) collective-permute-start(bf16[512,1024]{1,0:T(8,128)(2,1)S(1)} %collective-permute-done.2.refs_5_), channel_id=1, source_target_pairs={{0,48},{1,49},{2,50},{3,51},{4,52},{5,53},{6,54},{7,55},{8,56},{9,... | collective-permute-start | bytes 3145736 | tf_op jit(solution)/shard_map/ppermute | solution.py:270
  90.9 27.8 %collective-permute-start.12 = (bf16[1024,512]{1,0:T(8,128)(2,1)}, bf16[1024,512]{1,0:T(8,128)(2,1)S(1)}, u32[]{:S(2)}, u32[]{:S(2)}) collective-permute-start(bf16[1024,512]{1,0:T(8,128)(2,1)} %get-tuple-element.38.refs_8_), channel_id=1, source_target_pairs={{0,64},{1,65},{2,66},{3,67},{4,68},{5,69},{6,70},{7,71},{8,72},{9,... | collective-permute-start | bytes 3145736 | tf_op jit(solution)/shard_map/ppermute | solution.py:270
  104.0 27.0 %collective-permute-start.13 = (bf16[512,512]{1,0:T(8,128)(2,1)S(1)}, bf16[512,512]{1,0:T(8,128)(2,1)S(1)}, u32[]{:S(2)}, u32[]{:S(2)}) collective-permute-start(bf16[512,512]{1,0:T(8,128)(2,1)S(1)} %get-tuple-element.60), channel_id=1, source_target_pairs={{0,64},{1,65},{2,66},{3,67},{4,68},{5,69},{6,70},{7,71},{8,72},{9,... | collective-permute-start | bytes 1572872 | tf_op jit(solution)/shard_map/ppermute | solution.py:270
  131.0 7.4 %collective-permute-start.14 = (bf16[2048,1024]{1,0:T(8,128)(2,1)}, bf16[2048,1024]{1,0:T(8,128)(2,1)S(1)}, u32[]{:S(2)}, u32[]{:S(2)}) collective-permute-start(bf16[2048,1024]{1,0:T(8,128)(2,1)} %outer.2), channel_id=1, source_target_pairs={{0,1},{1,0},{2,3},{3,2},{4,5},{5,4},{6,7},{7,6},{8,9},{9,8},{10,11... | collective-permute-start | bytes 12582920 | tf_op jit(solution)/shard_map/ppermute | solution.py:270
  131.1 21.7 %collective-permute-start.15 = (bf16[512,512]{1,0:T(8,128)(2,1)S(1)}, bf16[512,512]{1,0:T(8,128)(2,1)S(1)}, u32[]{:S(2)}, u32[]{:S(2)}) collective-permute-start(bf16[512,512]{1,0:T(8,128)(2,1)S(1)} %get-tuple-element.59), channel_id=1, source_target_pairs={{0,64},{1,65},{2,66},{3,67},{4,68},{5,69},{6,70},{7,71},{8,72},{9,... | collective-permute-start | bytes 1572872 | tf_op jit(solution)/shard_map/ppermute | solution.py:270
  153.6 56.6 %all-to-all-start = ((bf16[8,512,512]{2,1,0:T(8,128)(2,1)}), bf16[8,512,512]{2,1,0:T(8,128)(2,1)}, u32[]{:S(2)}, u32[]{:S(2)}) async-start(bf16[8,512,512]{2,1,0:T(8,128)(2,1)} %bitcast.12), calls=%async_computation | async-start | bytes 8388608 | tf_op jit(solution)/shard_map/all_to_all | solution.py:327
  187.5 27.1 %collective-permute-start.17 = (bf16[128,1024]{1,0:T(8,128)(2,1)}, bf16[128,1024]{1,0:T(8,128)(2,1)S(1)}, u32[]{:S(2)}, u32[]{:S(2)}) collective-permute-start(bf16[128,1024]{1,0:T(8,128)(2,1)} %get-tuple-element.56), channel_id=1, source_target_pairs={{0,12},{1,13},{2,14},{3,15},{4,0},{5,1},{6,2},{7,3},{8,4},{9,5},{1... | collective-permute-start | bytes 786440 | tf_op jit(solution)/shard_map/ppermute | solution.py:270
  190.2 25.4 %collective-permute-start.19 = (bf16[128,1024]{1,0:T(8,128)(2,1)S(1)}, bf16[128,1024]{1,0:T(8,128)(2,1)S(1)}, u32[]{:S(2)}, u32[]{:S(2)}) collective-permute-start(bf16[128,1024]{1,0:T(8,128)(2,1)S(1)} %get-tuple-element.57), channel_id=1, source_target_pairs={{0,8},{1,9},{2,10},{3,11},{4,12},{5,13},{6,14},{7,15},{8,0},{9,1},... | collective-permute-start | bytes 786440 | tf_op jit(solution)/shard_map/ppermute | solution.py:270
  191.1 28.8 %collective-permute-start.18 = (bf16[128,1024]{1,0:T(8,128)(2,1)S(1)}, bf16[128,1024]{1,0:T(8,128)(2,1)S(1)}, u32[]{:S(2)}, u32[]{:S(2)}) collective-permute-start(bf16[128,1024]{1,0:T(8,128)(2,1)S(1)} %get-tuple-element.58), channel_id=1, source_target_pairs={{0,4},{1,5},{2,6},{3,7},{4,8},{5,9},{6,10},{7,11},{8,12},{9,13},{1... | collective-permute-start | bytes 786440 | tf_op jit(solution)/shard_map/ppermute | solution.py:270
  213.3 11.7 %collective-permute-start.21 = (bf16[256,512]{1,0:T(8,128)(2,1)S(1)}, bf16[256,512]{1,0:T(8,128)(2,1)S(1)}, u32[]{:S(2)}, u32[]{:S(2)}) collective-permute-start(bf16[256,512]{1,0:T(8,128)(2,1)S(1)} %slice.69), channel_id=1, source_target_pairs={{0,66},{1,67},{2,64},{3,65},{4,70},{5,71},{6,68},{7,69},{16,82},{1... | collective-permute-start | bytes 786440 | tf_op jit(solution)/shard_map/ppermute | solution.py:270
  220.0 6.3 %collective-permute-start.20 = (bf16[64,1024]{1,0:T(8,128)(2,1)S(1)}, bf16[64,1024]{1,0:T(8,128)(2,1)S(1)}, u32[]{:S(2)}, u32[]{:S(2)}) collective-permute-start(bf16[64,1024]{1,0:T(8,128)(2,1)S(1)} %slice.65), channel_id=1, source_target_pairs={{0,2},{1,3},{2,0},{3,1},{4,6},{5,7},{6,4},{7,5},{8,10},{9,11},{10,... | collective-permute-start | bytes 393224 | tf_op jit(solution)/shard_map/ppermute | solution.py:270
  221.0 13.2 %collective-permute-start.23 = (bf16[256,512]{1,0:T(8,128)(2,1)S(1)}, bf16[256,512]{1,0:T(8,128)(2,1)S(1)}, u32[]{:S(2)}, u32[]{:S(2)}) collective-permute-start(bf16[256,512]{1,0:T(8,128)(2,1)S(1)} %slice.69), channel_id=1, source_target_pairs={{8,70},{9,71},{10,68},{11,69},{12,66},{13,67},{14,64},{15,65},{24,... | collective-permute-start | bytes 786440 | tf_op jit(solution)/shard_map/ppermute | solution.py:270
  225.0 9.2 %collective-permute-start.22 = (bf16[256,512]{1,0:T(8,128)(2,1)S(1)}, bf16[256,512]{1,0:T(8,128)(2,1)S(1)}, u32[]{:S(2)}, u32[]{:S(2)}) collective-permute-start(bf16[256,512]{1,0:T(8,128)(2,1)S(1)} %get-tuple-element.62), channel_id=1, source_target_pairs={{8,4},{9,5},{10,6},{11,7},{12,0},{13,1},{14,2},{15,3},{24,20},{25,... | collective-permute-start | bytes 786440 | tf_op jit(solution)/shard_map/ppermute | solution.py:270
  (15 other events, 283.2 us)
Sparse Core Ops, SparseCore 0:
  38.2 51.7 all-gather.1
